TPU v7x, 32 devices: a whole 2x2x4 slice. The times are simulated.
32 devices in a mesh: dp: 4 (over x, core), seq: 8 (over z, y).
Axes of the slice: x: 2, y: 2, z: 4, core: 2. Of those that a mesh axis runs over, the one named last changes fastest.
Arguments:
- tokens_in: bfloat16 [8, 2048, 1024], P('dp', 'seq'), may hold values from -6 to 6
- lead_hours: int32 [8], P('dp'), may hold values from 6 to 168
- cotangent: bfloat16 [8, 2048, 1024], P('dp', 'seq'), may hold values from -6 to 6
- w_qkv: bfloat16 [1024, 3072], P(('dp', 'seq')), may hold values from -0.1875 to 0.1875
- w_out: bfloat16 [1024, 1024], P(('dp', 'seq')), may hold values from -6 to 6
- w_fc1: bfloat16 [1024, 4096], P(('dp', 'seq')), may hold values from -0.1875 to 0.1875
- w_fc2: bfloat16 [4096, 1024], P(('dp', 'seq')), may hold values from -0.09375 to 0.09375
- ln1_gain: bfloat16 [1024], P(('dp', 'seq')), may hold values from 0.25 to 1.75
- ln1_bias: bfloat16 [1024], P(('dp', 'seq')), may hold values from -3 to 3
- q_bias: bfloat16 [1024], P(('dp', 'seq')), may hold values from -3 to 3
- v_bias: bfloat16 [1024], P(('dp', 'seq')), may hold values from -3 to 3
- out_bias: bfloat16 [1024], P(('dp', 'seq')), may hold values from -3 to 3
- ln2_gain: bfloat16 [1024], P(('dp', 'seq')), may hold values from 0.25 to 1.75
- ln2_bias: bfloat16 [1024], P(('dp', 'seq')), may hold values from -3 to 3
- fc1_bias: bfloat16 [4096], P(('dp', 'seq')), may hold values from -3 to 3
- fc2_bias: bfloat16 [1024], P(('dp', 'seq')), may hold values from -3 to 3
- lead_weight: bfloat16 [1024], P(('dp', 'seq')), may hold values from -4 to 4
- lead_bias: bfloat16 [1024], P(('dp', 'seq')), may hold values from -3 to 3
Outputs:
- block_output: bfloat16 [8, 2048, 1024], P('dp', 'seq')
- input_grad: float32 [8, 2048, 1024], P('dp', 'seq')
- grad_qkv: float32 [1024, 3072], P(('dp', 'seq'))
- grad_out: float32 [1024, 1024], P(('dp', 'seq'))
- grad_fc1: float32 [1024, 4096], P(('dp', 'seq'))
- grad_fc2: float32 [4096, 1024], P(('dp', 'seq'))
- grad_ln1_gain: float32 [1024], P(('dp', 'seq'))
- grad_ln1_bias: float32 [1024], P(('dp', 'seq'))
- grad_q_bias: float32 [1024], P(('dp', 'seq'))
- grad_v_bias: float32 [1024], P(('dp', 'seq'))
- grad_out_bias: float32 [1024], P(('dp', 'seq'))
- grad_ln2_gain: float32 [1024], P(('dp', 'seq'))
- grad_ln2_bias: float32 [1024], P(('dp', 'seq'))
- grad_fc1_bias: float32 [4096], P(('dp', 'seq'))
- grad_fc2_bias: float32 [1024], P(('dp', 'seq'))
- grad_lead_weight: float32 [1024], P(('dp', 'seq'))
- grad_lead_bias: float32 [1024], P(('dp', 'seq'))
All inputs are finite; a program needn't handle non-finite values.
Results may differ from a plain program's by a relative error of at most 0.009.
Values may be sent and summed in bfloat16 or wider, within the bound.
A program may use at most 256 MiB of HBM per device.

v0:
```python
from functools import partial

import jax
import jax.numpy as jnp
from jax import lax
from jax.sharding import PartitionSpec as P

HEADS = 16


epsilon = 1e-06


def norm_rows(values, gain, shift):
    center = values - jnp.mean(values, axis=-1, keepdims=True)
    spread = jnp.mean(center * center, axis=-1, keepdims=True)
    return center * lax.rsqrt(spread + epsilon) * gain + shift


def gelu_exact(values):
    return jax.nn.gelu(values, approximate=False)


def product(left, right):
    return jnp.dot(left, right, preferred_element_type=jnp.float32)


def product_tleft(left, right):
    return lax.dot_general(
        left, right, (((0,), (0,)), ((), ())), preferred_element_type=jnp.float32
    )


def product_tright(left, right):
    return lax.dot_general(
        left, right, (((1,), (1,)), ((), ())), preferred_element_type=jnp.float32
    )


def split_heads(values):
    return values.reshape(values.shape[0], HEADS, values.shape[1] // HEADS)


def attend(operands):
    queries, keys_all, values_all = operands
    scale = (queries.shape[1] // HEADS) ** (-0.5)
    scores = (
        jnp.einsum(
            "qhd,khd->hqk",
            split_heads(queries),
            split_heads(keys_all),
            preferred_element_type=jnp.float32,
        )
        * scale
    )
    highest = jnp.max(scores, axis=-1, keepdims=True)
    exps = jnp.exp(scores - highest)
    totals = jnp.sum(exps, axis=-1, keepdims=True)
    probs_low = (exps / totals).astype(jnp.bfloat16)
    blended = jnp.einsum(
        "hqk,khd->qhd", probs_low, split_heads(values_all), preferred_element_type=jnp.float32
    ).reshape(queries.shape)
    return (blended, (highest + jnp.log(totals))[:, :, 0])


def recompute_probs(queries, keys_all, values_all, grads_in, log_totals):
    scale = (queries.shape[1] // HEADS) ** (-0.5)
    scores = (
        jnp.einsum(
            "qhd,khd->hqk",
            split_heads(queries),
            split_heads(keys_all),
            preferred_element_type=jnp.float32,
        )
        * scale
    )
    probs = jnp.exp(scores - log_totals[:, :, None])
    prob_grads = jnp.einsum(
        "qhd,khd->hqk",
        split_heads(grads_in),
        split_heads(values_all),
        preferred_element_type=jnp.float32,
    )
    return (probs, prob_grads, scale)


def key_side_grads(score_grads, probs, queries, grads_in, row_count):
    key_grads = jnp.einsum(
        "hqk,qhd->khd", score_grads, split_heads(queries), preferred_element_type=jnp.float32
    )
    value_grads = jnp.einsum(
        "hqk,qhd->khd",
        probs.astype(jnp.bfloat16),
        split_heads(grads_in),
        preferred_element_type=jnp.float32,
    )
    width = queries.shape[1]
    return (key_grads.reshape(row_count, width), value_grads.reshape(row_count, width))


def query_side(with_keys, operands):
    queries, keys_all, values_all, grads_in, log_totals = operands
    probs, prob_grads, scale = recompute_probs(queries, keys_all, values_all, grads_in, log_totals)
    row_delta = jnp.sum(probs * prob_grads, axis=-1)
    score_grads = (probs * (prob_grads - row_delta[:, :, None]) * scale).astype(jnp.bfloat16)
    query_grads = jnp.einsum(
        "hqk,khd->qhd", score_grads, split_heads(keys_all), preferred_element_type=jnp.float32
    ).reshape(queries.shape)
    key_grads, value_grads = key_side_grads(
        score_grads, probs, queries, grads_in, keys_all.shape[0]
    )
    return (query_grads, row_delta, key_grads, value_grads)


def on_device(
    tokens_in,
    lead_hours,
    cotangent,
    w_qkv,
    w_out,
    w_fc1,
    w_fc2,
    ln1_gain,
    ln1_bias,
    q_bias,
    v_bias,
    out_bias,
    ln2_gain,
    ln2_bias,
    fc1_bias,
    fc2_bias,
    lead_weight,
    lead_bias,
):
    gathered = (
        lax.all_gather(w_qkv, ("dp", "seq"), axis=0, tiled=True),
        lax.all_gather(w_out, ("dp", "seq"), axis=0, tiled=True),
        lax.all_gather(w_fc1, ("dp", "seq"), axis=0, tiled=True),
        lax.all_gather(w_fc2, ("dp", "seq"), axis=0, tiled=True),
        lax.all_gather(ln1_gain, ("dp", "seq"), axis=0, tiled=True),
        lax.all_gather(ln1_bias, ("dp", "seq"), axis=0, tiled=True),
        lax.all_gather(q_bias, ("dp", "seq"), axis=0, tiled=True),
        lax.all_gather(v_bias, ("dp", "seq"), axis=0, tiled=True),
        lax.all_gather(out_bias, ("dp", "seq"), axis=0, tiled=True),
        lax.all_gather(ln2_gain, ("dp", "seq"), axis=0, tiled=True),
        lax.all_gather(ln2_bias, ("dp", "seq"), axis=0, tiled=True),
        lax.all_gather(fc1_bias, ("dp", "seq"), axis=0, tiled=True),
        lax.all_gather(fc2_bias, ("dp", "seq"), axis=0, tiled=True),
        lax.all_gather(lead_weight, ("dp", "seq"), axis=0, tiled=True),
        lax.all_gather(lead_bias, ("dp", "seq"), axis=0, tiled=True),
    )
    (
        full_qkv,
        full_out,
        full_fc1,
        full_fc2,
        gain_one,
        shift_one,
        bias_query,
        bias_value,
        bias_out,
        gain_two,
        shift_two,
        bias_fc1,
        bias_fc2,
        lead_scale,
        lead_shift,
    ) = gathered
    items, rows, width = tokens_in.shape
    count = items * rows
    lead_times = lead_hours.astype(jnp.float32) / 100.0
    leading = (
        tokens_in.astype(jnp.float32)
        + lead_times[:, None, None] * lead_scale.astype(jnp.float32)
        + lead_shift.astype(jnp.float32)
    ).reshape(count, width)
    normed, norm_one_back = jax.vjp(
        norm_rows, leading, gain_one.astype(jnp.float32), shift_one.astype(jnp.float32)
    )
    normed_low = normed.astype(jnp.bfloat16)
    projected = product(normed_low, full_qkv)
    queries = (projected[:, :width] + bias_query.astype(jnp.float32)).astype(jnp.bfloat16)
    keys_own = projected[:, width : 2 * width].astype(jnp.bfloat16)
    values_own = (projected[:, 2 * width :] + bias_value.astype(jnp.float32)).astype(jnp.bfloat16)
    queries3 = queries.reshape(items, rows, width)
    keys_all, values_all = (
        lax.all_gather(keys_own.reshape(items, rows, width), "seq", axis=1, tiled=True),
        lax.all_gather(values_own.reshape(items, rows, width), "seq", axis=1, tiled=True),
    )
    blended, log_totals = lax.map(attend, (queries3, keys_all, values_all))
    blended_low = blended.reshape(count, width).astype(jnp.bfloat16)
    middle = leading + product(blended_low, full_out) + bias_out.astype(jnp.float32)
    normed_two, norm_two_back = jax.vjp(
        norm_rows, middle, gain_two.astype(jnp.float32), shift_two.astype(jnp.float32)
    )
    normed_two_low = normed_two.astype(jnp.bfloat16)
    hidden = product(normed_two_low, full_fc1) + bias_fc1.astype(jnp.float32)
    activated, gelu_back = jax.vjp(gelu_exact, hidden)
    activated_low = activated.astype(jnp.bfloat16)
    output = middle + product(activated_low, full_fc2) + bias_fc2.astype(jnp.float32)
    block_output = output.reshape(items, rows, width).astype(jnp.bfloat16)
    back_qkv, back_out, back_fc1, back_fc2 = (
        lax.all_gather(w_qkv, ("dp", "seq"), axis=0, tiled=True),
        lax.all_gather(w_out, ("dp", "seq"), axis=0, tiled=True),
        lax.all_gather(w_fc1, ("dp", "seq"), axis=0, tiled=True),
        lax.all_gather(w_fc2, ("dp", "seq"), axis=0, tiled=True),
    )
    out_grad = cotangent.reshape(count, width)
    upstream = out_grad.astype(jnp.float32)
    grad_fc2 = product_tleft(activated_low, out_grad)
    grad_fc2_bias = jnp.sum(upstream, axis=0)
    hidden_grad = gelu_back(product_tright(out_grad, back_fc2))[0].astype(jnp.bfloat16)
    grad_fc1 = product_tleft(normed_two_low, hidden_grad)
    grad_fc1_bias = jnp.sum(hidden_grad.astype(jnp.float32), axis=0)
    middle_part, grad_ln2_gain, grad_ln2_bias = norm_two_back(product_tright(hidden_grad, back_fc1))
    middle_grad = upstream + middle_part
    attn_grad = middle_grad.astype(jnp.bfloat16)
    grad_out = product_tleft(blended_low, attn_grad)
    grad_out_bias = jnp.sum(attn_grad.astype(jnp.float32), axis=0)
    blended_grad = (
        product_tright(attn_grad, back_out).astype(jnp.bfloat16).reshape(items, rows, width)
    )
    query_grads, row_delta, key_parts, value_parts = lax.map(
        partial(query_side, True), (queries3, keys_all, values_all, blended_grad, log_totals)
    )
    key_grads, value_grads = (
        lax.psum_scatter(
            key_parts.astype(jnp.bfloat16), "seq", scatter_dimension=1, tiled=True
        ).astype(jnp.float32),
        lax.psum_scatter(
            value_parts.astype(jnp.bfloat16), "seq", scatter_dimension=1, tiled=True
        ).astype(jnp.float32),
    )
    query_low = query_grads.reshape(count, width).astype(jnp.bfloat16)
    key_low = key_grads.reshape(count, width).astype(jnp.bfloat16)
    value_low = value_grads.reshape(count, width).astype(jnp.bfloat16)
    qkv_grad = jnp.concatenate([query_low, key_low, value_low], axis=1)
    grad_qkv = product_tleft(normed_low, qkv_grad)
    grad_q_bias = jnp.sum(query_low.astype(jnp.float32), axis=0)
    grad_v_bias = jnp.sum(value_low.astype(jnp.float32), axis=0)
    leading_part, grad_ln1_gain, grad_ln1_bias = norm_one_back(product_tright(qkv_grad, back_qkv))
    input_grad = (middle_grad + leading_part).reshape(items, rows, width)
    grad_lead_weight = jnp.sum(jnp.sum(input_grad, axis=1) * lead_times[:, None], axis=0)
    grad_lead_bias = jnp.sum(input_grad, axis=(0, 1))
    summed = (
        lax.psum_scatter(grad_qkv, ("dp", "seq"), scatter_dimension=0, tiled=True),
        lax.psum_scatter(grad_out, ("dp", "seq"), scatter_dimension=0, tiled=True),
        lax.psum_scatter(grad_fc1, ("dp", "seq"), scatter_dimension=0, tiled=True),
        lax.psum_scatter(grad_fc2, ("dp", "seq"), scatter_dimension=0, tiled=True),
        lax.psum_scatter(grad_ln1_gain, ("dp", "seq"), scatter_dimension=0, tiled=True),
        lax.psum_scatter(grad_ln1_bias, ("dp", "seq"), scatter_dimension=0, tiled=True),
        lax.psum_scatter(grad_q_bias, ("dp", "seq"), scatter_dimension=0, tiled=True),
        lax.psum_scatter(grad_v_bias, ("dp", "seq"), scatter_dimension=0, tiled=True),
        lax.psum_scatter(grad_out_bias, ("dp", "seq"), scatter_dimension=0, tiled=True),
        lax.psum_scatter(grad_ln2_gain, ("dp", "seq"), scatter_dimension=0, tiled=True),
        lax.psum_scatter(grad_ln2_bias, ("dp", "seq"), scatter_dimension=0, tiled=True),
        lax.psum_scatter(grad_fc1_bias, ("dp", "seq"), scatter_dimension=0, tiled=True),
        lax.psum_scatter(grad_fc2_bias, ("dp", "seq"), scatter_dimension=0, tiled=True),
        lax.psum_scatter(grad_lead_weight, ("dp", "seq"), scatter_dimension=0, tiled=True),
        lax.psum_scatter(grad_lead_bias, ("dp", "seq"), scatter_dimension=0, tiled=True),
    )
    return (block_output, input_grad) + tuple(summed)


def solution(mesh):
    in_specs = (
        P("dp", "seq", None),
        P("dp"),
        P("dp", "seq", None),
        P(("dp", "seq"), None),
        P(("dp", "seq"), None),
        P(("dp", "seq"), None),
        P(("dp", "seq"), None),
        P(("dp", "seq")),
        P(("dp", "seq")),
        P(("dp", "seq")),
        P(("dp", "seq")),
        P(("dp", "seq")),
        P(("dp", "seq")),
        P(("dp", "seq")),
        P(("dp", "seq")),
        P(("dp", "seq")),
        P(("dp", "seq")),
        P(("dp", "seq")),
    )
    out_specs = (
        P("dp", "seq", None),
        P("dp", "seq", None),
        P(("dp", "seq"), None),
        P(("dp", "seq"), None),
        P(("dp", "seq"), None),
        P(("dp", "seq"), None),
        P(("dp", "seq")),
        P(("dp", "seq")),
        P(("dp", "seq")),
        P(("dp", "seq")),
        P(("dp", "seq")),
        P(("dp", "seq")),
        P(("dp", "seq")),
        P(("dp", "seq")),
        P(("dp", "seq")),
        P(("dp", "seq")),
        P(("dp", "seq")),
    )
    return jax.shard_map(
        on_device, mesh=mesh, in_specs=in_specs, out_specs=out_specs, check_vma=False
    )
```

profile of v0, /device:TPU:0, one launch (start us, length us, event | category | flops | bytes accessed | tf_op | source)
XLA Modules:
  0.0 2203.3 jit_solution(13668097356900817039)
XLA Ops:
  16.4 42.9 %all-reduce.22 = (bf16[1024]{0:T(1024)(128)(2,1)S(1)}, bf16[1024]{0:T(1024)(128)(2,1)S(1)}, bf16[1024]{0:T(1024)(128)(2,1)S(1)}, bf16[1024]{0:T(1024)(128)(2,1)S...) all-reduce(bf16[1024]{0:T(1024)(128)(2,1)S(1)} %dynamic-update-slic, ...), channel_id=1, replica_groups=mesh['dp'=4,'seq'=8] {'dp','seq'}, use_global_device_ids=true, to_apply=%add.1 | all-reduce | flops 10240 | bytes 40960
  60.0 1.6 fusion.45
  61.6 1.7 multiply_reduce_fusion.7
  65.1 18.1 all-gather.8.cloned.1.call-done
  83.3 5.5 fusion.59
  88.8 2.6 copy-done.17
  91.6 1.3 copy.50
  93.0 2.8 fusion.39
  95.8 1.3 copy.49
  100.8 72.8 %all-gather = bf16[32,1,128]{2,1,0:T(2,128)(2,1)S(1)} all-gather(bf16[1,1,128]{2,1,0:T(2,128)(2,1)S(1)} %bitcast.193), channel_id=1, replica_groups=mesh['dp'=4,'seq'=8] {'dp','seq'}, dimensions={0}, use_global_device_ids=true | all-gather | bytes 8448 | tf_op jit(solution)/shard_map/all_gather | solution.py:147
  174.7 42.5 %all-gather.12.cloned.1.call-done = bf16[2,2048,1024]{1,2,0:T(8,128)(2,1)} async-done(((bf16[2,256,1024]{1,2,0:T(8,128)(2,1)}), bf16[2,2048,1024]{1,2,0:T(8,128)(2,1)}) %all-gather.12.cloned.1.call-update) | async-done | bytes 8388624 | tf_op jit(solution)/shard_map/all_gather | solution.py:187
  217.2 126.2 %all-gather.10.cloned.1.call-done = bf16[2,2048,1024]{1,2,0:T(8,128)(2,1)} async-done(((bf16[2,256,1024]{1,2,0:T(8,128)(2,1)}), bf16[2,2048,1024]{1,2,0:T(8,128)(2,1)}) %all-gather.10.cloned.1.call-update) | async-done | bytes 8388624 | tf_op jit(solution)/shard_map/all_gather | solution.py:188
  343.6 101.5 %while.26 = (s32[]{:T(128)}, bf16[2,256,1024]{2,1,0:T(8,128)(2,1)S(1)}, f32[2,16,256]{2,1,0:T(8,128)S(1)}, bf16[2,2048,1024]{1,2,0:T(8,128)(2,1)}, bf16[2,256,10...) while((s32[]{:T(128)}, bf16[2,256,1024]{2,1,0:T(8,128)(2,1)S(1)}, ...), condition=%wide.region_5.6_spmd, body=%wide.region_2.5_spmd.sunk | while | flops 2222977024 | bytes 130154592 | solution.py:190
  343.6 7.1 constant_dynamic-slice_fusion.13
  350.7 13.1 multiply_reduce_fusion.10
  363.9 14.1 fusion.128
  377.9 16.0 fusion.129
  394.2 7.1 constant_dynamic-slice_fusion.13
  401.4 13.4 multiply_reduce_fusion.10
  414.8 14.1 fusion.128
  428.8 15.8 fusion.129
  445.2 3.9 fusion.57
  450.4 29.8 %all-gather.16.cloned.1.call-done = bf16[1024,4096]{1,0:T(8,128)(2,1)} async-done(((bf16[32,4096]{1,0:T(8,128)(2,1)}), bf16[1024,4096]{1,0:T(8,128)(2,1)}) %all-gather.16.cloned.1.call-update) | async-done | bytes 8388624 | tf_op jit(solution)/shard_map/all_gather | solution.py:138
  480.2 11.8 fusion.51
  492.0 66.9 %all-gather.18.cloned.1.call-done = bf16[4096,1024]{1,0:T(8,128)(2,1)} async-done(((bf16[128,1024]{1,0:T(8,128)(2,1)}), bf16[4096,1024]{1,0:T(8,128)(2,1)}) %all-gather.18.cloned.1.call-update) | async-done | bytes 8388624 | tf_op jit(solution)/shard_map/all_gather | solution.py:139
  559.0 28.1 %convert_reduce_fusion = (f32[4096]{0:T(1024)}, bf16[512,4096]{1,0:T(8,128)(2,1)S(1)}, f32[512,4096]{1,0:T(8,128)}) fusion(f32[512,4096]{1,0:T(8,128)} %fusion.51, f32[4096]{0:T(1024)S(1)} %bitcast.186, bf16[512,1024]{1,0:T(8,128)(2,1)S(1)} %bitcast.173, bf16[4096,1024]{1,0:T(8,128)(2,1)} %all-gather.18.cloned.1.call-done), kind=kOutput, calls=%fused_computation.40 | convolution fusion | flops 4452249600 | bytes 30441472 | tf_op jit(solution)/shard_map/dot_general | solution.py:35
  587.1 5.5 multiply_reduce_fusion.2
  593.4 1.3 convert_reduce_fusion.2
  594.7 1.3 convolution_convert_fusion
  597.1 273.1 %while.27 = (s32[]{:T(128)}, bf16[2,256,1024]{2,1,0:T(8,128)(2,1)}, bf16[2,2048,1024]{2,1,0:T(8,128)(2,1)}, bf16[2,2048,1024]{2,1,0:T(8,128)(2,1)}, bf16[2,2048,...) while((s32[]{:T(128)}, bf16[2,256,1024]{2,1,0:T(8,128)(2,1)}, ...), condition=%wide.region_12.13_spmd, body=%wide.region_10.12_spmd.sunk | while | flops 8766107648 | bytes 276906240 | solution.py:223
  597.8 5.1 constant_dynamic-slice_fusion.18
  604.3 2.0 copy-done
  606.3 13.1 fusion.148
  619.4 39.1 %fusion.149 = bf16[16,64,256]{2,1,0:T(8,128)(2,1)S(1)} fusion(bf16[2048,16,64]{0,2,1:T(8,128)(2,1)} %bitcast.157, f32[16,256,2048]{2,1,0:T(8,128)} %fusion.148, f32[16,256]{1,0:T(8,128)S(1)} %dynamic-slice_bitcast_fusion.2, bf16[256,16,64]{0,2,1:T(8,128)(2,1)S(1)} %bitcast.166, bf16[2048,16,64]{0,2,1:T(8,128)(2,1)} %bitcast.161), kind=kOutput, calls=%fused_computation.24.clone.1 | convolution fusion | flops 3296729088 | bytes 43008000 | tf_op jit(solution)/shard_map/while/body/eval_jaxpr/hqk,khd->qhd/dot_general | solution.py:106
  658.5 38.0 %fusion.151 = bf16[16,64,2048]{2,1,0:T(8,128)(2,1)} fusion(bf16[256,16,64]{0,2,1:T(8,128)(2,1)S(1)} %bitcast.165, f32[16,256,2048]{2,1,0:T(8,128)} %fusion.148, f32[16,256]{1,0:T(8,128)S(1)} %dynamic-slice_bitcast_fusion.2, bf16[256,16,64]{0,2,1:T(8,128)(2,1)S(1)} %bitcast.167, bf16[2048,16,64]{0,2,1:T(8,128)(2,1)} %bitcast.162), kind=kOutput, calls=%fused_computation.23.clone.1 | convolution fusion | flops 3296729088 | bytes 43008000 | tf_op jit(solution)/shard_map/while/body/eval_jaxpr/hqk,qhd->khd/dot_general | solution.py:88
  696.5 15.7 fusion.150
  712.2 6.3 copy.97
  718.6 6.4 copy.98
  726.0 7.8 constant_dynamic-update-slice_fusion.9
  734.1 5.1 constant_dynamic-slice_fusion.18
  739.2 1.1 copy-done.1
  740.6 2.0 copy-done
  742.6 13.1 fusion.148
  755.7 39.1 %fusion.149 = bf16[16,64,256]{2,1,0:T(8,128)(2,1)S(1)} fusion(bf16[2048,16,64]{0,2,1:T(8,128)(2,1)} %bitcast.157, f32[16,256,2048]{2,1,0:T(8,128)} %fusion.148, f32[16,256]{1,0:T(8,128)S(1)} %dynamic-slice_bitcast_fusion.2, bf16[256,16,64]{0,2,1:T(8,128)(2,1)S(1)} %bitcast.166, bf16[2048,16,64]{0,2,1:T(8,128)(2,1)} %bitcast.161), kind=kOutput, calls=%fused_computation.24.clone.1 | convolution fusion | flops 3296729088 | bytes 43008000 | tf_op jit(solution)/shard_map/while/body/eval_jaxpr/hqk,khd->qhd/dot_general | solution.py:106
  794.8 38.0 %fusion.151 = bf16[16,64,2048]{2,1,0:T(8,128)(2,1)} fusion(bf16[256,16,64]{0,2,1:T(8,128)(2,1)S(1)} %bitcast.165, f32[16,256,2048]{2,1,0:T(8,128)} %fusion.148, f32[16,256]{1,0:T(8,128)S(1)} %dynamic-slice_bitcast_fusion.2, bf16[256,16,64]{0,2,1:T(8,128)(2,1)S(1)} %bitcast.167, bf16[2048,16,64]{0,2,1:T(8,128)(2,1)} %bitcast.162), kind=kOutput, calls=%fused_computation.23.clone.1 | convolution fusion | flops 3296729088 | bytes 43008000 | tf_op jit(solution)/shard_map/while/body/eval_jaxpr/hqk,qhd->khd/dot_general | solution.py:88
  832.8 15.7 fusion.150
  848.5 6.3 copy.97
  854.9 6.4 copy.98
  862.3 7.8 constant_dynamic-update-slice_fusion.9
  871.5 4.7 fusion.60
  876.3 10.6 fusion.50
  887.0 131.1 %reduce-scatter.9.cloned.1.call-done = bf16[2,256,1024]{2,1,0:T(8,128)(2,1)} async-done(((bf16[2,2048,1024]{2,1,0:T(8,128)(2,1)}), bf16[2,256,1024]{2,1,0:T(8,128)(2,1)}) %reduce-scatter.9.cloned.1.call-update) | async-done | bytes 1048592 | tf_op jit(solution)/shard_map/reduce_scatter | solution.py:230
  1018.1 152.1 %reduce-scatter.7.cloned.1.call-done = bf16[2,256,1024]{2,1,0:T(8,128)(2,1)} async-done(((bf16[2,2048,1024]{2,1,0:T(8,128)(2,1)}), bf16[2,256,1024]{2,1,0:T(8,128)(2,1)}) %reduce-scatter.7.cloned.1.call-update) | async-done | bytes 1048592 | tf_op jit(solution)/shard_map/reduce_scatter | solution.py:227
  1170.2 7.9 fusion.43
  1178.8 9.9 multiply_convert_fusion.1
  1188.7 10.6 fusion.61
  1200.4 10.8 add_convert_fusion.1
  1211.3 6.7 multiply_reduce_fusion.3
  1220.2 1.3 copy-done.12
  1221.9 43.1 %all-reduce.21 = (f32[1024]{0:T(1024)S(1)}, f32[1024]{0:T(1024)S(1)}, f32[1024]{0:T(1024)S(1)}, f32[1024]{0:T(1024)S(1)}, f32[1024]{0:T(1024)S(1)}, /*index=5*/f...) all-reduce(f32[1024]{0:T(1024)S(1)} %get-tuple-element.151, ...), channel_id=8, replica_groups=mesh['dp'=4,'seq'=8] {'dp','seq'}, use_global_device_ids=true, to_apply=%region_22.23.clone | all-reduce | flops 14336 | bytes 114688
  1271.4 45.0 %reduce-scatter.13.cloned.1.call-done = f32[32,1024]{1,0:T(8,128)} async-done(((f32[1024,1024]{1,0:T(8,128)}), f32[32,1024]{1,0:T(8,128)}) %reduce-scatter.13.cloned.1.call-update) | async-done | bytes 131088 | tf_op jit(solution)/shard_map/reduce_scatter | solution.py:247
  1316.4 358.6 %reduce-scatter.15.cloned.1.call-done = f32[32,4096]{1,0:T(8,128)} async-done(((f32[1024,4096]{1,0:T(8,128)}), f32[32,4096]{1,0:T(8,128)}) %reduce-scatter.15.cloned.1.call-update) | async-done | bytes 524304 | tf_op jit(solution)/shard_map/reduce_scatter | solution.py:248
  1675.0 161.2 %reduce-scatter.11.cloned.1.call-done = f32[32,3072]{1,0:T(8,128)} async-done(((f32[1024,3072]{1,0:T(8,128)}), f32[32,3072]{1,0:T(8,128)}) %reduce-scatter.11.cloned.1.call-update) | async-done | bytes 393232 | tf_op jit(solution)/shard_map/reduce_scatter | solution.py:246
  1836.2 360.1 %reduce-scatter.17.cloned.1.call-done = f32[128,1024]{1,0:T(8,128)} async-done(((f32[4096,1024]{1,0:T(8,128)}), f32[128,1024]{1,0:T(8,128)}) %reduce-scatter.17.cloned.1.call-update) | async-done | bytes 524304 | tf_op jit(solution)/shard_map/reduce_scatter | solution.py:249
  (232 shorter events, 36.7 us)
Async XLA Ops:
  7.2 76.1 %all-gather.8.cloned.1.call-start = ((), (), s32[]{:S(2)}) async-start(), calls=%async_computation.6 | async-start | bytes 6488064 | tf_op jit(solution)/shard_map/all_gather | solution.py:136
  7.9 209.3 %all-gather.12.cloned.1.call-start = ((), (), s32[]{:S(2)}) async-start(), calls=%async_computation.8 | async-start | bytes 9437184 | tf_op jit(solution)/shard_map/all_gather | solution.py:187
  59.3 4.7 copy-start.25
  60.0 3.5 copy-start.49
  61.6 2.4 copy-start.27
  63.4 1.3 copy-start.2
  65.1 23.7 %copy-start.18 = (bf16[512,1024]{1,0:T(8,128)(2,1)}, bf16[512,1024]{1,0:T(8,128)(2,1)S(1)}, u32[]{:S(2)}) copy-start(bf16[512,1024]{1,0:T(8,128)(2,1)S(1)} %add_convert_fusion.3) | copy-start | bytes 3145732
  88.8 2.6 copy-start.17
  91.6 9.2 copy-start.51
  92.9 250.5 %all-gather.10.cloned.1.call-start = ((), (), s32[]{:S(2)}) async-start(), calls=%async_computation.7 | async-start | bytes 9437184 | tf_op jit(solution)/shard_map/all_gather | solution.py:188
  97.2 347.9 %all-gather.14.cloned.1.call-start = ((), (), s32[]{:S(2)}) async-start(), calls=%async_computation.9 | async-start | bytes 2162688 | tf_op jit(solution)/shard_map/all_gather | solution.py:137
  97.8 382.4 %all-gather.16.cloned.1.call-start = ((), (), s32[]{:S(2)}) async-start(), calls=%async_computation.10 | async-start | bytes 8650752 | tf_op jit(solution)/shard_map/all_gather | solution.py:138
  98.3 460.6 %all-gather.18.cloned.1.call-start = ((), (), s32[]{:S(2)}) async-start(), calls=%async_computation.11 | async-start | bytes 8650752 | tf_op jit(solution)/shard_map/all_gather | solution.py:139
  98.9 919.2 %reduce-scatter.9.cloned.1.call-start = ((), (), s32[]{:S(2)}) async-start(), calls=%async_computation.13 | async-start | bytes 9437184 | tf_op jit(solution)/shard_map/reduce_scatter | solution.py:230
  343.6 101.6 %copy-start.47 = (f32[1024]{0:T(1024)S(1)}, f32[1024]{0:T(1024)}, u32[]{:S(2)}) copy-start(f32[1024]{0:T(1024)} %convert_element_type.142) | copy-start | bytes 12292
  445.1 4.0 copy-start.15
  445.1 35.0 %copy-start.39 = (f32[1024]{0:T(1024)S(1)}, f32[1024]{0:T(1024)}, u32[]{:S(2)}) copy-start(f32[1024]{0:T(1024)} %convert_element_type.143) | copy-start | bytes 12292
  445.2 35.0 %copy-start.45 = (f32[1024]{0:T(1024)S(1)}, f32[1024]{0:T(1024)}, u32[]{:S(2)}) copy-start(f32[1024]{0:T(1024)} %convert_element_type.144) | copy-start | bytes 12292
  449.1 143.5 %copy-start.35 = (f32[512]{0:T(512)}, f32[512]{0:T(512)S(1)}, u32[]{:S(2)}) copy-start(f32[512]{0:T(512)S(1)} %broadcast_multiply_fusion.1) | copy-start | bytes 6148
  450.4 142.2 %copy-start.41 = (f32[512]{0:T(512)}, f32[512]{0:T(512)S(1)}, u32[]{:S(2)}) copy-start(f32[512]{0:T(512)S(1)} %fusion.46) | copy-start | bytes 6148
  450.4 108.6 %copy-start.7 = (bf16[2,256,1024]{2,1,0:T(8,128)(2,1)S(1)}, bf16[2,256,1024]{2,1,0:T(8,128)(2,1)}, u32[]{:S(2)}) copy-start(bf16[2,256,1024]{2,1,0:T(8,128)(2,1)} %param.24) | copy-start | bytes 3145732
  450.4 108.6 %copy-start.23 = (f32[32,1,128]{2,1,0:T(1,128)S(1)}, f32[32,1,128]{2,1,0:T(1,128)}, u32[]{:S(2)}) copy-start(f32[32,1,128]{2,1,0:T(1,128)} %convert_element_type.166) | copy-start | bytes 49156
  558.9 28.2 %copy-start.10 = (f32[512,1024]{1,0:T(8,128)S(1)}, f32[512,1024]{1,0:T(8,128)}, u32[]{:S(2)}) copy-start(f32[512,1024]{1,0:T(8,128)} %copy-done.9) | copy-start | bytes 6291460
  558.9 28.2 %copy-start.52 = (bf16[1024,4096]{1,0:T(8,128)(2,1)S(1)}, bf16[1024,4096]{1,0:T(8,128)(2,1)}, u32[]{:S(2)}) copy-start(bf16[1024,4096]{1,0:T(8,128)(2,1)} %all-gather.16.cloned.1.call-done) | copy-start | bytes 25165828
  587.1 5.5 copy-start.54
  592.6 2.1 copy-start.53
  593.3 2.6 copy-start.4
  593.3 1.3 copy-start.31
  597.5 6.8 copy-start.13
  597.8 6.2 copy-start.1
  604.3 2.0 copy-start
  726.0 7.8 copy-start.14
  733.8 6.8 copy-start.13
  734.0 6.3 copy-start.1
  740.6 2.0 copy-start
  862.3 7.8 copy-start.14
  870.3 299.9 %reduce-scatter.7.cloned.1.call-start = ((), (), s32[]{:S(2)}) async-start(), calls=%async_computation.12 | async-start | bytes 9437184 | tf_op jit(solution)/shard_map/reduce_scatter | solution.py:227
  871.0 5.2 copy-start.11
  871.0 5.2 copy-start.36
  871.0 5.2 copy-start.40
  871.1 5.2 copy-start.42
  871.1 5.2 copy-start.46
  871.1 445.3 %reduce-scatter.13.cloned.1.call-start = ((), (), s32[]{:S(2)}) async-start(), calls=%async_computation.15 | async-start | bytes 4325376 | tf_op jit(solution)/shard_map/reduce_scatter | solution.py:247
  876.2 798.8 %reduce-scatter.15.cloned.1.call-start = ((), (), s32[]{:S(2)}) async-start(), calls=%async_computation.16 | async-start | bytes 17301504 | tf_op jit(solution)/shard_map/reduce_scatter | solution.py:248
  886.9 283.3 %copy-start.6 = (bf16[2,256,1024]{2,1,0:T(8,128)(2,1)S(1)}, bf16[2,256,1024]{2,1,0:T(8,128)(2,1)}, u32[]{:S(2)}) copy-start(bf16[2,256,1024]{2,1,0:T(8,128)(2,1)} %get-tuple-element.101) | copy-start | bytes 3145732
  886.9 283.3 %copy-start.19 = (bf16[512,1024]{1,0:T(8,128)(2,1)S(1)}, bf16[512,1024]{1,0:T(8,128)(2,1)}, u32[]{:S(2)}) copy-start(bf16[512,1024]{1,0:T(8,128)(2,1)} %copy-done.18) | copy-start | bytes 3145732
  886.9 949.3 %reduce-scatter.11.cloned.1.call-start = ((), (), s32[]{:S(2)}) async-start(), calls=%async_computation.14 | async-start | bytes 12976128 | tf_op jit(solution)/shard_map/reduce_scatter | solution.py:246
  1178.1 1018.1 %reduce-scatter.17.cloned.1.call-start = ((), (), s32[]{:S(2)}) async-start(), calls=%async_computation.17 | async-start | bytes 17301504 | tf_op jit(solution)/shard_map/reduce_scatter | solution.py:249
  1178.8 9.9 copy-start.8
  1200.4 10.9 copy-start.3
  1200.4 10.9 copy-start.20
  1200.4 10.9 copy-start.22
  1200.4 10.9 copy-start.26
  1200.4 10.9 copy-start.28
  1200.4 10.9 copy-start.30
  1211.3 6.7 copy-start.34
  1218.0 1.6 copy-start.5
  1218.0 1.6 copy-start.32
  1218.8 2.9 copy-start.50
  1218.8 3.1 copy-start.37
  1218.8 3.1 copy-start.38
  1218.8 3.1 copy-start.43
  1218.8 3.1 copy-start.44
  1220.2 1.3 copy-start.12
  (7 other events, 7.1 us)
Sparse Core Ops, SparseCore 0:
  10.9 72.2 all-gather.7
  93.1 124.0 all-gather.11
  219.8 123.5 all-gather.9
  346.3 54.7 all-gather.13
  403.8 76.2 all-gather.15
  483.0 75.8 all-gather.17
  870.4 147.6 reduce-scatter.8
  1022.1 147.9 reduce-scatter.6
  1173.0 143.3 reduce-scatter.12
  1319.1 355.8 reduce-scatter.14
  1681.6 154.5 reduce-scatter.10
  1839.0 357.1 reduce-scatter.16
where the time goes:
time: 2210 us; the launch traced here: 2200 us
  waiting for transfers between devices  1490 us (67%)
  matrix products  378 us (17%)
  blocking collectives  159 us (7%)
  local copies, waits for them, and re-layouts  103 us (5%)
  other arithmetic  52.1 us (2%)
    reduce_scatter x1, waiting for transfers between devices, on_device(): lax.psum_scatter(grad_fc2, ('dp', 'seq'), scatter_dimension=0, tiled=True)  360 us
    reduce_scatter x1, waiting for transfers between devices, on_device(): lax.psum_scatter(grad_fc1, ('dp', 'seq'), scatter_dimension=0, tiled=True)  359 us
    reduce_scatter x1, waiting for transfers between devices, on_device(): lax.psum_scatter(grad_qkv, ('dp', 'seq'), scatter_dimension=0, tiled=True)  161 us
    reduce_scatter x1, waiting for transfers between devices, on_device(): lax.psum_scatter(key_parts.astype(jnp.bfloat16), 'seq', scatter_dimension...  152 us
    reduce_scatter x1, waiting for transfers between devices, on_device(): lax.psum_scatter(value_parts.astype(jnp.bfloat16), 'seq', scatter_dimensi...  131 us
    all_gather x1, waiting for transfers between devices, on_device(): lax.all_gather(values_own.reshape(items, rows, width), 'seq', axis=1, til...  126 us
    unnamed x2, blocking collectives  86 us
    dot_general x2, matrix products, query_side(): jnp.einsum('hqk,khd->qhd', score_grads, split_heads(keys_all), preferred_...  78.2 us
  transfers between devices with their start and end apart: 12, of which 11 were waited for; matrix products, arithmetic and copies ran while one was open for 9% of the time, Pallas kernels for 0%

commit v1 on v0

--- a/solution.py
+++ b/solution.py
@@ -1,23 +1,587 @@
+import functools
 from functools import partial
-
-import jax
-import jax.numpy as jnp
+import jax, jax.numpy as jnp
 from jax import lax
+from jax.experimental import pallas as pl
+from jax.experimental.pallas import tpu as pltpu
 from jax.sharding import PartitionSpec as P
 
+MESH = pl.DeviceIdType.MESH
+f32, bf16 = jnp.float32, jnp.bfloat16
+LOG2E = 1.4426950408889634
+EPS = 1e-06
+
+
+def dot_nn(a, b):
+    return lax.dot_general(a, b, (((1,), (0,)), ((), ())), preferred_element_type=f32)
+
+
+def dot_nt(a, b):
+    return lax.dot_general(a, b, (((1,), (1,)), ((), ())), preferred_element_type=f32)
+
+
+def rcopy(src, dst, ssem, rsem, dev):
+    return pltpu.make_async_remote_copy(src_ref=src, dst_ref=dst, send_sem=ssem, recv_sem=rsem, device_id=dev, device_id_type=MESH)
+
+
+def place():
+    dp, seq = lax.axis_index("dp"), lax.axis_index("seq")
+    return lax.div(dp, 2), lax.rem(dp, 2), lax.div(seq, 2), lax.rem(seq, 2)
+
+
+def dev(x, c, z, y):
+    return (x * 2 + c, z * 2 + y)
+
+
+def greet(partners):
+    bar = pltpu.get_barrier_semaphore()
+    for p in partners:
+        pl.semaphore_signal(bar, inc=1, device_id=p, device_id_type=MESH)
+    pl.semaphore_wait(bar, len(partners))
+
+
+def fwd_kernel(hd, heads, tok, wp, normed, qkvT, oT, lse, own, vec, fb1, wT, bt,
+               T, Ws, k_s, o_s, st, rt, lt, sy, ry, sc, rc, scy, rcy, sa, ra, la, sz, rz, sx, rx, so, ro, lo):
+    x, c, z, y = place()
+    hg = c * 2 + y
+    W = heads * hd
+    D = T.shape[2]
+    R = T.shape[1]
+    N = qkvT.shape[1]
+    zoff = [lax.rem(z + k, 4) for k in (1, 2, 3)]
+    greet([dev(x, c, zz, y) for zz in zoff] + [dev(x, 1 - c, zz, y) for zz in zoff]
+          + [dev(x, 1 - c, z, y), dev(x, c, z, 1 - y), dev(x, 1 - c, z, 1 - y), dev(1 - x, c, z, y)])
+    sib, yp, diag, xp = dev(x, 1 - c, z, y), dev(x, c, z, 1 - y), dev(x, 1 - c, z, 1 - y), dev(1 - x, c, z, y)
+    pos = (lax.div(z, 2) * 2 + y) * 2 + lax.rem(z, 2)
+    tcp = []
+    for i in range(2):
+        zt = 2 * c + i
+        cp = rcopy(tok.at[i], T.at[pos], st.at[i], rt.at[lax.rem(z, 2)], dev(x, lax.div(z, 2), zt, y))
+        loc = pltpu.make_async_copy(tok.at[i], T.at[pos], lt)
+        @pl.when(zt != z)
+        def _():
+            cp.start()
+        @pl.when(zt == z)
+        def _():
+            loc.start()
+        tcp.append((zt, cp, loc))
+    xz = x * 4 + z
+    wloc = pltpu.make_async_copy(wp.at[hg], Ws.at[xz, hg], la)
+    wloc.start()
+    wa = []
+    for k, (d, g) in enumerate(((yp, c * 2 + 1 - y), (sib, (1 - c) * 2 + y), (diag, (1 - c) * 2 + 1 - y))):
+        cp = rcopy(wp.at[g], Ws.at[xz, hg], sa.at[k], ra.at[k], d)
+        cp.start()
+        wa.append(cp)
+    wloc.wait()
+    for cp in wa:
+        cp.wait()
+    wz = []
+    for k in range(3):
+        cp = rcopy(Ws.at[xz], Ws.at[xz], sz.at[k], rz.at[k], dev(x, c, zoff[k], y))
+        cp.start()
+        wz.append(cp)
+    wx = [rcopy(Ws.at[xz], Ws.at[xz], sx.at[3], rx.at[3], xp)]
+    wx[0].start()
+    ycp, ccp, cycp = [], [], []
+    for j in range(2):
+        src_z = 2 * c + j
+        p = hg * 2 + j
+        arr = rcopy(tok.at[0], T.at[p], st.at[0], rt.at[j], sib)
+        @pl.when(src_z != z)
+        def _():
+            arr.wait_recv()
+        @pl.when(src_z == z)
+        def _():
+            pltpu.make_async_copy(tok.at[0], T.at[p], lt).wait()
+        a = rcopy(T.at[p], T.at[p], sy.at[j], ry.at[j], yp)
+        b = rcopy(T.at[p], T.at[p], sc.at[j], rc.at[j], sib)
+        a.start()
+        b.start()
+        ycp.append(a)
+        ccp.append(b)
+    for k in range(3):
+        wz[k].wait()
+        zs = lax.rem(z + 3 - k, 4)
+        cp = rcopy(Ws.at[x * 4 + zs], Ws.at[x * 4 + zs], sx.at[k], rx.at[k], xp)
+        cp.start()
+        wx.append(cp)
+    for j in range(2):
+        ycp[j].wait()
+        p = (c * 2 + 1 - y) * 2 + j
+        cp = rcopy(T.at[p], T.at[p], scy.at[j], rcy.at[j], sib)
+        cp.start()
+        cycp.append(cp)
+    for cp in wx:
+        cp.wait()
+    for xx in range(2):
+        for zz in range(4):
+            for cc in range(2):
+                for yy in range(2):
+                    r = (xx * 2 + cc) * 8 + zz * 2 + yy
+                    blk = Ws[xx * 4 + zz, cc * 2 + yy, 0:16, 3 * W:3 * W + 128].astype(f32)
+                    vec[:, r * 32:(r + 1) * 32] = blk[:, 0:32]
+                    fb1[:, r * 128:(r + 1) * 128] = blk[8:16, :]
+                c0 = (xx * 2 + cc) * 256 + zz * 64
+                wT[:, c0:c0 + 64] = Ws[xx * 4 + zz, cc * 2:cc * 2 + 2, :, 0:3 * W].reshape(64, 3 * W).T
+    hours = jnp.zeros((1, 1), f32)
+    for zz in range(4):
+        hz = Ws[x * 4, (zz // 2) * 2, 0:16, 3 * W:3 * W + 128].astype(f32)[11:12, zz % 2:zz % 2 + 1]
+        hours = jnp.where(z == zz, hz, hours)
+    t = hours / 100.0
+    for j in range(2):
+        ccp[j].wait()
+        cycp[j].wait()
+    shift = t * vec[0:1, :] + vec[1:2, :]
+    vec[14:15, :] = jnp.broadcast_to(t, (1, D))
+    vec[15:16, :] = shift
+    gain, bias = vec[2:3, :], vec[3:4, :]
+    qb = vec[:, pl.ds(hg * W, W)].T
+    def blk(p, carry):
+        v = T[p].astype(f32) + shift
+        cen = v - jnp.mean(v, axis=-1, keepdims=True)
+        r = lax.rsqrt(jnp.mean(cen * cen, axis=-1, keepdims=True) + EPS)
+        nb = (cen * r * gain + bias).astype(bf16)
+        normed[p] = nb
+        pr = dot_nt(wT[...], nb)
+        cols = pl.ds(p * R, R)
+        qkvT[0:W, cols] = (pr[0:W] + qb[:, 4:5]).astype(bf16)
+        qkvT[W:2 * W, cols] = pr[W:2 * W].astype(bf16)
+        qkvT[2 * W:3 * W, cols] = (pr[2 * W:] + qb[:, 5:6]).astype(bf16)
+        return carry
+    lax.fori_loop(0, T.shape[0], blk, 0)
+    own[...] = T[pl.ds(hg * 2, 2)]
+    for h in range(heads):
+        k_s[h] = qkvT[W + h * hd:W + (h + 1) * hd, :].T
+    QB, KB = 2 * R, 512
+    cs = LOG2E * hd ** -0.5
+    nk = N // KB
+    def group(k, carry):
+        cc = jnp.where((k == 1) | (k == 2), 1 - c, c)
+        yy = jnp.where(k < 2, 1 - y, y)
+        g = cc * 2 + yy
+        qcols = pl.ds(g * QB, QB)
+        def head(h, carry):
+            qt = qkvT[pl.ds(h * hd, hd), qcols]
+            def scores(i):
+                return dot_nn(k_s[h, i * KB:(i + 1) * KB, :], qt)
+            m = None
+            s = scores(0)
+            for i in range(nk):
+                nxt = scores(i + 1) if i + 1 < nk else None
+                cm = jnp.max(s, axis=0, keepdims=True)
+                mn = cm if m is None else jnp.maximum(m, cm)
+                p = jnp.exp2(s * cs - mn * cs)
+                ps = jnp.sum(p, axis=0, keepdims=True)
+                vt = qkvT[pl.ds(2 * W + h * hd, hd), i * KB:(i + 1) * KB]
+                ov = dot_nn(vt, p.astype(bf16))
+                if m is None:
+                    l, o = ps, ov
+                else:
+                    a = jnp.exp2((m - mn) * cs)
+                    l = l * a + ps
+                    o = o * a + ov
+                m = mn
+                s = nxt
+            o = o / l
+            o_s[g, pl.ds(h * hd, hd), :] = o.astype(bf16)
+            oT[pl.ds(h * hd, hd), qcols] = o
+            lse[pl.ds(h, 1), qcols] = m * cs + jnp.log2(l)
+            return carry
+        lax.fori_loop(0, heads, head, 0)
+        @pl.when(k < 3)
+        def _():
+            rcopy(o_s.at[g], bt.at[hg], so.at[k], ro.at[k], dev(x, cc, z, yy)).start()
+        @pl.when(k == 3)
+        def _():
+            pltpu.make_async_copy(o_s.at[g], bt.at[hg], lo).start()
+        return carry
+    lax.fori_loop(0, 4, group, 0)
+    for k, d in enumerate((yp, diag, sib)):
+        rcopy(o_s.at[0], bt.at[hg], so.at[k], ro.at[k], d).wait()
+    pltpu.make_async_copy(o_s.at[0], bt.at[hg], lo).wait()
+    for i in range(2):
+        zt, cp, loc = tcp[i]
+        @pl.when(zt != z)
+        def _():
+            cp.wait_send()
+
+
+def forward_kernel(tok, wp, heads, hd, FF):
+    n_it, R, D = tok.shape
+    W = heads * hd
+    N = 8 * R
+    S = pltpu.SemaphoreType.DMA
+    vm = pl.BlockSpec(memory_space=pltpu.VMEM)
+    hbm = pl.BlockSpec(memory_space=pl.ANY)
+    return pl.pallas_call(
+        functools.partial(fwd_kernel, hd, heads),
+        in_specs=[hbm, hbm],
+        out_specs=[vm, vm, vm, vm, vm, vm, vm, vm, hbm],
+        out_shape=[
+            jax.ShapeDtypeStruct((8, R, D), bf16),
+            jax.ShapeDtypeStruct((3 * W, N), bf16),
+            jax.ShapeDtypeStruct((W, N), f32),
+            jax.ShapeDtypeStruct((heads, N), f32),
+            jax.ShapeDtypeStruct((2, R, D), bf16),
+            jax.ShapeDtypeStruct((16, D), f32),
+            jax.ShapeDtypeStruct((8, FF), f32),
+            jax.ShapeDtypeStruct((3 * W, D), bf16),
+            jax.ShapeDtypeStruct((4, W, 2 * R), bf16),
+        ],
+        scratch_shapes=[
+            pltpu.VMEM((8, R, D), bf16),
+            pltpu.VMEM((8, 4, 32, 3 * W + 128), bf16),
+            pltpu.VMEM((heads, N, hd), bf16),
+            pltpu.VMEM((4, W, 2 * R), bf16),
+            S((2,)), S((2,)), S, S((2,)), S((2,)), S((2,)), S((2,)), S((2,)), S((2,)),
+            S((3,)), S((3,)), S, S((3,)), S((3,)), S((4,)), S((4,)), S((3,)), S((3,)), S,
+        ],
+        compiler_params=pltpu.CompilerParams(collective_id=0, has_side_effects=True, vmem_limit_bytes=56 << 20),
+        name="forward",
+    )(tok, wp)
+
+
+def put_sum(dst, pieces):
+    total = pieces[0].astype(f32)
+    for p in pieces[1:]:
+        total = total + p.astype(f32)
+    dst[...] = total.astype(dst.dtype)
+
+
+def tail_kernel(hd, heads, dob, qkvT, oT, lse, a1, a2, a3, normed, wT, own, rows, mgrad, sums0,
+                o1, o2, o3, gq, home, sums,
+                do_s, dq_s, k1, r11, r12, r13, k2, r21, r22, r23, k3, r31, r32, r33,
+                Gb, gx, gz, go, ds_s, dr_c, dy_s, dr_y, ig, hm, vs, vr,
+                sd, rd, ld, s1, q1, s2, q2, s3, q3, lk, sg, qg, sgz, qgz, sga, qga, sdc, qdc, sdy, qdy, sh, qh, lh, sv, qv, ll):
+    x, c, z, y = place()
+    hg = c * 2 + y
+    W = heads * hd
+    N = qkvT.shape[1]
+    zoff = [lax.rem(z + k, 4) for k in (1, 2, 3)]
+    sib, yp, diag, xp = dev(x, 1 - c, z, y), dev(x, c, z, 1 - y), dev(x, 1 - c, z, 1 - y), dev(1 - x, c, z, y)
+    zp = [dev(x, c, zz, y) for zz in zoff]
+    greet(zp + [dev(x, 1 - c, zz, y) for zz in zoff] + [sib, yp, diag, xp])
+    peers = ((sib, (1 - c) * 2 + y), (yp, c * 2 + 1 - y), (diag, (1 - c) * 2 + 1 - y))
+    for k, (d, g) in enumerate(peers):
+        rcopy(dob.at[g], do_s.at[hg], sd.at[k], rd.at[k], d).start()
+    loc = pltpu.make_async_copy(dob.at[hg], do_s.at[hg], ld)
+    loc.start()
+
+    def part(ref, h, n):
+        return ref if n is None else ref.at[..., pl.ds(h * n, n), :]
+    n1, n2 = k1.shape[2] // 2, k2.shape[2] // 2
+
+    class Piece:
+        def __init__(self, i, h, n, a, k, r1, r2, r3, out, s, q, lsem, yfirst):
+            self.a, self.k, self.r1, self.r2, self.r3, self.out = [part(v, h, n) for v in (a, k, r1, r2, r3, out)]
+            self.s, self.q, self.lsem, self.yfirst, self.b = s, q, lsem, yfirst, h * 5
+            self.i = i
+        def copies(self):
+            b, s, q = self.b, self.s, self.q
+            if self.yfirst:
+                first = rcopy(self.a.at[:, :, 1 - y], self.r1, s.at[b], q.at[b], yp)
+                second = rcopy(self.k.at[1 - x], self.r2, s.at[b + 1], q.at[b + 1], xp)
+                kept = self.a.at[:, :, y]
+                mine = lambda zz: self.k.at[x, zz]
+            else:
+                first = rcopy(self.a.at[1 - x], self.r1, s.at[b], q.at[b], xp)
+                second = rcopy(self.k.at[:, 1 - y], self.r2, s.at[b + 1], q.at[b + 1], yp)
+                kept = self.a.at[x]
+                mine = lambda zz: self.k.at[zz, y]
+            zs = [rcopy(mine(zoff[j]), self.r3.at[j], s.at[b + 2 + j], q.at[b + 2 + j], zp[j]) for j in range(3)]
+            return first, second, zs, pltpu.make_async_copy(kept, self.k, self.lsem.at[self.i]), mine
+        def start(self):
+            first, _, _, keep, _ = self.copies()
+            keep.start()
+            first.start()
+        def second(self):
+            first, second, _, keep, _ = self.copies()
+            keep.wait()
+            first.wait()
+            n0, n1_ = self.k.shape[0], self.k.shape[1]
+            def add(j, carry):
+                p, q_ = lax.div(j, n1_), lax.rem(j, n1_)
+                put_sum(self.k.at[p, q_], [self.k[p, q_], self.r1[p, q_]])
+                return carry
+            lax.fori_loop(0, n0 * n1_, add, 0)
+            second.start()
+        def third(self):
+            _, second, zs, _, mine = self.copies()
+            second.wait()
+            def add(zz, carry):
+                put_sum(mine(zz), [mine(zz)[...], self.r2[zz]])
+                return carry
+            lax.fori_loop(0, 4, add, 0)
+            for cp in zs:
+                cp.start()
+        def finish(self):
+            _, _, zs, _, mine = self.copies()
+            for cp in zs:
+                cp.wait()
+            put_sum(self.out, [mine(z)[...]] + [self.r3[j] for j in range(3)])
+
+    f1 = [Piece(h, h, n1, a1, k1, r11, r12, r13, o1, s1, q1, lk, True) for h in range(2)]
+    f2 = [Piece(2 + h, h, n2, a2, k2, r21, r22, r23, o2, s2, q2, lk, False) for h in range(2)]
+    f3 = Piece(4, 0, None, a3, k3, r31, r32, r33, o3, s3, q3, lk, False)
+    f2[0].start()
+    f1[0].start()
+
+    QB, KB = N // 4, 512
+    cs = LOG2E * hd ** -0.5
+    sc = hd ** -0.5
+    nk = N // KB
+
+    def attention(k_s, v_s, dk_s, dv_s):
+        for h in range(heads):
+            k_s[h] = qkvT[W + h * hd:W + (h + 1) * hd, :].T
+            v_s[h] = qkvT[2 * W + h * hd:2 * W + (h + 1) * hd, :].T
+        dk_s[...] = jnp.zeros_like(dk_s)
+        dv_s[...] = jnp.zeros_like(dv_s)
+        loc.wait()
+        def group(k, carry):
+            @pl.when(k > 0)
+            def _():
+                rcopy(dob.at[0], do_s.at[0], sd.at[k - 1], rd.at[k - 1], sib).wait()
+            cc = jnp.where((k == 1) | (k == 3), 1 - c, c)
+            yy = jnp.where(k >= 2, 1 - y, y)
+            g = cc * 2 + yy
+            qcols = pl.ds(g * QB, QB)
+            def head(h, carry):
+                @pl.when((k == 1) & (h == 1))
+                def _():
+                    f2[1].start()
+                    f1[1].start()
+                @pl.when((k == 2) & (h == 1))
+                def _():
+                    f2[0].second()
+                @pl.when((k == 2) & (h == 3))
+                def _():
+                    f1[0].second()
+                    f3.start()
+                hr = pl.ds(h * hd, hd)
+                qt = qkvT[hr, qcols]
+                dt = do_s[g, hr, :]
+                delta = jnp.sum(dt.astype(f32) * oT[hr, qcols], axis=0, keepdims=True)
+                ls = lse[pl.ds(h, 1), qcols]
+                def first(i):
+                    ks = slice(i * KB, (i + 1) * KB)
+                    return dot_nn(k_s[h, ks, :], qt), dot_nn(v_s[h, ks, :], dt)
+                dq = None
+                cur = first(0)
+                for i in range(nk):
+                    nxt = first(i + 1) if i + 1 < nk else None
+                    s, dp = cur
+                    ks = slice(i * KB, (i + 1) * KB)
+                    p = jnp.exp2(s * cs - ls)
+                    ds = (p * (dp - delta)).astype(bf16)
+                    prt = dot_nn(qkvT[pl.ds(W + h * hd, hd), ks], ds)
+                    dq = prt if dq is None else dq + prt
+                    dk_s[h, :, ks] += dot_nt(qt, ds)
+                    dv_s[h, :, ks] += dot_nt(dt, p.astype(bf16))
+                    cur = nxt
+                dq_s[hr, qcols] = (dq * sc).astype(bf16)
+                return carry
+            lax.fori_loop(0, heads, head, 0)
+            return carry
+        lax.fori_loop(0, 4, group, 0)
+        for h in range(heads):
+            dq_s[W + h * hd:W + (h + 1) * hd, :] = (dk_s[h] * sc).astype(bf16)
+            dq_s[2 * W + h * hd:2 * W + (h + 1) * hd, :] = dv_s[h].astype(bf16)
+
+    pl.run_scoped(attention, pltpu.VMEM((heads, N, hd), bf16), pltpu.VMEM((heads, N, hd), bf16),
+                  pltpu.VMEM((heads, hd, N), f32), pltpu.VMEM((heads, hd, N), f32))
+
+    def after(nm, w_s, tok_s, mg_s, dn, lsem):
+        R = tok_s.shape[1]
+        loads = [pltpu.make_async_copy(a, b, lsem.at[i]) for i, (a, b) in enumerate(((normed, nm), (wT, w_s), (own, tok_s), (mgrad, mg_s)))]
+        for cp in loads:
+            cp.start()
+        loads[1].wait()
+        def proj(g, j):
+            cols = pl.ds(g * QB + j * R, R)
+            return dot_nn(dq_s[:, cols].T, w_s[...])
+        g_sy, g_s, g_oy = (1 - c) * 2 + 1 - y, (1 - c) * 2 + y, c * 2 + 1 - y
+        def to_sib(a, j):
+            return rcopy(ds_s.at[a, j], dr_c.at[a, j], sdc.at[a * 2 + j], qdc.at[a * 2 + j], sib)
+        def to_y(j):
+            return rcopy(dy_s.at[j], dr_y.at[j], sdy.at[j], qdy.at[j], yp)
+        for j in range(2):
+            ds_s[0, j] = proj(g_sy, j).astype(bf16)
+            to_sib(0, j).start()
+        for j in range(2):
+            mine = proj(g_oy, j)
+            to_sib(0, j).wait()
+            dy_s[j] = (mine + dr_c[0, j].astype(f32)).astype(bf16)
+            to_y(j).start()
+        f2[1].second()
+        f1[1].second()
+        loads[0].wait()
+        nm2 = nm[...].reshape(N, nm.shape[2])
+        for q in range(3):
+            t = dot_nn(dq_s[q * W:(q + 1) * W, :], nm2).astype(bf16).T
+            Gb[..., q * W:(q + 1) * W] = t.reshape(2, 2, 4, 2, Gb.shape[4], W)
+        gxc = rcopy(Gb.at[1 - x], gx, sg, qg, xp)
+        gxc.start()
+        for j in range(2):
+            ds_s[1, j] = proj(g_s, j).astype(bf16)
+            to_sib(1, j).start()
+        for j in range(2):
+            dn[j] = proj(hg, j)
+        f2[0].third()
+        f1[0].third()
+        f3.second()
+        ones = jnp.ones((8, N), bf16)
+        vs[...] = sums0[...]
+        for row, q in ((12, 0), (13, 2)):
+            tot = dot_nt(ones, dq_s[q * W:(q + 1) * W, :])
+            vs[row:row + 1, :] = jnp.zeros((1, vs.shape[1]), f32)
+            vs[row:row + 1, pl.ds(pl.multiple_of(hg * W, W), W)] = tot[0:1]
+        gxc.wait()
+        for cc in range(2):
+            for zz in range(4):
+                put_sum(Gb.at[x, cc, zz], [Gb[x, cc, zz], gx[cc, zz]])
+        gzs = [rcopy(Gb.at[x, :, zoff[j]], gz.at[j], sgz.at[j], qgz.at[j], zp[j]) for j in range(3)]
+        for cp in gzs:
+            cp.start()
+        f2[1].third()
+        f1[1].third()
+        gain = rows[2:3, :]
+        shift = rows[15:16, :]
+        acc = [jnp.zeros((1, dn.shape[2]), f32) for _ in range(3)]
+        loads[2].wait()
+        loads[3].wait()
+        homes = []
+        for j in range(2):
+            to_sib(1, j).wait()
+            to_y(j).wait()
+            u = dn[j] + dr_c[1, j].astype(f32) + dr_y[j].astype(f32)
+            v = tok_s[j].astype(f32) + shift
+            cen = v - jnp.mean(v, axis=-1, keepdims=True)
+            r = lax.rsqrt(jnp.mean(cen * cen, axis=-1, keepdims=True) + EPS)
+            xh = cen * r
+            e = u * gain
+            res = mg_s[j] + r * (e - jnp.mean(e, axis=-1, keepdims=True) - xh * jnp.mean(e * xh, axis=-1, keepdims=True))
+            ig[j] = res.astype(bf16)
+            for n, val in enumerate((u * xh, u, res)):
+                acc[n] = acc[n] + jnp.sum(val, axis=0, keepdims=True)
+            zt = 2 * c + j
+            cp = rcopy(ig.at[j], hm.at[lax.rem(z, 2)], sh.at[j], qh.at[lax.rem(z, 2)], dev(x, lax.div(z, 2), zt, y))
+            lc = pltpu.make_async_copy(ig.at[j], hm.at[lax.rem(z, 2)], lh)
+            @pl.when(zt != z)
+            def _():
+                cp.start()
+            @pl.when(zt == z)
+            def _():
+                lc.start()
+            homes.append((zt, cp, lc))
+        vs[8:9, :] = acc[0]
+        vs[9:10, :] = acc[1]
+        vs[10:11, :] = acc[2] * rows[14:15, :]
+        vs[11:12, :] = acc[2]
+        for k, d in enumerate((sib, yp, xp)):
+            cp = rcopy(vs, vr.at[k], sv.at[k], qv.at[k], d)
+            cp.start()
+            cp.wait()
+            vs[...] = vs[...] + vr[k]
+        zv = [rcopy(vs, vr.at[3 + k], sv.at[3 + k], qv.at[3 + k], zp[k]) for k in range(3)]
+        for cp in zv:
+            cp.start()
+        f3.third()
+        for cp in gzs:
+            cp.wait()
+        for cc in range(2):
+            for yy in range(2):
+                put_sum(Gb.at[x, cc, z, yy], [Gb[x, cc, z, yy]] + [gz[k, cc, yy] for k in range(3)])
+        gas = []
+        for k, (d, cc, yy) in enumerate(((sib, 1 - c, y), (yp, c, 1 - y), (diag, 1 - c, 1 - y))):
+            cp = rcopy(Gb.at[x, cc, z, yy], go.at[hg], sga.at[k], qga.at[k], d)
+            cp.start()
+            gas.append(cp)
+        lcl = pltpu.make_async_copy(Gb.at[x, c, z, y], go.at[hg], ll)
+        lcl.start()
+        for cp in zv:
+            cp.wait()
+        sums[...] = vs[...] + vr[3] + vr[4] + vr[5]
+        f2[0].finish()
+        f1[0].finish()
+        f2[1].finish()
+        f1[1].finish()
+        f3.finish()
+        lcl.wait()
+        for cp in gas:
+            cp.wait()
+        D = gq.shape[1] // 3
+        for g in range(4):
+            for q in range(3):
+                gq[:, q * D + g * W:q * D + (g + 1) * W] = go[g, :, q * W:(q + 1) * W].astype(f32)
+        for i in range(2):
+            src = 2 * c + i
+            arr = rcopy(ig.at[0], hm.at[i], sh.at[0], qh.at[i], sib)
+            @pl.when(src != z)
+            def _():
+                arr.wait_recv()
+            @pl.when(src == z)
+            def _():
+                pltpu.make_async_copy(ig.at[0], hm.at[i], lh).wait()
+            home[i] = hm[i].astype(f32)
+        for zt, cp, lc in homes:
+            @pl.when(zt != z)
+            def _():
+                cp.wait_send()
+
+    R = own.shape[1]
+    D = own.shape[2]
+    pl.run_scoped(after, pltpu.VMEM(normed.shape, bf16), pltpu.VMEM(wT.shape, bf16), pltpu.VMEM((2, R, D), bf16),
+                  pltpu.VMEM((2, R, D), f32), pltpu.VMEM((2, R, D), f32), pltpu.SemaphoreType.DMA((4,)))
+
+
+def backward_kernel(dob, qkvT, oT, lse, a1, a2, a3, normed, wT, own, rows, mgrad, sums0, heads, hd):
+    W3, N = qkvT.shape
+    W = heads * hd
+    _, R, D = own.shape
+    S = pltpu.SemaphoreType.DMA
+    V = pltpu.VMEM
+    vm = pl.BlockSpec(memory_space=pltpu.VMEM)
+    hbm = pl.BlockSpec(memory_space=pl.ANY)
+    b1, b2, b3 = a1.shape[3:], a2.shape[3:], a3.shape[3:]
+    def bufs(b, yfirst):
+        k = (2, 4) if yfirst else (4, 2)
+        return [V(k + b, bf16), V(k + b, bf16), V((4,) + b, bf16), V((3,) + b, bf16)]
+    rq = D // 32
+    return pl.pallas_call(
+        functools.partial(tail_kernel, hd, heads),
+        in_specs=[hbm, vm, vm, vm, hbm, hbm, hbm, hbm, hbm, hbm, vm, hbm, vm],
+        out_specs=[vm] * 6,
+        out_shape=[
+            jax.ShapeDtypeStruct(b1, f32), jax.ShapeDtypeStruct(b2, f32), jax.ShapeDtypeStruct(b3, f32),
+            jax.ShapeDtypeStruct((rq, 3 * D), f32), jax.ShapeDtypeStruct((2, R, D), f32), jax.ShapeDtypeStruct((16, D), f32),
+        ],
+        scratch_shapes=[V((4, W, N // 4), bf16), V((W3, N), bf16)] + bufs(b1, True) + bufs(b2, False) + bufs(b3, False) + [
+            V((2, 2, 4, 2, rq, W3), bf16), V((2, 4, 2, rq, W3), bf16), V((3, 2, 2, rq, W3), bf16), V((4, rq, W3), bf16),
+            V((2, 2, R, D), bf16), V((2, 2, R, D), bf16), V((2, R, D), bf16), V((2, R, D), bf16), V((2, R, D), bf16), V((2, R, D), bf16),
+            V((16, D), f32), V((6, 16, D), f32),
+            S((3,)), S((3,)), S, S((10,)), S((10,)), S((10,)), S((10,)), S((5,)), S((5,)), S((5,)),
+            S, S, S((3,)), S((3,)), S((3,)), S((3,)), S((4,)), S((4,)), S((2,)), S((2,)), S((2,)), S((2,)), S, S((6,)), S((6,)), S,
+        ],
+        compiler_params=pltpu.CompilerParams(collective_id=1, has_side_effects=True, vmem_limit_bytes=60 << 20),
+        name="backward",
+    )(dob, qkvT, oT, lse, a1, a2, a3, normed, wT, own, rows, mgrad, sums0)
+
+
 HEADS = 16
 
 
-epsilon = 1e-06
-
-
-def norm_rows(values, gain, shift):
+epsilon = EPS
+
+
+def norm_rows_s(values, gain, shift):
     center = values - jnp.mean(values, axis=-1, keepdims=True)
     spread = jnp.mean(center * center, axis=-1, keepdims=True)
     return center * lax.rsqrt(spread + epsilon) * gain + shift
 
 
-def gelu_exact(values):
+def gelu_exact_s(values):
     return jax.nn.gelu(values, approximate=False)
 
 
@@ -112,7 +676,7 @@
     return (query_grads, row_delta, key_grads, value_grads)
 
 
-def on_device(
+def spread_on_device(
     tokens_in,
     lead_hours,
     cotangent,
@@ -175,7 +739,7 @@
         + lead_shift.astype(jnp.float32)
     ).reshape(count, width)
     normed, norm_one_back = jax.vjp(
-        norm_rows, leading, gain_one.astype(jnp.float32), shift_one.astype(jnp.float32)
+        norm_rows_s, leading, gain_one.astype(jnp.float32), shift_one.astype(jnp.float32)
     )
     normed_low = normed.astype(jnp.bfloat16)
     projected = product(normed_low, full_qkv)
@@ -191,11 +755,11 @@
     blended_low = blended.reshape(count, width).astype(jnp.bfloat16)
     middle = leading + product(blended_low, full_out) + bias_out.astype(jnp.float32)
     normed_two, norm_two_back = jax.vjp(
-        norm_rows, middle, gain_two.astype(jnp.float32), shift_two.astype(jnp.float32)
+        norm_rows_s, middle, gain_two.astype(jnp.float32), shift_two.astype(jnp.float32)
     )
     normed_two_low = normed_two.astype(jnp.bfloat16)
     hidden = product(normed_two_low, full_fc1) + bias_fc1.astype(jnp.float32)
-    activated, gelu_back = jax.vjp(gelu_exact, hidden)
+    activated, gelu_back = jax.vjp(gelu_exact_s, hidden)
     activated_low = activated.astype(jnp.bfloat16)
     output = middle + product(activated_low, full_fc2) + bias_fc2.astype(jnp.float32)
     block_output = output.reshape(items, rows, width).astype(jnp.bfloat16)
@@ -262,46 +826,137 @@
     return (block_output, input_grad) + tuple(summed)
 
 
+def moves(mesh_shape, back):
+    seq_n = mesh_shape["seq"]
+    out = []
+    for p in range(2):
+        pairs = []
+        for dp in range(mesh_shape["dp"]):
+            for seq in range(seq_n):
+                x, c, z, y = dp // 2, dp % 2, seq // 2, seq % 2
+                i = p ^ (z % 2)
+                t = (x * 2 + z // 2) * seq_n + (2 * c + i) * 2 + y
+                s = dp * seq_n + seq
+                pairs.append((t, s) if back else (s, t))
+        out.append(pairs)
+    return out
+
+
+def pick(bit, first, second):
+    return jnp.where(bit == 0, first, second)
+
+
+def carry_out(mesh_shape, values):
+    x, c, z, y = place()
+    b = lax.rem(z, 2)
+    got = [lax.ppermute(pick(b, values[p], values[1 - p]), ("dp", "seq"), m) for p, m in enumerate(moves(mesh_shape, False))]
+    return jnp.stack([pick(b, got[0], got[1]), pick(b, got[1], got[0])])
+
+
+def carry_home(mesh_shape, values):
+    x, c, z, y = place()
+    b = lax.rem(z, 2)
+    got = [lax.ppermute(pick(b, values[p], values[1 - p]), ("dp", "seq"), m) for p, m in enumerate(moves(mesh_shape, True))]
+    return jnp.stack([pick(b, got[0], got[1]), pick(b, got[1], got[0])])
+
+
+def partner(mesh_shape, kind):
+    seq_n = mesh_shape["seq"]
+    n = seq_n * mesh_shape["dp"]
+    if kind == "core":
+        return [(s, s ^ seq_n) for s in range(n)]
+    return [(s, s ^ 1) for s in range(n)]
+
+
+def norm_rows(values, gain, shift):
+    center = values - jnp.mean(values, axis=-1, keepdims=True)
+    spread = jnp.mean(center * center, axis=-1, keepdims=True)
+    return center * lax.rsqrt(spread + EPS) * gain + shift
+
+
+def gelu_exact(values):
+    return jax.nn.gelu(values, approximate=False)
+
+
+def mm(a, b, ca, cb):
+    return lax.dot_general(a, b, (((ca,), (cb,)), ((), ())), preferred_element_type=f32)
+
+
+def on_device(mesh_shape, tokens_in, lead_hours, cotangent, w_qkv, w_out, w_fc1, w_fc2, ln1_gain, ln1_bias, q_bias, v_bias,
+              out_bias, ln2_gain, ln2_bias, fc1_bias, fc2_bias, lead_weight, lead_bias):
+    AX = ("dp", "seq")
+    x, c, z, y = place()
+    hg = c * 2 + y
+    _, R, D = tokens_in.shape
+    FF = w_fc1.shape[1]
+    hd = D // HEADS
+    heads = HEADS // 4
+    W = heads * hd
+    rows = w_qkv.shape[0]
+    small = jnp.zeros((32, 128), bf16)
+    for k, v in enumerate((lead_weight, lead_bias, ln1_gain, ln1_bias, q_bias, v_bias, out_bias, ln2_gain, ln2_bias, fc2_bias)):
+        small = small.at[k, :rows].set(v)
+    small = small.at[10].set(fc1_bias).at[11, :2].set(lead_hours.astype(bf16))
+    slices = w_qkv.reshape(rows, 3, 4, W).transpose(2, 0, 1, 3).reshape(4, rows, 3 * W)
+    wp = jnp.concatenate([slices, jnp.broadcast_to(small, (4, 32, 128))], axis=2)
+    normed, qkvT, oT, lse, own, vec, fb1, wfull, bt = forward_kernel(tokens_in, wp, heads, hd, FF)
+    full_out = lax.all_gather(w_out, AX, axis=0, tiled=True)
+    full_fc1 = lax.all_gather(w_fc1, AX, axis=0, tiled=True)
+    full_fc2 = lax.all_gather(w_fc2, AX, axis=0, tiled=True)
+    upstream_low = carry_out(mesh_shape, cotangent).reshape(2 * R, D)
+    bias_fc1 = fb1[2:3]
+    leading = own.reshape(2 * R, D).astype(f32) + vec[15:16]
+    blendedT = bt.reshape(D, 2 * R)
+    middle = leading + mm(blendedT, full_out, 0, 0) + vec[6:7]
+    normed2, norm2_back = jax.vjp(norm_rows, middle, vec[7:8], vec[8:9])
+    normed2 = normed2.astype(bf16)
+    hidden = mm(normed2, full_fc1, 1, 0) + bias_fc1
+    activated, gelu_back = jax.vjp(gelu_exact, hidden)
+    activated = activated.astype(bf16)
+    output = middle + mm(activated, full_fc2, 1, 0) + vec[9:10]
+    block_output = carry_home(mesh_shape, output.astype(bf16).reshape(2, R, D))
+    upstream = upstream_low.astype(f32)
+    core = partner(mesh_shape, "core")
+    def chip_sum(left, right, rows):
+        cut = left.reshape(2 * R, 2, 2, -1)
+        def half(which):
+            return mm(lax.dynamic_index_in_dim(cut, which, 2, keepdims=False).reshape(2 * R, -1), right, 0, 0)
+        there = lax.ppermute(half(1 - c).astype(bf16), AX, core)
+        both = (half(c) + there.astype(f32)).astype(bf16)
+        return both.reshape(2, 4, 2, rows, -1)
+    a2 = chip_sum(activated, upstream_low, w_fc2.shape[0])
+    grad_fc2_bias = jnp.sum(upstream, axis=0)
+    hidden_grad = gelu_back(mm(upstream_low, full_fc2, 1, 1))[0].astype(bf16)
+    a1 = chip_sum(normed2, hidden_grad, rows)
+    grad_fc1_bias = jnp.sum(hidden_grad.astype(f32), axis=0)
+    middle_part, g_ln2_gain, g_ln2_bias = norm2_back(mm(hidden_grad, full_fc1, 1, 1))
+    middle_grad = upstream + middle_part
+    attn_grad = middle_grad.astype(bf16)
+    dob = mm(full_out, attn_grad, 1, 1).astype(bf16).reshape(4, W, 2 * R)
+    a3 = chip_sum(blendedT.T, attn_grad, rows)
+    grad_out_bias = jnp.sum(attn_grad.astype(f32), axis=0)
+    sums0 = jnp.concatenate([grad_out_bias[None], g_ln2_gain.reshape(1, D), g_ln2_bias.reshape(1, D), grad_fc2_bias[None],
+                             grad_fc1_bias.reshape(-1, D), jnp.zeros((12 - FF // D, D), f32)])
+    grad_fc1, grad_fc2, grad_out, grad_qkv, home, sums = backward_kernel(
+        dob, qkvT, oT, lse, a1, a2, a3, normed, wfull, own, vec, middle_grad.reshape(2, R, D), sums0, heads, hd)
+    index = (x * 2 + c) * 8 + z * 2 + y
+    mine = lax.dynamic_slice(sums, (0, index * rows), (16, rows))
+    g_fc1_bias = lax.dynamic_slice(sums[4:4 + FF // D].reshape(FF), (index * fc1_bias.shape[0],), (fc1_bias.shape[0],))
+    return (block_output, home, grad_qkv, grad_out, grad_fc1, grad_fc2, mine[8], mine[9], mine[12], mine[13], mine[0],
+            mine[1], mine[2], g_fc1_bias, mine[3], mine[10], mine[11])
+
+
+def choose(mesh_shape, *args):
+    items, rows = args[0].shape[0], args[3].shape[0]
+    planes = mesh_shape["seq"] // 2
+    if items == 2 and planes == 2 * items and mesh_shape["dp"] == 4 and rows % 16 == 0:
+        return on_device(mesh_shape, *args)
+    return spread_on_device(*args)
+
+
 def solution(mesh):
-    in_specs = (
-        P("dp", "seq", None),
-        P("dp"),
-        P("dp", "seq", None),
-        P(("dp", "seq"), None),
-        P(("dp", "seq"), None),
-        P(("dp", "seq"), None),
-        P(("dp", "seq"), None),
-        P(("dp", "seq")),
-        P(("dp", "seq")),
-        P(("dp", "seq")),
-        P(("dp", "seq")),
-        P(("dp", "seq")),
-        P(("dp", "seq")),
-        P(("dp", "seq")),
-        P(("dp", "seq")),
-        P(("dp", "seq")),
-        P(("dp", "seq")),
-        P(("dp", "seq")),
-    )
-    out_specs = (
-        P("dp", "seq", None),
-        P("dp", "seq", None),
-        P(("dp", "seq"), None),
-        P(("dp", "seq"), None),
-        P(("dp", "seq"), None),
-        P(("dp", "seq"), None),
-        P(("dp", "seq")),
-        P(("dp", "seq")),
-        P(("dp", "seq")),
-        P(("dp", "seq")),
-        P(("dp", "seq")),
-        P(("dp", "seq")),
-        P(("dp", "seq")),
-        P(("dp", "seq")),
-        P(("dp", "seq")),
-        P(("dp", "seq")),
-        P(("dp", "seq")),
-    )
-    return jax.shard_map(
-        on_device, mesh=mesh, in_specs=in_specs, out_specs=out_specs, check_vma=False
-    )
+    big, rows, vec = P("dp", "seq", None), P(("dp", "seq"), None), P(("dp", "seq"))
+    in_specs = (big, P("dp"), big) + (rows,) * 4 + (vec,) * 11
+    out_specs = (big, big) + (rows,) * 4 + (vec,) * 11
+    body = functools.partial(choose, dict(mesh.shape))
+    return jax.shard_map(body, mesh=mesh, in_specs=in_specs, out_specs=out_specs, check_vma=False)

time: 2210 us -> 590 us (0.27)
  waiting for transfers between devices: 1490 us -> 69.3 us
  Pallas kernels: 0 us -> 299 us
  matrix products: 378 us -> 88.4 us
  blocking collectives: 159 us -> 0 us
  other arithmetic: 52.1 us -> 21.3 us
    reduce_scatter x6 -> x0, waiting for transfers between devices: 1210 us -> none  [the longest x1 360 us: on_device(): lax.psum_scatter(grad_fc2, ('dp', 'seq'), scatter_dimension=0, tiled=True)]
    pallas_call x0 -> x2, Pallas kernels: none -> 299 us  [the longest x1 182 us: backward_kernel(): pl.pallas_call(functools.partial(tail_kernel, hd, heads), in_specs=[hbm,...]
    dot_general x24 -> x12, matrix products: 378 us -> 88.4 us  [mm(): lax.dot_general(a, b, (((ca,), (cb,)), ((), ())), preferred_element_type=...]
    all_gather x6 -> x3, waiting for transfers between devices: 284 us -> 67.3 us  [the longest x1 67.2 us: on_device(): full_fc2 = lax.all_gather(w_fc2, AX, axis=0, tiled=True)]
    unnamed x2 -> x0, blocking collectives: 86 us -> none
    all_gather x1 -> x0, blocking collectives: 72.8 us -> none  [on_device(): lax.all_gather(fc1_bias, ('dp', 'seq'), axis=0, tiled=True)]
    dynamic_update_slice x14 -> x0, local copies, waits for them, and re-layouts: 43.6 us -> none  [the longest x6 41 us: on_device(): lax.map(partial(query_side, True), (queries3, keys_all, values_all, blend...]
    reduce_sum x8 -> x1, other arithmetic: 30.5 us -> 1.73 us  [on_device(): grad_out_bias = jnp.sum(attn_grad.astype(f32), axis=0)]
  transfers between devices with their start and end apart: 12 -> 10, of which waited for: 11 -> 1; matrix products, arithmetic and copies ran while one was open for 9% -> 14% of each run, Pallas kernels for 0% -> 20%
where the time goes in v1:
time: 590 us; the launch traced here: 585 us
  Pallas kernels  299 us (51%)
  matrix products  88.4 us (15%)
  local copies, waits for them, and re-layouts  81.1 us (14%)
  waiting for transfers between devices  69.3 us (12%)
  other arithmetic  21.3 us (4%)
  between operations  14.4 us (2%)
  starting transfers between devices  11.5 us (2%)
    pallas_call x1, Pallas kernels, backward_kernel(): pl.pallas_call(functools.partial(tail_kernel, hd, heads), in_specs=[hbm,...  182 us
    pallas_call x1, Pallas kernels, forward_kernel(): pl.pallas_call(functools.partial(fwd_kernel, hd, heads), in_specs=[hbm, h...  117 us
    dot_general x12, matrix products, mm(): lax.dot_general(a, b, (((ca,), (cb,)), ((), ())), preferred_element_type=...  88.4 us
    all_gather x1, waiting for transfers between devices, on_device(): full_fc2 = lax.all_gather(w_fc2, AX, axis=0, tiled=True)  67.2 us
    unnamed x45, local copies, waits for them, and re-layouts  39.1 us
    dynamic_slice x3, local copies, waits for them, and re-layouts, half(): lax.dynamic_index_in_dim(cut, which, 2, keepdims=False).reshape(2 * R, -1)  15.6 us
  transfers between devices with their start and end apart: 10, of which 1 were waited for; matrix products, arithmetic and copies ran while one was open for 14% of the time, Pallas kernels for 20%

profile of v1, /device:TPU:0, one launch (start us, length us, event | category | flops | bytes accessed | tf_op | source)
XLA Modules:
  0.0 585.0 jit_solution(15519731501872005735)
XLA Ops:
  7.2 0.7 all-gather.4.cloned.1.call-update
  8.0 0.7 all-gather.6.cloned.1.call-update
  8.7 0.7 all-gather.8.cloned.1.call-update
  9.4 1.3 select_bitcast_fusion.3
  10.7 0.7 collective-permute-start.2
  11.4 3.1 collective-permute-start.3
  15.1 1.1 reshape.487
  16.5 0.7 scatter.40
  17.2 0.8 scatter.41
  18.0 0.8 scatter.44
  18.8 0.8 scatter.45
  19.6 0.8 scatter.46
  20.4 0.8 scatter.49
  21.2 0.8 scatter.50
  22.0 0.8 scatter.51
  22.8 0.8 scatter.54
  23.6 0.8 scatter.55
  24.4 0.8 scatter.56
  25.4 0.7 pad_maximum_fusion.2.wp
  26.1 117.3 %forward.1 = (bf16[8,256,1024]{2,1,0:T(8,128)(2,1)}, bf16[768,2048]{1,0:T(8,128)(2,1)}, f32[256,2048]{1,0:T(8,128)}, f32[4,2048]{1,0:T(4,128)}, bf16[2,256,1024]...) custom-call(bf16[2,256,1024]{2,1,0:T(8,128)(2,1)} %tok.1, ...), custom_call_target="tpu_custom_call" | custom-call | tf_op jit(solution)/shard_map/forward/pallas_call | solution.py:217
  143.4 0.9 slice.294
  144.4 2.3 constant_dynamic-slice_fusion.1
  146.7 0.9 fusion.13
  147.7 0.8 copy-done.2
  148.7 1.1 pad_maximum_fusion.1
  149.8 3.6 fusion.14
  153.7 1.4 add_convert_fusion.5
  155.1 1.8 reshape.504
  156.9 3.5 constant_dynamic-slice_fusion.5
  160.4 3.7 copy.44
  164.1 11.5 %fusion.15 = f32[512,4096]{1,0:T(8,128)} fusion(bf16[512,1024]{1,0:T(8,128)(2,1)} %add_convert_fusion.5, bf16[1024,4096]{1,0:T(8,128)(2,1)} %all-gather.6.cloned.1.call-done), kind=kOutput, calls=%fused_computation.78 | convolution fusion | flops 4294967296 | bytes 17825792 | tf_op jit(solution)/shard_map/dot_general | solution.py:882
  175.7 67.2 %all-gather.8.cloned.1.call-done = bf16[4096,1024]{1,0:T(8,128)(2,1)} async-done(((bf16[128,1024]{1,0:T(8,128)(2,1)}), bf16[4096,1024]{1,0:T(8,128)(2,1)}) %all-gather.8.cloned.1.call-update) | async-done | bytes 8388624 | tf_op jit(solution)/shard_map/all_gather | solution.py:905
  242.9 28.0 %convert_reduce_fusion = (f32[4096]{0:T(1024)S(1)}, bf16[512,4096]{1,0:T(8,128)(2,1)S(1)}, f32[512,4096]{1,0:T(8,128)}) fusion(f32[512,4096]{1,0:T(8,128)} %fusion.15, f32[4096]{0:T(1024)S(1)} %bitcast.130, bf16[512,1024]{1,0:T(8,128)(2,1)S(1)} %bitcast.111, bf16[4096,1024]{1,0:T(8,128)(2,1)} %all-gather.8.cloned.1.call-done), kind=kOutput, calls=%fused_computation.2 | convolution fusion | flops 4452249600 | bytes 30441472 | tf_op jit(solution)/shard_map/dot_general | solution.py:882
  271.0 6.2 %multiply_reduce_fusion = (f32[1024]{0:T(1024)S(1)}, f32[512]{0:T(512)S(1)}, f32[1024]{0:T(1024)S(1)}, f32[512,1024]{1,0:T(8,128)}) fusion(f32[512,1024]{1,0:T(8,128)S(1)} %get-tuple-element.232, f32[512]{0:T(512)S(1)} %fusion.9, f32[512]{0:T(512)S(1)} %broadcast_multiply_fusion, f32[1024]{0:T(1024)S(1)} %bitcast.133, ...), kind=kOutput, calls=%fused_computation.27 | convolution fusion | flops 4299159040 | bytes 16795648 | tf_op jit(solution)/shard_map/dot_general | solution.py:882
  277.2 9.7 %multiply_convert_fusion = bf16[512,4096]{1,0:T(8,128)(2,1)} fusion(f32[512,4096]{1,0:T(8,128)} %get-tuple-element.196, f32[512,4096]{1,0:T(8,128)} %fusion.15, f32[4096]{0:T(1024)S(1)} %bitcast.131), kind=kLoop, calls=%fused_computation.6 | loop fusion | flops 8388608 | bytes 20987904 | tf_op jit(solution)/shard_map/convert_element_type | solution.py:915
  286.9 7.8 %reshape.508 = bf16[512,2,2,1024]{3,2,1,0:T(2,128)(2,1)} reshape(bf16[512,4096]{1,0:T(8,128)(2,1)} %multiply_convert_fusion) | data formatting | bytes 8388608 | tf_op jit(solution)/shard_map/reshape | solution.py:921
  294.8 6.8 %convolution_convert_fusion = bf16[512,4096]{1,0:T(8,128)(2,1)} fusion(bf16[512,512]{0,1:T(8,128)(2,1)} %bitcast.125, bf16[512,4096]{1,0:T(8,128)(2,1)} %copy-done.13), kind=kOutput, calls=%fused_computation.20 | convolution fusion | flops 2149580800 | bytes 8912896 | tf_op jit(solution)/shard_map/dot_general | solution.py:882
  301.6 9.8 %constant_dynamic-slice_fusion.3 = (bf16[512,2,1,1024]{3,2,1,0:T(2,128)(2,1)}, bf16[512,2,1,1024]{3,2,1,0:T(2,128)(2,1)}) fusion(bf16[512,2,2,1024]{3,2,1,0:T(2,128)(2,1)S(1)} %copy-done, s32[]{:T(128)S(6)} %select_n.75, s32[]{:T(128)S(6)} %select_n.74), kind=kLoop, calls=%fused_computation.58 | loop fusion | bytes 8388616 | tf_op jit(solution)/shard_map/jit(dynamic_index_in_dim)/dynamic_slice | solution.py:923
  311.4 10.7 %copy.46 = bf16[512,2,1,1024]{0,3,1,2:T(8,128)(2,1)} copy(bf16[512,2,1,1024]{3,2,1,0:T(2,128)(2,1)} %get-tuple-element.202) | data formatting | bytes 4194304
  322.1 6.1 %convolution_convert_fusion.1 = bf16[2048,1024]{1,0:T(8,128)(2,1)} fusion(bf16[512,2048]{0,1:T(8,128)(2,1)} %bitcast.121, bf16[512,1024]{1,0:T(8,128)(2,1)S(1)} %bitcast.112), kind=kOutput, calls=%fused_computation.21 | convolution fusion | flops 2149580800 | bytes 7340032 | tf_op jit(solution)/shard_map/dot_general | solution.py:882
  329.4 1.7 convert_reduce_fusion.2
  331.1 1.7 convolution_convert_fusion.3
  333.2 4.6 add_convert_fusion.4
  337.8 1.0 broadcast_select_fusion.1
  338.8 5.4 collective-permute-start
  344.2 1.5 collective-permute-start.1
  345.9 3.7 copy.43
  349.6 3.2 fusion.8
  352.8 1.3 copy.38
  354.2 9.0 %copy.45 = bf16[512,2,1,1024]{0,3,1,2:T(8,128)(2,1)S(1)} copy(bf16[512,2,1,1024]{3,2,1,0:T(2,128)(2,1)} %get-tuple-element.203) | data formatting | bytes 4194304
  363.1 1.3 concatenate.31.sums0
  364.4 1.3 select_bitcast_fusion.5
  365.7 1.1 pad_maximum_fusion
  366.8 3.4 add_convert_fusion.3
  370.2 6.6 %add_convert_fusion = bf16[2048,1024]{1,0:T(8,128)(2,1)} fusion(bf16[2048,1024]{1,0:T(8,128)(2,1)} %collective-permute-done.5, bf16[512,2048]{0,1:T(8,128)(2,1)S(1)} %bitcast.120, bf16[512,1024]{1,0:T(8,128)(2,1)S(1)} %bitcast.113), kind=kOutput, calls=%fused_computation.3 | convolution fusion | flops 2153775104 | bytes 11534336 | tf_op jit(solution)/shard_map/dot_general | solution.py:882
  376.8 6.7 %add_convert_fusion.1 = bf16[512,4096]{1,0:T(8,128)(2,1)} fusion(bf16[512,4096]{1,0:T(8,128)(2,1)} %collective-permute-done.4, bf16[512,512]{0,1:T(8,128)(2,1)S(1)} %bitcast.124, bf16[512,4096]{1,0:T(8,128)(2,1)S(1)} %copy-done.14), kind=kOutput, calls=%fused_computation.4 | convolution fusion | flops 2153775104 | bytes 13107200 | tf_op jit(solution)/shard_map/dot_general | solution.py:882
  383.5 181.6 %backward.1 = (f32[32,4096]{1,0:T(8,128)}, f32[128,1024]{1,0:T(8,128)}, f32[32,1024]{1,0:T(8,128)}, f32[32,3072]{1,0:T(8,128)}, f32[2,256,1024]{2,1,0:T(8,128)}, /*index=5*/f32[16,1024]{1,0:T(8,128)}) custom-call(bf16[4,256,512]{2,1,0:T(8,128)(2,1)} %bitcast.114, bf16[768,2048]{1,0:T(8,128)(2,1)} %get-tuple-element.180.qkvT, ...), custom_call_target="tpu_custom_call" | custom-call | tf_op jit(solution)/shard_map/backward/pallas_call | solution.py:552
  565.1 0.8 slice_bitcast_fusion
  566.4 1.5 dynamic-slice_bitcast_fusion
  568.0 3.2 copy.68
  571.1 1.8 copy.69
  572.9 1.6 copy.70
  574.4 1.9 copy.71
  576.3 1.9 copy.72
  (66 shorter events, 4.3 us)
Async XLA Ops:
  7.2 142.6 %all-gather.4.cloned.1.call-start = ((), (), s32[]{:S(2)}) async-start(), calls=%async_computation | async-start | bytes 2162688 | tf_op jit(solution)/shard_map/all_gather | solution.py:903
  7.9 156.2 %all-gather.6.cloned.1.call-start = ((), (), s32[]{:S(2)}) async-start(), calls=%async_computation.1 | async-start | bytes 8650752 | tf_op jit(solution)/shard_map/all_gather | solution.py:904
  8.7 234.3 %all-gather.8.cloned.1.call-start = ((), (), s32[]{:S(2)}) async-start(), calls=%async_computation.2 | async-start | bytes 8650752 | tf_op jit(solution)/shard_map/all_gather | solution.py:905
  10.7 136.9 %collective-permute-start.2 = (bf16[256,1024]{1,0:T(8,128)(2,1)S(1)}, bf16[256,1024]{1,0:T(8,128)(2,1)S(1)}, u32[]{:S(2)}, u32[]{:S(2)}) collective-permute-start(bf16[256,1024]{1,0:T(8,128)(2,1)S(1)} %get-tuple-element.214), channel_id=1, source_target_pairs={{0,0},{1,1},{2,2},{3,3},{4,8},{5,9},{6,10},{7,11},{8,4},{9,5},{10,... | collective-permute-start | bytes 1572872 | tf_op jit(solution)/shard_map/ppermute | solution.py:852
  11.4 136.2 %collective-permute-start.3 = (bf16[256,1024]{1,0:T(8,128)(2,1)S(1)}, bf16[256,1024]{1,0:T(8,128)(2,1)S(1)}, u32[]{:S(2)}, u32[]{:S(2)}) collective-permute-start(bf16[256,1024]{1,0:T(8,128)(2,1)S(1)} %get-tuple-element.215), channel_id=1, source_target_pairs={{0,2},{1,3},{2,0},{3,1},{4,10},{5,11},{6,8},{7,9},{8,6},{9,7},{10,... | collective-permute-start | bytes 1572872 | tf_op jit(solution)/shard_map/ppermute | solution.py:852
  147.7 0.8 copy-start.2
  147.7 1.0 copy-start.4
  164.1 78.8 %copy-start.6 = (bf16[2,256,1024]{2,1,0:T(8,128)(2,1)S(1)}, bf16[2,256,1024]{2,1,0:T(8,128)(2,1)}, u32[]{:S(2)}) copy-start(bf16[2,256,1024]{2,1,0:T(8,128)(2,1)} %pad_maximum_fusion.1) | copy-start | bytes 3145732
  242.9 28.1 %copy-start.12 = (bf16[1024,4096]{1,0:T(8,128)(2,1)S(1)}, bf16[1024,4096]{1,0:T(8,128)(2,1)}, u32[]{:S(2)}) copy-start(bf16[1024,4096]{1,0:T(8,128)(2,1)} %all-gather.6.cloned.1.call-done) | copy-start | bytes 25165828
  271.0 6.2 %copy-start.13 = (bf16[512,4096]{1,0:T(8,128)(2,1)}, bf16[512,4096]{1,0:T(8,128)(2,1)S(1)}, u32[]{:S(2)}) copy-start(bf16[512,4096]{1,0:T(8,128)(2,1)S(1)} %get-tuple-element.195) | copy-start | bytes 12582916
  294.8 6.8 %copy-start = (bf16[512,2,2,1024]{3,2,1,0:T(2,128)(2,1)S(1)}, bf16[512,2,2,1024]{3,2,1,0:T(2,128)(2,1)}, u32[]{:S(2)}) copy-start(bf16[512,2,2,1024]{3,2,1,0:T(2,128)(2,1)} %reshape.508) | copy-start | bytes 12582916
  322.1 6.6 %copy-start.8 = (f32[512,1024]{1,0:T(8,128)S(1)}, f32[512,1024]{1,0:T(8,128)}, u32[]{:S(2)}) copy-start(f32[512,1024]{1,0:T(8,128)} %get-tuple-element.233) | copy-start | bytes 6291460
  322.1 11.0 %slice-start = ((s8[8388608]{0:T(1024)(128)(4,1)}), s8[4194304]{0:T(1024)(128)(4,1)S(1)}, s32[]{:S(2)}) async-start(s8[8388608]{0:T(1024)(128)(4,1)} %bitcast.153), calls=%async_computation.3 | async-start | bytes 8388608
  328.2 2.9 copy-start.11
  328.2 4.9 copy-start.1
  328.2 41.9 %collective-permute-start.5 = (bf16[2048,1024]{1,0:T(8,128)(2,1)}, bf16[2048,1024]{1,0:T(8,128)(2,1)}, u32[]{:S(2)}, u32[]{:S(2)}) collective-permute-start(bf16[2048,1024]{1,0:T(8,128)(2,1)} %convolution_convert_fusion.1), channel_id=1, source_target_pairs={{0,8},{1,9},{2,10},{3,11},{4,12},{5,13},{6,14},{7,15},{8,0},{9,1},... | collective-permute-start | bytes 12582920 | tf_op jit(solution)/shard_map/ppermute | solution.py:924
  328.5 48.3 %collective-permute-start.4 = (bf16[512,4096]{1,0:T(8,128)(2,1)}, bf16[512,4096]{1,0:T(8,128)(2,1)}, u32[]{:S(2)}, u32[]{:S(2)}) collective-permute-start(bf16[512,4096]{1,0:T(8,128)(2,1)} %convolution_convert_fusion), channel_id=1, source_target_pairs={{0,8},{1,9},{2,10},{3,11},{4,12},{5,13},{6,14},{7,15},{8,0},{9,1},... | collective-permute-start | bytes 12582920 | tf_op jit(solution)/shard_map/ppermute | solution.py:924
  328.7 4.5 slice-start.1
  331.1 2.0 copy-start.9
  332.9 33.9 %collective-permute-start.6 = (bf16[512,1024]{1,0:T(8,128)(2,1)}, bf16[512,1024]{1,0:T(8,128)(2,1)}, u32[]{:S(2)}, u32[]{:S(2)}) collective-permute-start(bf16[512,1024]{1,0:T(8,128)(2,1)} %convolution_convert_fusion.3), channel_id=1, source_target_pairs={{0,8},{1,9},{2,10},{3,11},{4,12},{5,13},{6,14},{7,15},{8,0},{9,1},... | collective-permute-start | bytes 3145736 | tf_op jit(solution)/shard_map/ppermute | solution.py:924
  333.2 12.5 %copy-start.3 = (bf16[1,256,1024]{2,1,0:T(8,128)(2,1)S(1)}, bf16[1,256,1024]{2,1,0:T(8,128)(2,1)}, u32[]{:S(2)}) copy-start(bf16[1,256,1024]{2,1,0:T(8,128)(2,1)} %copy-done.2) | copy-start | bytes 1572868
  333.2 12.5 %copy-start.5 = (bf16[1,256,1024]{2,1,0:T(8,128)(2,1)S(1)}, bf16[1,256,1024]{2,1,0:T(8,128)(2,1)}, u32[]{:S(2)}) copy-start(bf16[1,256,1024]{2,1,0:T(8,128)(2,1)} %copy-done.4) | copy-start | bytes 1572868
  338.8 25.6 %collective-permute-start = (bf16[256,1024]{1,0:T(8,128)(2,1)}, bf16[256,1024]{1,0:T(8,128)(2,1)}, u32[]{:S(2)}, u32[]{:S(2)}) collective-permute-start(bf16[256,1024]{1,0:T(8,128)(2,1)} %get-tuple-element.210), channel_id=1, source_target_pairs={{0,0},{1,1},{2,2},{3,3},{8,4},{9,5},{10,6},{11,7},{4,8},{5,9},{6,1... | collective-permute-start | bytes 1572872 | tf_op jit(solution)/shard_map/ppermute | solution.py:859
  344.2 20.2 %collective-permute-start.1 = (bf16[256,1024]{1,0:T(8,128)(2,1)}, bf16[256,1024]{1,0:T(8,128)(2,1)}, u32[]{:S(2)}, u32[]{:S(2)}) collective-permute-start(bf16[256,1024]{1,0:T(8,128)(2,1)} %get-tuple-element.211), channel_id=1, source_target_pairs={{2,0},{3,1},{0,2},{1,3},{10,4},{11,5},{8,6},{9,7},{6,8},{7,9},{4,1... | collective-permute-start | bytes 1572872 | tf_op jit(solution)/shard_map/ppermute | solution.py:859
  352.8 17.4 %copy-start.7 = (bf16[2,256,1024]{2,1,0:T(8,128)(2,1)S(1)}, bf16[2,256,1024]{2,1,0:T(8,128)(2,1)}, u32[]{:S(2)}) copy-start(bf16[2,256,1024]{2,1,0:T(8,128)(2,1)} %pad_maximum_fusion.1) | copy-start | bytes 3145732
  370.2 6.7 %copy-start.10 = (bf16[512,2,1,256]{0,3,1,2:T(8,128)(2,1)S(1)}, bf16[512,2,1,256]{0,3,1,2:T(8,128)(2,1)}, u32[]{:S(2)}) copy-start(bf16[512,2,1,256]{0,3,1,2:T(8,128)(2,1)} %copy.43) | copy-start | bytes 1572868
  370.2 6.6 %copy-start.14 = (bf16[512,4096]{1,0:T(8,128)(2,1)S(1)}, bf16[512,4096]{1,0:T(8,128)(2,1)}, u32[]{:S(2)}) copy-start(bf16[512,4096]{1,0:T(8,128)(2,1)} %copy-done.13) | copy-start | bytes 12582916
Sparse Core Ops, SparseCore 0:
  11.0 71.9 all-gather.3
  86.0 77.9 all-gather.5
  167.0 75.8 all-gather.7

commit v2 on v1

--- a/solution.py
+++ b/solution.py
@@ -40,8 +40,9 @@
     pl.semaphore_wait(bar, len(partners))
 
 
-def fwd_kernel(hd, heads, tok, wp, normed, qkvT, oT, lse, own, vec, fb1, wT, bt,
-               T, Ws, k_s, o_s, st, rt, lt, sy, ry, sc, rc, scy, rcy, sa, ra, la, sz, rz, sx, rx, so, ro, lo):
+def fwd_kernel(hd, heads, tok, cot, wp, fa, fb, fc, normed, qkvT, oT, lse, own, vec, wT, a1, a2, a3, dob, mgrad, bout, sums, ga, gb, gc,
+               T, Ws, fb1, bt, up, r2, k1, r3, st, rt, lt, sy, ry, sc, rc, scy, rcy, sa, ra, la, sz, rz, sx, rx, so, ro, lo, ln,
+               su, ru, lu, gss, grs, gsz, grz, gs1, gr1, gs2, gr2, gsc, grc, sf1, rf1, sf2, rf2, sf3, rf3, la1, la2, la3):
     x, c, z, y = place()
     hg = c * 2 + y
     W = heads * hd
@@ -49,6 +50,7 @@
     R = T.shape[1]
     N = qkvT.shape[1]
     zoff = [lax.rem(z + k, 4) for k in (1, 2, 3)]
+    sums[...] = jnp.zeros_like(sums)
     greet([dev(x, c, zz, y) for zz in zoff] + [dev(x, 1 - c, zz, y) for zz in zoff]
           + [dev(x, 1 - c, z, y), dev(x, c, z, 1 - y), dev(x, 1 - c, z, 1 - y), dev(1 - x, c, z, y)])
     sib, yp, diag, xp = dev(x, 1 - c, z, y), dev(x, c, z, 1 - y), dev(x, 1 - c, z, 1 - y), dev(1 - x, c, z, y)
@@ -83,6 +85,96 @@
         wz.append(cp)
     wx = [rcopy(Ws.at[xz], Ws.at[xz], sx.at[3], rx.at[3], xp)]
     wx[0].start()
+    ca = 1 - c
+    gat = ((fa, ga, True), (fb, gb, False), (fc, gc, False))
+
+    def zz_of(u):
+        return z if u == 0 else (z - u if u <= 3 else z + (u - 3))
+
+    def ok(u):
+        return True if u == 0 else (z >= u if u <= 3 else z + (u - 3) <= 3)
+
+    def guard(cond, f):
+        if cond is True:
+            f()
+        else:
+            pl.when(cond)(f)
+
+    def g_start(p):
+        f, g, _ = gat[p]
+        return rcopy(f, g.at[x, c, z, y], gss.at[p], grs.at[p], sib)
+
+    def g_z(p, u, down):
+        g = gat[p][1]
+        v = g.at[x, ca, zz_of(u), y]
+        d = u if u <= 3 else u - 3
+        k = d + (3 if down else 0)
+        return rcopy(v, v, gsz.at[p, k], grz.at[p, k], dev(x, c, z - 1 if down else z + 1, y))
+
+    def g_zarr(p, u):
+        g = gat[p][1]
+        v = g.at[x, ca, zz_of(u), y]
+        return rcopy(v, v, gsz.at[p, u - 1], grz.at[p, u - 1], sib)
+
+    def g_one(p, u):
+        g, xfirst = gat[p][1:]
+        v = g.at[x, ca, zz_of(u), y]
+        return rcopy(v, v, gs1.at[p, u], gr1.at[p, u], xp if xfirst else yp)
+
+    def g_two(p, u):
+        g, xfirst = gat[p][1:]
+        v = g.at[:, ca, zz_of(u), y] if xfirst else g.at[x, ca, zz_of(u)]
+        return rcopy(v, v, gs2.at[p, u], gr2.at[p, u], yp if xfirst else xp)
+
+    def g_core(p, u):
+        v = gat[p][1].at[:, ca, zz_of(u)]
+        return rcopy(v, v, gsc.at[p, u], grc.at[p, u], sib)
+
+    def ag_own(p):
+        g_start(p).wait()
+        g_one(p, 0).start()
+
+    def ag_z0(p):
+        guard(z < 3, lambda: g_z(p, 0, False).start())
+        guard(z > 0, lambda: g_z(p, 0, True).start())
+
+    def ag_recv(p, d):
+        for u in (d, d + 3):
+            def go(u=u):
+                g_zarr(p, u).wait_recv()
+                if d < 3:
+                    guard((z > 0) if u > 3 else (z < 3), lambda: g_z(p, u, u > 3).start())
+                g_one(p, u).start()
+            guard(ok(u), go)
+
+    def units(d):
+        return (0,) if d == 0 else (d, d + 3)
+
+    def ag_two(p, d):
+        for u in units(d):
+            def go(u=u):
+                g_one(p, u).wait()
+                g_two(p, u).start()
+            guard(ok(u), go)
+
+    def ag_core(p, d):
+        for u in units(d):
+            def go(u=u):
+                g_two(p, u).wait()
+                g_core(p, u).start()
+            guard(ok(u), go)
+
+    def ag_end(p):
+        for u in range(7):
+            guard(ok(u), lambda: g_core(p, u).wait())
+        for u in (0, 1, 2):
+            guard((z >= u) & (z < 3), lambda: g_z(p, u, False).wait_send())
+            guard((z + u <= 3) & (z > 0), lambda: g_z(p, u + 3 if u else 0, True).wait_send())
+
+    for p in (2, 0, 1):
+        g_start(p).start()
+    for p in (2, 0, 1):
+        ag_own(p)
     ycp, ccp, cycp = [], [], []
     for j in range(2):
         src_z = 2 * c + j
@@ -106,12 +198,17 @@
         cp = rcopy(Ws.at[x * 4 + zs], Ws.at[x * 4 + zs], sx.at[k], rx.at[k], xp)
         cp.start()
         wx.append(cp)
+    ag_z0(2)
+    ag_z0(0)
+    for p in (2, 0, 1):
+        ag_two(p, 0)
     for j in range(2):
         ycp[j].wait()
         p = (c * 2 + 1 - y) * 2 + j
         cp = rcopy(T.at[p], T.at[p], scy.at[j], rcy.at[j], sib)
         cp.start()
         cycp.append(cp)
+    ag_z0(1)
     for cp in wx:
         cp.wait()
     for xx in range(2):
@@ -142,64 +239,107 @@
         cen = v - jnp.mean(v, axis=-1, keepdims=True)
         r = lax.rsqrt(jnp.mean(cen * cen, axis=-1, keepdims=True) + EPS)
         nb = (cen * r * gain + bias).astype(bf16)
-        normed[p] = nb
+        T[p] = nb
         pr = dot_nt(wT[...], nb)
         cols = pl.ds(p * R, R)
         qkvT[0:W, cols] = (pr[0:W] + qb[:, 4:5]).astype(bf16)
         qkvT[W:2 * W, cols] = pr[W:2 * W].astype(bf16)
         qkvT[2 * W:3 * W, cols] = (pr[2 * W:] + qb[:, 5:6]).astype(bf16)
         return carry
+    own[...] = T[pl.ds(hg * 2, 2)]
     lax.fori_loop(0, T.shape[0], blk, 0)
-    own[...] = T[pl.ds(hg * 2, 2)]
-    for h in range(heads):
-        k_s[h] = qkvT[W + h * hd:W + (h + 1) * hd, :].T
-    QB, KB = 2 * R, 512
-    cs = LOG2E * hd ** -0.5
-    nk = N // KB
-    def group(k, carry):
-        cc = jnp.where((k == 1) | (k == 2), 1 - c, c)
-        yy = jnp.where(k < 2, 1 - y, y)
-        g = cc * 2 + yy
-        qcols = pl.ds(g * QB, QB)
-        def head(h, carry):
-            qt = qkvT[pl.ds(h * hd, hd), qcols]
-            def scores(i):
-                return dot_nn(k_s[h, i * KB:(i + 1) * KB, :], qt)
-            m = None
-            s = scores(0)
-            for i in range(nk):
-                nxt = scores(i + 1) if i + 1 < nk else None
-                cm = jnp.max(s, axis=0, keepdims=True)
-                mn = cm if m is None else jnp.maximum(m, cm)
-                p = jnp.exp2(s * cs - mn * cs)
-                ps = jnp.sum(p, axis=0, keepdims=True)
-                vt = qkvT[pl.ds(2 * W + h * hd, hd), i * KB:(i + 1) * KB]
-                ov = dot_nn(vt, p.astype(bf16))
-                if m is None:
-                    l, o = ps, ov
-                else:
-                    a = jnp.exp2((m - mn) * cs)
-                    l = l * a + ps
-                    o = o * a + ov
-                m = mn
-                s = nxt
-            o = o / l
-            o_s[g, pl.ds(h * hd, hd), :] = o.astype(bf16)
-            oT[pl.ds(h * hd, hd), qcols] = o
-            lse[pl.ds(h, 1), qcols] = m * cs + jnp.log2(l)
+    keep = pltpu.make_async_copy(T, normed, ln)
+    keep.start()
+    keep.wait()
+    def cot_copy(i):
+        zt = 2 * c + i
+        return zt, rcopy(cot.at[i], up.at[lax.rem(z, 2)], su.at[i], ru.at[lax.rem(z, 2)], dev(x, lax.div(z, 2), zt, y))
+    def cot_start():
+        for i in range(2):
+            zt, cp = cot_copy(i)
+            @pl.when(zt != z)
+            def _():
+                cp.start()
+            @pl.when(zt == z)
+            def _():
+                pltpu.make_async_copy(cot.at[i], up.at[lax.rem(z, 2)], lu).start()
+    def cot_wait():
+        for j in range(2):
+            @pl.when(2 * c + j != z)
+            def _():
+                rcopy(cot.at[0], up.at[j], su.at[0], ru.at[j], sib).wait_recv()
+            @pl.when(2 * c + j == z)
+            def _():
+                pltpu.make_async_copy(cot.at[0], up.at[j], lu).wait()
+            zt, cp = cot_copy(j)
+            @pl.when(zt != z)
+            def _():
+                cp.wait_send()
+    def attention(k_s, o_s):
+        for h in range(heads):
+            k_s[h] = qkvT[W + h * hd:W + (h + 1) * hd, :].T
+        QB, KB = 2 * R, 512
+        cs = LOG2E * hd ** -0.5
+        nk = N // KB
+        PLAN = {0: [(ag_recv, 2, 1), (ag_recv, 0, 1), (ag_core, 2, 0), (ag_core, 0, 0)], 1: [(ag_recv, 1, 1), (ag_core, 1, 0)],
+                2: [(ag_two, 2, 1), (ag_two, 0, 1)], 3: [(ag_recv, 2, 2), (ag_recv, 0, 2)], 4: [(ag_recv, 1, 2)], 5: [(ag_two, 1, 1)],
+                6: [(ag_two, 2, 2), (ag_two, 0, 2), (ag_core, 2, 1), (ag_core, 0, 1)], 7: [(ag_recv, 2, 3), (ag_recv, 0, 3)],
+                8: [(ag_recv, 1, 3)], 9: [(ag_two, 1, 2), (ag_core, 1, 1)], 10: [(ag_two, 2, 3), (ag_two, 0, 3), (ag_core, 2, 2), (ag_core, 0, 2)],
+                12: [(ag_two, 1, 3), (ag_core, 1, 2)], 14: [(ag_core, 2, 3), (ag_core, 0, 3)]}
+        def group(k, carry):
+            cc = jnp.where((k == 1) | (k == 2), 1 - c, c)
+            yy = jnp.where(k < 2, 1 - y, y)
+            g = cc * 2 + yy
+            qcols = pl.ds(g * QB, QB)
+            def head(h, carry):
+                step = k * heads + h
+                for when, work in PLAN.items():
+                    @pl.when(step == when)
+                    def _():
+                        for f, p, d in work:
+                            f(p, d)
+                @pl.when(step == 9)
+                def _():
+                    cot_start()
+                qt = qkvT[pl.ds(h * hd, hd), qcols]
+                def scores(i):
+                    return dot_nn(k_s[h, i * KB:(i + 1) * KB, :], qt)
+                m = None
+                s = scores(0)
+                for i in range(nk):
+                    nxt = scores(i + 1) if i + 1 < nk else None
+                    cm = jnp.max(s, axis=0, keepdims=True)
+                    mn = cm if m is None else jnp.maximum(m, cm)
+                    p = jnp.exp2(s * cs - mn * cs)
+                    ps = jnp.sum(p, axis=0, keepdims=True)
+                    vt = qkvT[pl.ds(2 * W + h * hd, hd), i * KB:(i + 1) * KB]
+                    ov = dot_nn(vt, p.astype(bf16))
+                    if m is None:
+                        l, o = ps, ov
+                    else:
+                        a = jnp.exp2((m - mn) * cs)
+                        l = l * a + ps
+                        o = o * a + ov
+                    m = mn
+                    s = nxt
+                o = o / l
+                o_s[g, pl.ds(h * hd, hd), :] = o.astype(bf16)
+                oT[pl.ds(h * hd, hd), qcols] = o
+                lse[pl.ds(h, 1), qcols] = m * cs + jnp.log2(l)
+                return carry
+            lax.fori_loop(0, heads, head, 0)
+            @pl.when(k < 3)
+            def _():
+                rcopy(o_s.at[g], bt.at[hg], so.at[k], ro.at[k], dev(x, cc, z, yy)).start()
+            @pl.when(k == 3)
+            def _():
+                pltpu.make_async_copy(o_s.at[g], bt.at[hg], lo).start()
             return carry
-        lax.fori_loop(0, heads, head, 0)
-        @pl.when(k < 3)
-        def _():
-            rcopy(o_s.at[g], bt.at[hg], so.at[k], ro.at[k], dev(x, cc, z, yy)).start()
-        @pl.when(k == 3)
-        def _():
-            pltpu.make_async_copy(o_s.at[g], bt.at[hg], lo).start()
-        return carry
-    lax.fori_loop(0, 4, group, 0)
-    for k, d in enumerate((yp, diag, sib)):
-        rcopy(o_s.at[0], bt.at[hg], so.at[k], ro.at[k], d).wait()
-    pltpu.make_async_copy(o_s.at[0], bt.at[hg], lo).wait()
+        lax.fori_loop(0, 4, group, 0)
+        for k, d in enumerate((yp, diag, sib)):
+            rcopy(o_s.at[0], bt.at[hg], so.at[k], ro.at[k], d).wait()
+        pltpu.make_async_copy(o_s.at[0], bt.at[hg], lo).wait()
+    pl.run_scoped(attention, pltpu.VMEM((heads, N, hd), bf16), pltpu.VMEM((4, W, 2 * R), bf16))
     for i in range(2):
         zt, cp, loc = tcp[i]
         @pl.when(zt != z)
@@ -207,39 +347,186 @@
             cp.wait_send()
 
 
-def forward_kernel(tok, wp, heads, hd, FF):
+    FF = fb1.shape[1]
+    C = 2 * R
+
+    def middle_part(Wo, mid_s, n2, n2T, oacc, dacc, f1b, f2b, sb1, sb2, sb3, lw, l1, l2):
+        ag_core(1, 3)
+        ag_end(2)
+        cpw = pltpu.make_async_copy(gc, Wo, lw)
+        cpw.start()
+        bT = bt[...].reshape(4 * W, C).T
+        cpw.wait()
+        w_o = Wo[...].reshape(D, D)
+        def norm(v):
+            cen = v - jnp.mean(v, axis=-1, keepdims=True)
+            return cen, lax.rsqrt(jnp.mean(cen * cen, axis=-1, keepdims=True) + EPS)
+        for j in range(2):
+            v = own[j].astype(f32) + vec[15:16, :] + dot_nn(bT[j * R:(j + 1) * R], w_o) + vec[6:7, :]
+            mid_s[j] = v
+            cen, r = norm(v)
+            nb = (cen * r * vec[7:8, :] + vec[8:9, :]).astype(bf16)
+            n2[j] = nb
+            n2T[:, :, j * R:(j + 1) * R] = nb.T.reshape(4, D // 4, R)
+        ag_end(0)
+        ag_end(1)
+        cot_wait()
+
+        def order(s):
+            cc = jnp.where(s < 4, 1 - c, c)
+            xx = jnp.where(lax.rem(lax.div(s, 2), 2) == 0, x, 1 - x)
+            zp = lax.rem(s, 2)
+            return xx, cc, zp, (xx * 2 + cc) * 2 + zp
+        def loads(s):
+            xx, cc, zp, j = order(s)
+            slot = lax.rem(s, 2)
+            return (pltpu.make_async_copy(ga.at[:, :, :, :, :, pl.ds(pl.multiple_of(j * C, C), C)], f1b.at[slot], l1.at[slot]),
+                    pltpu.make_async_copy(gb.at[xx, cc, pl.ds(zp * 2, 2)], f2b.at[slot], l2.at[slot]))
+        for cp in loads(0):
+            cp.start()
+        oacc[...] = jnp.zeros_like(oacc)
+        dacc[...] = jnp.zeros_like(dacc)
+        def sends(s):
+            slot = lax.rem(s, 2)
+            return (rcopy(sb1.at[slot], T.at[lax.rem(s + 4, 8)], sf1.at[s], rf1.at[lax.rem(s + 4, 8)], sib),
+                    rcopy(sb2.at[slot], r2.at[lax.rem(s, 4)], sf2.at[lax.rem(s, 4)], rf2.at[lax.rem(s, 4)], sib))
+        def out1(s):
+            j = order(s)[3]
+            return [pltpu.make_async_copy(T.at[s, :, pl.ds(q * C, C)], a1.at[q, :, pl.ds(pl.multiple_of(j * C, C), C)], la1.at[s, q]) for q in range(2)]
+        def out2(s):
+            xx, cc, zp, j = order(s)
+            return pltpu.make_async_copy(r2.at[s - 4], a2.at[xx, zp], la2.at[s - 4])
+        def chunk(s, carry):
+            slot = lax.rem(s, 2)
+            xx, cc, zp, j = order(s)
+            for cp in loads(s):
+                cp.wait()
+            @pl.when(s < 7)
+            def _():
+                for cp in loads(s + 1):
+                    cp.start()
+            @pl.when(s >= 2)
+            def _():
+                sends(s - 2)[0].wait_send()
+            @pl.when((s >= 2) & (s < 6))
+            def _():
+                sends(s - 2)[1].wait_send()
+            f1c = f1b[slot].reshape(D, C)
+            f2c = f2b[slot].reshape(C, D)
+            u2 = up[...].reshape(C, D)
+            h = dot_nn(n2[...].reshape(C, D), f1c) + fb1[2:3, pl.ds(pl.multiple_of(j * C, C), C)]
+            da = dot_nt(u2, f2c)
+            ph = 0.5 + 0.5 * lax.erf(h * 0.7071067811865476)
+            act = (h * ph).astype(bf16)
+            hgr = (da * (ph + h * (jnp.exp(-0.5 * h * h) * 0.3989422804014327))).astype(bf16)
+            oacc[...] += dot_nn(act, f2c).reshape(2, R, D)
+            sums[pl.ds(4 + lax.div(j, 2), 1), pl.ds(pl.multiple_of(lax.rem(j, 2) * C, C), C)] = jnp.sum(hgr.astype(f32), axis=0, keepdims=True)
+            g2 = dot_nn(act.T, u2)
+            dacc[...] += dot_nt(hgr, f1c).reshape(2, R, D)
+            for q in range(2):
+                sb1[slot, :, q * C:(q + 1) * C] = dot_nn(n2T[q * 2 + 1 - c], hgr).astype(bf16)
+            @pl.when(s < 4)
+            def _():
+                sb2[slot] = g2.astype(bf16)
+                sends(s)[1].start()
+                for q in range(2):
+                    k1[s, :, q * C:(q + 1) * C] = dot_nn(n2T[q * 2 + c], hgr).astype(bf16)
+            sends(s)[0].start()
+            @pl.when(s >= 4)
+            def _():
+                sends(s)[1].wait_recv()
+                r2[s - 4] = (r2[s - 4].astype(f32) + g2).astype(bf16)
+                out2(s).start()
+                rcopy(sb1.at[0], T.at[s], sf1.at[0], rf1.at[s], sib).wait_recv()
+                for q in range(2):
+                    cols = slice(q * C, (q + 1) * C)
+                    T[s, :, cols] = (T[s, :, cols].astype(f32) + dot_nn(n2T[q * 2 + c], hgr)).astype(bf16)
+                for cp in out1(s):
+                    cp.start()
+            return carry
+        lax.fori_loop(0, 8, chunk, 0)
+
+        tot = [jnp.zeros((1, D), f32) for _ in range(4)]
+        ags = []
+        for j in range(2):
+            v = mid_s[j]
+            bout[j] = (v + oacc[j] + vec[9:10, :]).astype(bf16)
+            cen, r = norm(v)
+            xh = cen * r
+            u = dacc[j]
+            e = u * vec[7:8, :]
+            g = up[j].astype(f32) + r * (e - jnp.mean(e, axis=-1, keepdims=True) - xh * jnp.mean(e * xh, axis=-1, keepdims=True))
+            mgrad[j] = g
+            ag = g.astype(bf16)
+            ags.append(ag)
+            for n, val in enumerate((ag.astype(f32), u * xh, u, up[j].astype(f32))):
+                tot[n] = tot[n] + jnp.sum(val, axis=0, keepdims=True)
+        for n in range(4):
+            sums[n:n + 1, :] = tot[n]
+        ag = jnp.concatenate(ags, axis=0)
+        for q in range(2):
+            sb3[q] = dot_nn(bt[q * 2 + 1 - c], ag).astype(bf16)
+            rcopy(sb3.at[q], r3.at[q], sf3.at[q], rf3.at[q], sib).start()
+        for q in range(4):
+            dob[q] = dot_nt(Wo[q // 2, q % 2].reshape(D // 4, D), ag).astype(bf16)
+        for s in range(4):
+            rcopy(sb1.at[0], T.at[s], sf1.at[0], rf1.at[s], sib).wait_recv()
+            T[s] = (T[s].astype(f32) + k1[s].astype(f32)).astype(bf16)
+            for cp in out1(s):
+                cp.start()
+        for q in range(2):
+            rcopy(sb3.at[q], r3.at[q], sf3.at[q], rf3.at[q], sib).wait()
+            r3[q] = (r3[q].astype(f32) + dot_nn(bt[q * 2 + c], ag)).astype(bf16)
+        cp3 = pltpu.make_async_copy(r3, a3, la3)
+        cp3.start()
+        for s in (6, 7):
+            sends(s)[0].wait_send()
+        for s in range(8):
+            for cp in out1(s):
+                cp.wait()
+        for s in range(4, 8):
+            out2(s).wait()
+        cp3.wait()
+
+    SD = pltpu.SemaphoreType.DMA
+    V = pltpu.VMEM
+    pl.run_scoped(middle_part, V(gc.shape, bf16), V((2, R, D), f32), V((2, R, D), bf16), V((4, D // 4, C), bf16), V((2, R, D), f32),
+                  V((2, R, D), f32), V((2,) + ga.shape[:5] + (C,), bf16), V((2, 2) + gb.shape[3:], bf16),
+                  V((2, D // 4, 2 * C), bf16), V((2, C, D), bf16), V((2, D // 4, D), bf16), SD, SD((2,)), SD((2,)))
+
+
+def forward_kernel(tok, cot, wp, fa, fb, fc, heads, hd):
     n_it, R, D = tok.shape
+    FF = fa.shape[1]
     W = heads * hd
     N = 8 * R
+    C = 2 * R
     S = pltpu.SemaphoreType.DMA
+    V = pltpu.VMEM
     vm = pl.BlockSpec(memory_space=pltpu.VMEM)
     hbm = pl.BlockSpec(memory_space=pl.ANY)
+    sd = jax.ShapeDtypeStruct
+    full = lambda a: sd((2, 2, 4, 2) + a.shape, bf16)
     return pl.pallas_call(
         functools.partial(fwd_kernel, hd, heads),
-        in_specs=[hbm, hbm],
-        out_specs=[vm, vm, vm, vm, vm, vm, vm, vm, hbm],
+        in_specs=[hbm] * 6,
+        out_specs=[hbm] + [vm] * 6 + [hbm] * 3 + [vm] * 4 + [hbm] * 3,
         out_shape=[
-            jax.ShapeDtypeStruct((8, R, D), bf16),
-            jax.ShapeDtypeStruct((3 * W, N), bf16),
-            jax.ShapeDtypeStruct((W, N), f32),
-            jax.ShapeDtypeStruct((heads, N), f32),
-            jax.ShapeDtypeStruct((2, R, D), bf16),
-            jax.ShapeDtypeStruct((16, D), f32),
-            jax.ShapeDtypeStruct((8, FF), f32),
-            jax.ShapeDtypeStruct((3 * W, D), bf16),
-            jax.ShapeDtypeStruct((4, W, 2 * R), bf16),
+            sd((8, R, D), bf16), sd((3 * W, N), bf16), sd((W, N), f32), sd((heads, N), f32), sd((2, R, D), bf16), sd((16, D), f32),
+            sd((3 * W, D), bf16), sd((2, D // 4, FF), bf16), sd((2, 2, C, D), bf16), sd((2, D // 4, D), bf16), sd((4, W, C), bf16),
+            sd((2, R, D), f32), sd((2, R, D), bf16), sd((16, D), f32), full(fa), full(fb), full(fc),
         ],
         scratch_shapes=[
-            pltpu.VMEM((8, R, D), bf16),
-            pltpu.VMEM((8, 4, 32, 3 * W + 128), bf16),
-            pltpu.VMEM((heads, N, hd), bf16),
-            pltpu.VMEM((4, W, 2 * R), bf16),
+            V((8, R, D), bf16), V((8, 4, 32, 3 * W + 128), bf16), V((8, FF), f32), V((4, W, C), bf16), V((2, R, D), bf16),
+            V((4, C, D), bf16), V((4, D // 4, D), bf16), V((2, D // 4, D), bf16),
             S((2,)), S((2,)), S, S((2,)), S((2,)), S((2,)), S((2,)), S((2,)), S((2,)),
-            S((3,)), S((3,)), S, S((3,)), S((3,)), S((4,)), S((4,)), S((3,)), S((3,)), S,
+            S((3,)), S((3,)), S, S((3,)), S((3,)), S((4,)), S((4,)), S((3,)), S((3,)), S, S,
+            S((2,)), S((2,)), S, S((3,)), S((3,)), S((3, 6)), S((3, 6)), S((3, 7)), S((3, 7)), S((3, 7)), S((3, 7)), S((3, 7)), S((3, 7)),
+            S((8,)), S((8,)), S((4,)), S((4,)), S((2,)), S((2,)), S((8, 2)), S((4,)), S,
         ],
-        compiler_params=pltpu.CompilerParams(collective_id=0, has_side_effects=True, vmem_limit_bytes=56 << 20),
+        compiler_params=pltpu.CompilerParams(collective_id=0, has_side_effects=True, vmem_limit_bytes=60 << 20),
         name="forward",
-    )(tok, wp)
+    )(tok, cot, wp, fa, fb, fc)
 
 
 def put_sum(dst, pieces):
@@ -249,11 +536,11 @@
     dst[...] = total.astype(dst.dtype)
 
 
-def tail_kernel(hd, heads, dob, qkvT, oT, lse, a1, a2, a3, normed, wT, own, rows, mgrad, sums0,
-                o1, o2, o3, gq, home, sums,
+def tail_kernel(hd, heads, dob, qkvT, oT, lse, a1, a2, a3, normed, wT, own, rows, mgrad, sums0, bout,
+                o1, o2, o3, gq, home, sums, bo,
                 do_s, dq_s, k1, r11, r12, r13, k2, r21, r22, r23, k3, r31, r32, r33,
                 Gb, gx, gz, go, ds_s, dr_c, dy_s, dr_y, ig, hm, vs, vr,
-                sd, rd, ld, s1, q1, s2, q2, s3, q3, lk, sg, qg, sgz, qgz, sga, qga, sdc, qdc, sdy, qdy, sh, qh, lh, sv, qv, ll):
+                sd, rd, ld, s1, q1, s2, q2, s3, q3, lk, sg, qg, sgz, qgz, sga, qga, sdc, qdc, sdy, qdy, sh, qh, lh, sv, qv, ll, sb, qb, lb):
     x, c, z, y = place()
     hg = c * 2 + y
     W = heads * hd
@@ -326,6 +613,32 @@
     f3 = Piece(4, 0, None, a3, k3, r31, r32, r33, o3, s3, q3, lk, False)
     f2[0].start()
     f1[0].start()
+
+    def out_copy(j):
+        zt = 2 * c + j
+        return zt, rcopy(bout.at[j], bo.at[lax.rem(z, 2)], sb.at[j], qb.at[lax.rem(z, 2)], dev(x, lax.div(z, 2), zt, y))
+    def out_start():
+        for j in range(2):
+            zt, cp = out_copy(j)
+            @pl.when(zt != z)
+            def _():
+                cp.start()
+            @pl.when(zt == z)
+            def _():
+                pltpu.make_async_copy(bout.at[j], bo.at[lax.rem(z, 2)], lb).start()
+    def out_wait():
+        for i in range(2):
+            @pl.when(2 * c + i != z)
+            def _():
+                rcopy(bout.at[0], bo.at[i], sb.at[0], qb.at[i], sib).wait_recv()
+            @pl.when(2 * c + i == z)
+            def _():
+                pltpu.make_async_copy(bout.at[0], bo.at[i], lb).wait()
+            zt, cp = out_copy(i)
+            @pl.when(zt != z)
+            def _():
+                cp.wait_send()
+    out_start()
 
     QB, KB = N // 4, 512
     cs = LOG2E * hd ** -0.5
@@ -525,6 +838,7 @@
             def _():
                 pltpu.make_async_copy(ig.at[0], hm.at[i], lh).wait()
             home[i] = hm[i].astype(f32)
+        out_wait()
         for zt, cp, lc in homes:
             @pl.when(zt != z)
             def _():
@@ -536,7 +850,7 @@
                   pltpu.VMEM((2, R, D), f32), pltpu.VMEM((2, R, D), f32), pltpu.SemaphoreType.DMA((4,)))
 
 
-def backward_kernel(dob, qkvT, oT, lse, a1, a2, a3, normed, wT, own, rows, mgrad, sums0, heads, hd):
+def backward_kernel(dob, qkvT, oT, lse, a1, a2, a3, normed, wT, own, rows, mgrad, sums0, bout, heads, hd):
     W3, N = qkvT.shape
     W = heads * hd
     _, R, D = own.shape
@@ -551,11 +865,12 @@
     rq = D // 32
     return pl.pallas_call(
         functools.partial(tail_kernel, hd, heads),
-        in_specs=[hbm, vm, vm, vm, hbm, hbm, hbm, hbm, hbm, hbm, vm, hbm, vm],
-        out_specs=[vm] * 6,
+        in_specs=[hbm, vm, vm, vm, hbm, hbm, hbm, hbm, hbm, hbm, vm, hbm, vm, hbm],
+        out_specs=[vm] * 6 + [hbm],
         out_shape=[
             jax.ShapeDtypeStruct(b1, f32), jax.ShapeDtypeStruct(b2, f32), jax.ShapeDtypeStruct(b3, f32),
             jax.ShapeDtypeStruct((rq, 3 * D), f32), jax.ShapeDtypeStruct((2, R, D), f32), jax.ShapeDtypeStruct((16, D), f32),
+            jax.ShapeDtypeStruct((2, R, D), bf16),
         ],
         scratch_shapes=[V((4, W, N // 4), bf16), V((W3, N), bf16)] + bufs(b1, True) + bufs(b2, False) + bufs(b3, False) + [
             V((2, 2, 4, 2, rq, W3), bf16), V((2, 4, 2, rq, W3), bf16), V((3, 2, 2, rq, W3), bf16), V((4, rq, W3), bf16),
@@ -563,10 +878,11 @@
             V((16, D), f32), V((6, 16, D), f32),
             S((3,)), S((3,)), S, S((10,)), S((10,)), S((10,)), S((10,)), S((5,)), S((5,)), S((5,)),
             S, S, S((3,)), S((3,)), S((3,)), S((3,)), S((4,)), S((4,)), S((2,)), S((2,)), S((2,)), S((2,)), S, S((6,)), S((6,)), S,
+            S((2,)), S((2,)), S,
         ],
         compiler_params=pltpu.CompilerParams(collective_id=1, has_side_effects=True, vmem_limit_bytes=60 << 20),
         name="backward",
-    )(dob, qkvT, oT, lse, a1, a2, a3, normed, wT, own, rows, mgrad, sums0)
+    )(dob, qkvT, oT, lse, a1, a2, a3, normed, wT, own, rows, mgrad, sums0, bout)
 
 
 HEADS = 16
@@ -826,67 +1142,9 @@
     return (block_output, input_grad) + tuple(summed)
 
 
-def moves(mesh_shape, back):
-    seq_n = mesh_shape["seq"]
-    out = []
-    for p in range(2):
-        pairs = []
-        for dp in range(mesh_shape["dp"]):
-            for seq in range(seq_n):
-                x, c, z, y = dp // 2, dp % 2, seq // 2, seq % 2
-                i = p ^ (z % 2)
-                t = (x * 2 + z // 2) * seq_n + (2 * c + i) * 2 + y
-                s = dp * seq_n + seq
-                pairs.append((t, s) if back else (s, t))
-        out.append(pairs)
-    return out
-
-
-def pick(bit, first, second):
-    return jnp.where(bit == 0, first, second)
-
-
-def carry_out(mesh_shape, values):
-    x, c, z, y = place()
-    b = lax.rem(z, 2)
-    got = [lax.ppermute(pick(b, values[p], values[1 - p]), ("dp", "seq"), m) for p, m in enumerate(moves(mesh_shape, False))]
-    return jnp.stack([pick(b, got[0], got[1]), pick(b, got[1], got[0])])
-
-
-def carry_home(mesh_shape, values):
-    x, c, z, y = place()
-    b = lax.rem(z, 2)
-    got = [lax.ppermute(pick(b, values[p], values[1 - p]), ("dp", "seq"), m) for p, m in enumerate(moves(mesh_shape, True))]
-    return jnp.stack([pick(b, got[0], got[1]), pick(b, got[1], got[0])])
-
-
-def partner(mesh_shape, kind):
-    seq_n = mesh_shape["seq"]
-    n = seq_n * mesh_shape["dp"]
-    if kind == "core":
-        return [(s, s ^ seq_n) for s in range(n)]
-    return [(s, s ^ 1) for s in range(n)]
-
-
-def norm_rows(values, gain, shift):
-    center = values - jnp.mean(values, axis=-1, keepdims=True)
-    spread = jnp.mean(center * center, axis=-1, keepdims=True)
-    return center * lax.rsqrt(spread + EPS) * gain + shift
-
-
-def gelu_exact(values):
-    return jax.nn.gelu(values, approximate=False)
-
-
-def mm(a, b, ca, cb):
-    return lax.dot_general(a, b, (((ca,), (cb,)), ((), ())), preferred_element_type=f32)
-
-
 def on_device(mesh_shape, tokens_in, lead_hours, cotangent, w_qkv, w_out, w_fc1, w_fc2, ln1_gain, ln1_bias, q_bias, v_bias,
               out_bias, ln2_gain, ln2_bias, fc1_bias, fc2_bias, lead_weight, lead_bias):
-    AX = ("dp", "seq")
     x, c, z, y = place()
-    hg = c * 2 + y
     _, R, D = tokens_in.shape
     FF = w_fc1.shape[1]
     hd = D // HEADS
@@ -899,46 +1157,11 @@
     small = small.at[10].set(fc1_bias).at[11, :2].set(lead_hours.astype(bf16))
     slices = w_qkv.reshape(rows, 3, 4, W).transpose(2, 0, 1, 3).reshape(4, rows, 3 * W)
     wp = jnp.concatenate([slices, jnp.broadcast_to(small, (4, 32, 128))], axis=2)
-    normed, qkvT, oT, lse, own, vec, fb1, wfull, bt = forward_kernel(tokens_in, wp, heads, hd, FF)
-    full_out = lax.all_gather(w_out, AX, axis=0, tiled=True)
-    full_fc1 = lax.all_gather(w_fc1, AX, axis=0, tiled=True)
-    full_fc2 = lax.all_gather(w_fc2, AX, axis=0, tiled=True)
-    upstream_low = carry_out(mesh_shape, cotangent).reshape(2 * R, D)
-    bias_fc1 = fb1[2:3]
-    leading = own.reshape(2 * R, D).astype(f32) + vec[15:16]
-    blendedT = bt.reshape(D, 2 * R)
-    middle = leading + mm(blendedT, full_out, 0, 0) + vec[6:7]
-    normed2, norm2_back = jax.vjp(norm_rows, middle, vec[7:8], vec[8:9])
-    normed2 = normed2.astype(bf16)
-    hidden = mm(normed2, full_fc1, 1, 0) + bias_fc1
-    activated, gelu_back = jax.vjp(gelu_exact, hidden)
-    activated = activated.astype(bf16)
-    output = middle + mm(activated, full_fc2, 1, 0) + vec[9:10]
-    block_output = carry_home(mesh_shape, output.astype(bf16).reshape(2, R, D))
-    upstream = upstream_low.astype(f32)
-    core = partner(mesh_shape, "core")
-    def chip_sum(left, right, rows):
-        cut = left.reshape(2 * R, 2, 2, -1)
-        def half(which):
-            return mm(lax.dynamic_index_in_dim(cut, which, 2, keepdims=False).reshape(2 * R, -1), right, 0, 0)
-        there = lax.ppermute(half(1 - c).astype(bf16), AX, core)
-        both = (half(c) + there.astype(f32)).astype(bf16)
-        return both.reshape(2, 4, 2, rows, -1)
-    a2 = chip_sum(activated, upstream_low, w_fc2.shape[0])
-    grad_fc2_bias = jnp.sum(upstream, axis=0)
-    hidden_grad = gelu_back(mm(upstream_low, full_fc2, 1, 1))[0].astype(bf16)
-    a1 = chip_sum(normed2, hidden_grad, rows)
-    grad_fc1_bias = jnp.sum(hidden_grad.astype(f32), axis=0)
-    middle_part, g_ln2_gain, g_ln2_bias = norm2_back(mm(hidden_grad, full_fc1, 1, 1))
-    middle_grad = upstream + middle_part
-    attn_grad = middle_grad.astype(bf16)
-    dob = mm(full_out, attn_grad, 1, 1).astype(bf16).reshape(4, W, 2 * R)
-    a3 = chip_sum(blendedT.T, attn_grad, rows)
-    grad_out_bias = jnp.sum(attn_grad.astype(f32), axis=0)
-    sums0 = jnp.concatenate([grad_out_bias[None], g_ln2_gain.reshape(1, D), g_ln2_bias.reshape(1, D), grad_fc2_bias[None],
-                             grad_fc1_bias.reshape(-1, D), jnp.zeros((12 - FF // D, D), f32)])
-    grad_fc1, grad_fc2, grad_out, grad_qkv, home, sums = backward_kernel(
-        dob, qkvT, oT, lse, a1, a2, a3, normed, wfull, own, vec, middle_grad.reshape(2, R, D), sums0, heads, hd)
+    normed, qkvT, oT, lse, own, vec, wT, a1, a2, a3, dob, mgrad, bout, sums0 = forward_kernel(
+        tokens_in, cotangent, wp, w_fc1, w_fc2, w_out, heads, hd)[:14]
+    grad_fc1, grad_fc2, grad_out, grad_qkv, home, sums, block_output = backward_kernel(
+        dob, qkvT, oT, lse, a1.reshape(2, 4, 2, rows, FF), a2.reshape(2, 4, 2, -1, D), a3.reshape(2, 4, 2, rows, D), normed, wT,
+        own, vec, mgrad, sums0, bout, heads, hd)
     index = (x * 2 + c) * 8 + z * 2 + y
     mine = lax.dynamic_slice(sums, (0, index * rows), (16, rows))
     g_fc1_bias = lax.dynamic_slice(sums[4:4 + FF // D].reshape(FF), (index * fc1_bias.shape[0],), (fc1_bias.shape[0],))
@@ -949,7 +1172,7 @@
 def choose(mesh_shape, *args):
     items, rows = args[0].shape[0], args[3].shape[0]
     planes = mesh_shape["seq"] // 2
-    if items == 2 and planes == 2 * items and mesh_shape["dp"] == 4 and rows % 16 == 0:
+    if items == 2 and planes == 2 * items and mesh_shape["dp"] == 4 and rows % 16 == 0 and 4 * args[0].shape[1] == args[0].shape[2]:
         return on_device(mesh_shape, *args)
     return spread_on_device(*args)
 

time: 590 us -> 399 us (0.68)
  matrix products: 88.4 us -> 0 us
  Pallas kernels: 299 us -> 376 us
  waiting for transfers between devices: 69.3 us -> 0 us
  local copies, waits for them, and re-layouts: 81.1 us -> 19.7 us
  other arithmetic: 21.3 us -> 1.37 us
  between operations: 14.4 us -> 0.81 us
  starting transfers between devices: 11.5 us -> 0 us
    dot_general x12 -> x0, matrix products: 88.4 us -> none  [mm(): lax.dot_general(a, b, (((ca,), (cb,)), ((), ())), preferred_element_type=...]
    pallas_call x1, Pallas kernels: 117 us -> 188 us  [forward_kernel(): pl.pallas_call(functools.partial(fwd_kernel, hd, heads), in_specs=[hbm] *...]
    all_gather x3 -> x0, waiting for transfers between devices: 67.3 us -> none  [the longest x1 67.2 us: on_device(): full_fc2 = lax.all_gather(w_fc2, AX, axis=0, tiled=True)]
    unnamed x45 -> x18, local copies, waits for them, and re-layouts: 39.1 us -> 7.56 us
    dynamic_slice x3 -> x0, local copies, waits for them, and re-layouts: 15.6 us -> none  [half(): lax.dynamic_index_in_dim(cut, which, 2, keepdims=False).reshape(2 * R, -1)]
    ppermute x7 -> x0, starting transfers between devices: 11.4 us -> none  [the longest x2 6.88 us: carry_home(): lax.ppermute(pick(b, values[p], values[1 - p]), ('dp', 'seq'), m)]
    convert_element_type x2 -> x0, other arithmetic: 11.1 us -> none  [the longest x1 9.72 us: on_device(): activated = activated.astype(bf16)]
    reshape x3 -> x0, local copies, waits for them, and re-layouts: 9.68 us -> none  [the longest x2 9.67 us: chip_sum(): cut = left.reshape(2 * R, 2, 2, -1)]
  transfers between devices with their start and end apart: 10 -> 0, of which waited for: 1 -> 0; matrix products, arithmetic and copies ran while one was open for 14% -> 0% of each run, Pallas kernels for 20% -> 0%
where the time goes in v2:
time: 399 us; the launch traced here: 398 us
  Pallas kernels  376 us (94%)
  local copies, waits for them, and re-layouts  19.7 us (5%)
    pallas_call x1, Pallas kernels, backward_kernel(): pl.pallas_call(functools.partial(tail_kernel, hd, heads), in_specs=[hbm,...  188 us
    pallas_call x1, Pallas kernels, forward_kernel(): pl.pallas_call(functools.partial(fwd_kernel, hd, heads), in_specs=[hbm] *...  188 us

profile of v2, /device:TPU:0, one launch (start us, length us, event | category | flops | bytes accessed | tf_op | source)
XLA Modules:
  0.0 398.1 jit_solution(8561985772964973325)
XLA Ops:
  0.7 1.1 reshape.397
  1.7 0.1 copy.40
  1.8 0.2 reshape.398
  2.1 0.7 scatter.40
  2.7 0.8 scatter.41
  3.5 0.8 scatter.44
  4.3 0.8 scatter.45
  5.1 0.8 scatter.46
  5.9 0.8 scatter.49
  6.7 0.8 scatter.50
  7.5 0.8 scatter.51
  8.3 0.8 scatter.54
  9.1 0.8 scatter.55
  9.9 0.7 scatter.56
  10.6 0.7 convert_bitcast_fusion
  11.2 0.1 scatter.59
  11.3 0.7 pad_maximum_fusion.wp
  12.0 187.9 %forward.1 = (bf16[8,256,1024]{2,1,0:T(8,128)(2,1)}, bf16[768,2048]{1,0:T(8,128)(2,1)}, f32[256,2048]{1,0:T(8,128)}, f32[4,2048]{1,0:T(4,128)}, bf16[2,256,1024]...) custom-call(bf16[2,256,1024]{2,1,0:T(8,128)(2,1)} %tok.1, ...), custom_call_target="tpu_custom_call" | custom-call | tf_op jit(solution)/shard_map/forward/pallas_call | solution.py:510
  200.0 188.4 %backward.1 = (f32[32,4096]{1,0:T(8,128)}, f32[128,1024]{1,0:T(8,128)}, f32[32,1024]{1,0:T(8,128)}, f32[32,3072]{1,0:T(8,128)}, f32[2,256,1024]{2,1,0:T(8,128)},...) custom-call(bf16[4,256,512]{2,1,0:T(8,128)(2,1)} %get-tuple-element.182.dob, ...), custom_call_target="tpu_custom_call" | custom-call | tf_op jit(solution)/shard_map/backward/pallas_call | solution.py:866
  388.3 0.0 copy-start
  388.3 0.9 slice_bitcast_fusion
  389.3 0.6 dynamic_slice.7
  389.8 1.6 dynamic-slice_bitcast_fusion
  391.5 0.0 copy-start.3
  391.5 0.0 copy-start.4
  391.5 2.3 copy.59
  393.8 0.0 copy-done
  393.8 0.0 copy-start.2
  393.8 0.0 copy-start.1
  393.8 1.3 copy.60
  395.1 0.0 copy-done.3
  395.1 0.7 copy.61
  395.9 0.0 copy-done.4
  395.9 0.7 copy.62
  396.5 0.0 copy-done.2
  396.5 0.8 copy.63
  397.3 0.0 copy-done.1
  397.3 0.8 copy.64
  (2 shorter events, 0.0 us)
Async XLA Ops:
  388.3 5.5 %copy-start = (f32[2,256,1024]{2,1,0:T(8,128)S(1)}, f32[2,256,1024]{2,1,0:T(8,128)}, u32[]{:S(2)}) copy-start(f32[2,256,1024]{2,1,0:T(8,128)} %get-tuple-element.231) | copy-start | bytes 6291460
  391.5 3.7 copy-start.3
  391.5 4.4 %copy-start.4 = (f32[32,1024]{1,0:T(8,128)S(1)}, f32[32,1024]{1,0:T(8,128)}, u32[]{:S(2)}) copy-start(f32[32,1024]{1,0:T(8,128)} %get-tuple-element.233) | copy-start | bytes 393220
  393.8 2.7 copy-start.2
  393.8 3.5 copy-start.1

commit v3 on v2

--- a/solution.py
+++ b/solution.py
@@ -40,9 +40,10 @@
     pl.semaphore_wait(bar, len(partners))
 
 
-def fwd_kernel(hd, heads, tok, cot, wp, fa, fb, fc, normed, qkvT, oT, lse, own, vec, wT, a1, a2, a3, dob, mgrad, bout, sums, ga, gb, gc,
-               T, Ws, fb1, bt, up, r2, k1, r3, st, rt, lt, sy, ry, sc, rc, scy, rcy, sa, ra, la, sz, rz, sx, rx, so, ro, lo, ln,
-               su, ru, lu, gss, grs, gsz, grz, gs1, gr1, gs2, gr2, gsc, grc, sf1, rf1, sf2, rf2, sf3, rf3, la1, la2, la3):
+def fwd_kernel(hd, heads, tok, cot, wq, small, fa, fb, fc, normed, qkvT, oT, lse, own, vec, wT, a1, h1, a2, h2, a3, dob, mgrad, bo, sums,
+               ga, gb, gc, T, Ws, fb1, bt, up, r1, r2, r3, st, rt, lt, sy, ry, sc, rc, scy, rcy, sa, ra, la, sz, rz, sx, rx, so, ro, lo,
+               ln, su, ru, lu, gss, grs, gsz, grz, gs1, gr1, gs2, gr2, gsc, grc, sf1, rf1, sf2, rf2, sf3, rf3, la1, la2, la3,
+               sh1, qh1, sh2, qh2, sbo, qbo, lbo):
     x, c, z, y = place()
     hg = c * 2 + y
     W = heads * hd
@@ -68,26 +69,17 @@
             loc.start()
         tcp.append((zt, cp, loc))
     xz = x * 4 + z
-    wloc = pltpu.make_async_copy(wp.at[hg], Ws.at[xz, hg], la)
-    wloc.start()
-    wa = []
+    def slices(g):
+        dst = Ws.at[xz, hg]
+        out = [(wq.at[:, pl.ds(pl.multiple_of(q * D + g * W, W), W)], dst.at[:, q * W:(q + 1) * W]) for q in range(3)]
+        return out + [(small, dst.at[:, 3 * W:3 * W + 128])]
+    wa = [pltpu.make_async_copy(a, b, la.at[n]) for n, (a, b) in enumerate(slices(hg))]
     for k, (d, g) in enumerate(((yp, c * 2 + 1 - y), (sib, (1 - c) * 2 + y), (diag, (1 - c) * 2 + 1 - y))):
-        cp = rcopy(wp.at[g], Ws.at[xz, hg], sa.at[k], ra.at[k], d)
+        wa += [rcopy(a, b, sa.at[k, n], ra.at[k, n], d) for n, (a, b) in enumerate(slices(g))]
+    for cp in wa:
         cp.start()
-        wa.append(cp)
-    wloc.wait()
     for cp in wa:
         cp.wait()
-    wz = []
-    for k in range(3):
-        cp = rcopy(Ws.at[xz], Ws.at[xz], sz.at[k], rz.at[k], dev(x, c, zoff[k], y))
-        cp.start()
-        wz.append(cp)
-    wx = [rcopy(Ws.at[xz], Ws.at[xz], sx.at[3], rx.at[3], xp)]
-    wx[0].start()
-    ca = 1 - c
-    gat = ((fa, ga, True), (fb, gb, False), (fc, gc, False))
-
     def zz_of(u):
         return z if u == 0 else (z - u if u <= 3 else z + (u - 3))
 
@@ -99,6 +91,34 @@
             f()
         else:
             pl.when(cond)(f)
+
+    def w_z(u, down):
+        v = Ws.at[x * 4 + zz_of(u)]
+        k = (u if u <= 3 else u - 3) + (3 if down else 0)
+        return rcopy(v, v, sz.at[k], rz.at[k], dev(x, c, z - 1 if down else z + 1, y))
+
+    def w_arr(u):
+        v = Ws.at[x * 4 + zz_of(u)]
+        return rcopy(v, v, sz.at[u - 1], rz.at[u - 1], sib)
+
+    def w_x(u):
+        v = Ws.at[x * 4 + zz_of(u)]
+        return rcopy(v, v, sx.at[u], rx.at[u], xp)
+
+    def w_recv(d):
+        for u in (d, d + 3):
+            def go(u=u):
+                w_arr(u).wait_recv()
+                if d < 3:
+                    guard((z > 0) if u > 3 else (z < 3), lambda: w_z(u, u > 3).start())
+                w_x(u).start()
+            guard(ok(u), go)
+
+    guard(z < 3, lambda: w_z(0, False).start())
+    guard(z > 0, lambda: w_z(0, True).start())
+    w_x(0).start()
+    ca = 1 - c
+    gat = ((fa, ga, False), (fb, gb, True), (fc, gc, False))
 
     def g_start(p):
         f, g, _ = gat[p]
@@ -134,7 +154,7 @@
         g_start(p).wait()
         g_one(p, 0).start()
 
-    def ag_z0(p):
+    def ag_z0(p, d):
         guard(z < 3, lambda: g_z(p, 0, False).start())
         guard(z > 0, lambda: g_z(p, 0, True).start())
 
@@ -164,25 +184,64 @@
                 g_core(p, u).start()
             guard(ok(u), go)
 
-    def ag_end(p):
-        for u in range(7):
-            guard(ok(u), lambda: g_core(p, u).wait())
+    def ag_got(p, half):
+        own_half = ((0, True), (1, lax.rem(z, 2) == 1), (4, lax.rem(z, 2) == 0))
+        rest = ((1, z == 2), (2, z >= 2), (3, z == 3), (4, z == 1), (5, z <= 1), (6, z == 0))
+        for u, cond in (own_half if half == 0 else rest):
+            guard(cond, lambda: g_core(p, u).wait())
+
+    def ag_sent(p):
         for u in (0, 1, 2):
             guard((z >= u) & (z < 3), lambda: g_z(p, u, False).wait_send())
             guard((z + u <= 3) & (z > 0), lambda: g_z(p, u + 3 if u else 0, True).wait_send())
+
+    PLAN = {
+        0: ((ag_z0, 2, 0), (ag_two, 0, 0), (ag_two, 1, 0),),
+        1: ((ag_two, 2, 0),),
+        2: ((ag_z0, 1, 0),),
+        3: ((ag_z0, 0, 0), (ag_core, 0, 0),),
+        6: ((ag_recv, 0, 1), (ag_recv, 1, 1),),
+        7: ((ag_recv, 0, 2), (ag_recv, 1, 2),),
+        8: ((ag_two, 1, 1),),
+        10: ((ag_two, 0, 1),),
+        12: ((ag_core, 2, 0),),
+        13: ((ag_recv, 2, 1), (ag_recv, 2, 2), (ag_recv, 0, 3),),
+        14: ((ag_two, 0, 2),),
+        16: ((ag_two, 2, 1), (ag_two, 2, 2), (ag_recv, 2, 3),),
+        17: ((ag_core, 0, 1),),
+        19: ((ag_recv, 1, 3),),
+        20: ((ag_two, 2, 3),),
+        21: ((ag_two, 1, 2),),
+        22: ((ag_core, 2, 2),),
+        23: ((ag_two, 0, 3), (ag_core, 1, 0),),
+        24: ((ag_core, 2, 1), (ag_core, 2, 3), (ag_core, 0, 2), (ag_core, 1, 1),),
+        25: ((ag_core, 0, 3),),
+        26: ((ag_two, 1, 3),),
+        28: ((ag_core, 1, 2),),
+        29: ((ag_core, 1, 3),),
+    }
+
+    COT = 9
+
+    def ag_slot(i):
+        for f, p, d in PLAN.get(i, ()):
+            f(p, d)
 
     for p in (2, 0, 1):
         g_start(p).start()
     for p in (2, 0, 1):
         ag_own(p)
+    ag_slot(0)
+    w_recv(1)
+    ag_slot(1)
     ycp, ccp, cycp = [], [], []
-    for j in range(2):
+    j0 = jnp.where(lax.div(z, 2) == c, lax.rem(z, 2), 0)
+    for j in (j0, 1 - j0):
         src_z = 2 * c + j
         p = hg * 2 + j
-        arr = rcopy(tok.at[0], T.at[p], st.at[0], rt.at[j], sib)
         @pl.when(src_z != z)
         def _():
-            arr.wait_recv()
+            rcopy(tok.at[0], T.at[p], st.at[0], rt.at[j], sib).wait_recv()
         @pl.when(src_z == z)
         def _():
             pltpu.make_async_copy(tok.at[0], T.at[p], lt).wait()
@@ -192,25 +251,23 @@
         b.start()
         ycp.append(a)
         ccp.append(b)
-    for k in range(3):
-        wz[k].wait()
-        zs = lax.rem(z + 3 - k, 4)
-        cp = rcopy(Ws.at[x * 4 + zs], Ws.at[x * 4 + zs], sx.at[k], rx.at[k], xp)
-        cp.start()
-        wx.append(cp)
-    ag_z0(2)
-    ag_z0(0)
-    for p in (2, 0, 1):
-        ag_two(p, 0)
-    for j in range(2):
-        ycp[j].wait()
+    ag_slot(2)
+    w_recv(2)
+    ag_slot(3)
+    w_recv(3)
+    ag_slot(4)
+    for n, j in enumerate((j0, 1 - j0)):
+        ycp[n].wait()
         p = (c * 2 + 1 - y) * 2 + j
         cp = rcopy(T.at[p], T.at[p], scy.at[j], rcy.at[j], sib)
         cp.start()
         cycp.append(cp)
-    ag_z0(1)
-    for cp in wx:
-        cp.wait()
+    ag_slot(5)
+    for u in range(7):
+        guard(ok(u), lambda: w_x(u).wait())
+    for u in (0, 1, 2):
+        guard((z >= u) & (z < 3), lambda: w_z(u, False).wait_send())
+        guard((z + u <= 3) & (z > 0), lambda: w_z(u + 3 if u else 0, True).wait_send())
     for xx in range(2):
         for zz in range(4):
             for cc in range(2):
@@ -229,6 +286,7 @@
     for j in range(2):
         ccp[j].wait()
         cycp[j].wait()
+    ag_slot(6)
     shift = t * vec[0:1, :] + vec[1:2, :]
     vec[14:15, :] = jnp.broadcast_to(t, (1, D))
     vec[15:16, :] = shift
@@ -250,6 +308,7 @@
     lax.fori_loop(0, T.shape[0], blk, 0)
     keep = pltpu.make_async_copy(T, normed, ln)
     keep.start()
+    ag_slot(7)
     keep.wait()
     def cot_copy(i):
         zt = 2 * c + i
@@ -281,11 +340,6 @@
         QB, KB = 2 * R, 512
         cs = LOG2E * hd ** -0.5
         nk = N // KB
-        PLAN = {0: [(ag_recv, 2, 1), (ag_recv, 0, 1), (ag_core, 2, 0), (ag_core, 0, 0)], 1: [(ag_recv, 1, 1), (ag_core, 1, 0)],
-                2: [(ag_two, 2, 1), (ag_two, 0, 1)], 3: [(ag_recv, 2, 2), (ag_recv, 0, 2)], 4: [(ag_recv, 1, 2)], 5: [(ag_two, 1, 1)],
-                6: [(ag_two, 2, 2), (ag_two, 0, 2), (ag_core, 2, 1), (ag_core, 0, 1)], 7: [(ag_recv, 2, 3), (ag_recv, 0, 3)],
-                8: [(ag_recv, 1, 3)], 9: [(ag_two, 1, 2), (ag_core, 1, 1)], 10: [(ag_two, 2, 3), (ag_two, 0, 3), (ag_core, 2, 2), (ag_core, 0, 2)],
-                12: [(ag_two, 1, 3), (ag_core, 1, 2)], 14: [(ag_core, 2, 3), (ag_core, 0, 3)]}
         def group(k, carry):
             cc = jnp.where((k == 1) | (k == 2), 1 - c, c)
             yy = jnp.where(k < 2, 1 - y, y)
@@ -293,14 +347,13 @@
             qcols = pl.ds(g * QB, QB)
             def head(h, carry):
                 step = k * heads + h
-                for when, work in PLAN.items():
-                    @pl.when(step == when)
-                    def _():
-                        for f, p, d in work:
-                            f(p, d)
-                @pl.when(step == 9)
-                def _():
-                    cot_start()
+                for i in range(16):
+                    if 8 + i in PLAN or COT == 8 + i:
+                        @pl.when(step == i)
+                        def _():
+                            ag_slot(8 + i)
+                            if COT == 8 + i:
+                                cot_start()
                 qt = qkvT[pl.ds(h * hd, hd), qcols]
                 def scores(i):
                     return dot_nn(k_s[h, i * KB:(i + 1) * KB, :], qt)
@@ -350,9 +403,27 @@
     FF = fb1.shape[1]
     C = 2 * R
 
-    def middle_part(Wo, mid_s, n2, n2T, oacc, dacc, f1b, f2b, sb1, sb2, sb3, lw, l1, l2):
-        ag_core(1, 3)
-        ag_end(2)
+    def out_copy(bout, j):
+        zt = 2 * c + j
+        return zt, rcopy(bout.at[j], bo.at[lax.rem(z, 2)], sbo.at[j], qbo.at[lax.rem(z, 2)], dev(x, lax.div(z, 2), zt, y)), \
+            pltpu.make_async_copy(bout.at[j], bo.at[lax.rem(z, 2)], lbo)
+    def out_wait(bout):
+        for i in range(2):
+            zt, cp, lc = out_copy(bout, i)
+            @pl.when(2 * c + i != z)
+            def _():
+                rcopy(bout.at[0], bo.at[i], sbo.at[0], qbo.at[i], sib).wait_recv()
+            @pl.when(2 * c + i == z)
+            def _():
+                pltpu.make_async_copy(bout.at[0], bo.at[i], lbo).wait()
+            @pl.when(zt != z)
+            def _():
+                cp.wait_send()
+
+    def middle_part(Wo, mid_s, n2, n2T, oacc, dacc, f1b, f2b, p1, sb1, k1, p2, sb2, k2, sb3, bout, lw, l1, l2):
+        ag_slot(24)
+        ag_got(2, 0)
+        ag_got(2, 1)
         cpw = pltpu.make_async_copy(gc, Wo, lw)
         cpw.start()
         bT = bt[...].reshape(4 * W, C).T
@@ -368,14 +439,16 @@
             nb = (cen * r * vec[7:8, :] + vec[8:9, :]).astype(bf16)
             n2[j] = nb
             n2T[:, :, j * R:(j + 1) * R] = nb.T.reshape(4, D // 4, R)
-        ag_end(0)
-        ag_end(1)
+        ag_slot(25)
+        ag_got(0, 0)
+        ag_got(0, 1)
         cot_wait()
+        ag_got(1, 0)
 
         def order(s):
-            cc = jnp.where(s < 4, 1 - c, c)
-            xx = jnp.where(lax.rem(lax.div(s, 2), 2) == 0, x, 1 - x)
-            zp = lax.rem(s, 2)
+            zp = jnp.where(s < 4, lax.div(z, 2), 1 - lax.div(z, 2))
+            xx = jnp.where(lax.rem(lax.div(s, 2), 2) == 0, 1 - x, x)
+            cc = lax.rem(s, 2)
             return xx, cc, zp, (xx * 2 + cc) * 2 + zp
         def loads(s):
             xx, cc, zp, j = order(s)
@@ -388,29 +461,70 @@
         dacc[...] = jnp.zeros_like(dacc)
         def sends(s):
             slot = lax.rem(s, 2)
-            return (rcopy(sb1.at[slot], T.at[lax.rem(s + 4, 8)], sf1.at[s], rf1.at[lax.rem(s + 4, 8)], sib),
-                    rcopy(sb2.at[slot], r2.at[lax.rem(s, 4)], sf2.at[lax.rem(s, 4)], rf2.at[lax.rem(s, 4)], sib))
-        def out1(s):
-            j = order(s)[3]
-            return [pltpu.make_async_copy(T.at[s, :, pl.ds(q * C, C)], a1.at[q, :, pl.ds(pl.multiple_of(j * C, C), C)], la1.at[s, q]) for q in range(2)]
-        def out2(s):
-            xx, cc, zp, j = order(s)
-            return pltpu.make_async_copy(r2.at[s - 4], a2.at[xx, zp], la2.at[s - 4])
+            return (rcopy(sb1.at[slot], r1.at[slot], sf1.at[s], rf1.at[s], sib), rcopy(sb2, r2, sf2.at[s], rf2.at[s], sib))
+        def cols_of(s):
+            return pl.ds(pl.multiple_of(order(s)[3] * C, C), C)
+        def go1(s):
+            slot = lax.rem(s, 2)
+            out = []
+            for q in range(2):
+                cs_ = pl.ds(q * C, C)
+                out.append(rcopy(k1.at[slot, :, 1 - y, :, cs_], h1.at[q, :, :, cols_of(s)], sh1.at[s, q], qh1.at[s, q], yp))
+                out.append(pltpu.make_async_copy(k1.at[slot, :, y, :, cs_], a1.at[q, :, :, cols_of(s)], la1.at[s, q]))
+            return out
+        def go2(s):
+            slot, zp = lax.rem(lax.div(s, 2), 2), order(s)[2]
+            i = lax.div(s, 4)
+            return (rcopy(k2.at[slot], h2.at[pl.ds(zp * 2, 2)], sh2.at[i], qh2.at[i], xp),
+                    pltpu.make_async_copy(k2.at[slot], a2.at[pl.ds(zp * 2, 2)], la2.at[i]))
+        def keeps(s):
+            return lax.rem(s, 2) == c
+        def away(s):
+            return lax.rem(lax.div(s, 2), 2) == 0
+        def finish(s):
+            slot = lax.rem(s, 2)
+            sends(s)[0].wait_recv()
+            @pl.when(s >= 2)
+            def _():
+                for n, cp in enumerate(go1(s - 2)):
+                    cp.wait() if n % 2 else cp.wait_send()
+            k1[slot] = (p1[...].astype(f32) + r1[slot].astype(f32)).astype(bf16)
+            for cp in go1(s):
+                cp.start()
+            @pl.when(keeps(s))
+            def _():
+                sends(s)[1].wait_recv()
+                @pl.when(s >= 4)
+                def _():
+                    @pl.when(away(s))
+                    def _():
+                        go2(s - 4)[0].wait_send()
+                    @pl.when(jnp.logical_not(away(s)))
+                    def _():
+                        go2(s - 4)[1].wait()
+                k2[lax.rem(lax.div(s, 2), 2)] = (p2[...].astype(f32) + r2[...].astype(f32)).astype(bf16).reshape(k2.shape[1:])
+                @pl.when(away(s))
+                def _():
+                    go2(s)[0].start()
+                @pl.when(jnp.logical_not(away(s)))
+                def _():
+                    go2(s)[1].start()
         def chunk(s, carry):
             slot = lax.rem(s, 2)
             xx, cc, zp, j = order(s)
             for cp in loads(s):
                 cp.wait()
+            for i in range(8):
+                if 26 + i in PLAN or i == 3:
+                    @pl.when(s == i)
+                    def _():
+                        ag_slot(26 + i)
+                        if i == 3:
+                            ag_got(1, 1)
             @pl.when(s < 7)
             def _():
                 for cp in loads(s + 1):
                     cp.start()
-            @pl.when(s >= 2)
-            def _():
-                sends(s - 2)[0].wait_send()
-            @pl.when((s >= 2) & (s < 6))
-            def _():
-                sends(s - 2)[1].wait_send()
             f1c = f1b[slot].reshape(D, C)
             f2c = f2b[slot].reshape(C, D)
             u2 = up[...].reshape(C, D)
@@ -421,36 +535,47 @@
             hgr = (da * (ph + h * (jnp.exp(-0.5 * h * h) * 0.3989422804014327))).astype(bf16)
             oacc[...] += dot_nn(act, f2c).reshape(2, R, D)
             sums[pl.ds(4 + lax.div(j, 2), 1), pl.ds(pl.multiple_of(lax.rem(j, 2) * C, C), C)] = jnp.sum(hgr.astype(f32), axis=0, keepdims=True)
-            g2 = dot_nn(act.T, u2)
             dacc[...] += dot_nt(hgr, f1c).reshape(2, R, D)
+            @pl.when(s > 0)
+            def _():
+                finish(s - 1)
+            @pl.when(s >= 2)
+            def _():
+                sends(s - 2)[0].wait_send()
+            @pl.when((s >= 2) & jnp.logical_not(keeps(s)))
+            def _():
+                sends(s - 2)[1].wait_send()
             for q in range(2):
-                sb1[slot, :, q * C:(q + 1) * C] = dot_nn(n2T[q * 2 + 1 - c], hgr).astype(bf16)
-            @pl.when(s < 4)
-            def _():
-                sb2[slot] = g2.astype(bf16)
+                sb1[slot, :, :, :, q * C:(q + 1) * C] = dot_nn(n2T[q * 2 + 1 - c], hgr).astype(bf16).reshape(4, 2, R // 8, C)
+            sends(s)[0].start()
+            g2 = dot_nn(act.T, u2).astype(bf16)
+            @pl.when(keeps(s))
+            def _():
+                p2[...] = g2
+            @pl.when(jnp.logical_not(keeps(s)))
+            def _():
+                sb2[...] = g2
                 sends(s)[1].start()
-                for q in range(2):
-                    k1[s, :, q * C:(q + 1) * C] = dot_nn(n2T[q * 2 + c], hgr).astype(bf16)
-            sends(s)[0].start()
-            @pl.when(s >= 4)
-            def _():
-                sends(s)[1].wait_recv()
-                r2[s - 4] = (r2[s - 4].astype(f32) + g2).astype(bf16)
-                out2(s).start()
-                rcopy(sb1.at[0], T.at[s], sf1.at[0], rf1.at[s], sib).wait_recv()
-                for q in range(2):
-                    cols = slice(q * C, (q + 1) * C)
-                    T[s, :, cols] = (T[s, :, cols].astype(f32) + dot_nn(n2T[q * 2 + c], hgr)).astype(bf16)
-                for cp in out1(s):
-                    cp.start()
+            for q in range(2):
+                p1[:, :, :, q * C:(q + 1) * C] = dot_nn(n2T[q * 2 + c], hgr).astype(bf16).reshape(4, 2, R // 8, C)
             return carry
         lax.fori_loop(0, 8, chunk, 0)
+        for j in range(2):
+            bout[j] = (mid_s[j] + oacc[j] + vec[9:10, :]).astype(bf16)
+            zt, cp, lc = out_copy(bout, j)
+            @pl.when(zt != z)
+            def _():
+                cp.start()
+            @pl.when(zt == z)
+            def _():
+                lc.start()
+        last = jnp.int32(7)
+        finish(last)
 
         tot = [jnp.zeros((1, D), f32) for _ in range(4)]
         ags = []
         for j in range(2):
             v = mid_s[j]
-            bout[j] = (v + oacc[j] + vec[9:10, :]).astype(bf16)
             cen, r = norm(v)
             xh = cen * r
             u = dacc[j]
@@ -469,11 +594,6 @@
             rcopy(sb3.at[q], r3.at[q], sf3.at[q], rf3.at[q], sib).start()
         for q in range(4):
             dob[q] = dot_nt(Wo[q // 2, q % 2].reshape(D // 4, D), ag).astype(bf16)
-        for s in range(4):
-            rcopy(sb1.at[0], T.at[s], sf1.at[0], rf1.at[s], sib).wait_recv()
-            T[s] = (T[s].astype(f32) + k1[s].astype(f32)).astype(bf16)
-            for cp in out1(s):
-                cp.start()
         for q in range(2):
             rcopy(sb3.at[q], r3.at[q], sf3.at[q], rf3.at[q], sib).wait()
             r3[q] = (r3[q].astype(f32) + dot_nn(bt[q * 2 + c], ag)).astype(bf16)
@@ -481,21 +601,33 @@
         cp3.start()
         for s in (6, 7):
             sends(s)[0].wait_send()
+            @pl.when(c != s % 2)
+            def _():
+                sends(s)[1].wait_send()
+            for n, cp in enumerate(go1(jnp.int32(s))):
+                cp.wait() if n % 2 else cp.wait_send()
         for s in range(8):
-            for cp in out1(s):
-                cp.wait()
-        for s in range(4, 8):
-            out2(s).wait()
+            for cp in go1(jnp.int32(s))[::2]:
+                cp.wait_recv()
+        go2(4 + c)[0].wait_send()
+        go2(6 + c)[1].wait()
+        for i in range(2):
+            go2(i * 4 + c)[0].wait_recv()
         cp3.wait()
+        out_wait(bout)
+        for p in range(3):
+            ag_sent(p)
 
     SD = pltpu.SemaphoreType.DMA
     V = pltpu.VMEM
+    blk1 = (4, 2, R // 8, 2 * C)
     pl.run_scoped(middle_part, V(gc.shape, bf16), V((2, R, D), f32), V((2, R, D), bf16), V((4, D // 4, C), bf16), V((2, R, D), f32),
                   V((2, R, D), f32), V((2,) + ga.shape[:5] + (C,), bf16), V((2, 2) + gb.shape[3:], bf16),
-                  V((2, D // 4, 2 * C), bf16), V((2, C, D), bf16), V((2, D // 4, D), bf16), SD, SD((2,)), SD((2,)))
-
-
-def forward_kernel(tok, cot, wp, fa, fb, fc, heads, hd):
+                  V(blk1, bf16), V((2,) + blk1, bf16), V((2,) + blk1, bf16), V((C, D), bf16), V((C, D), bf16), V((2, 2) + gb.shape[3:], bf16),
+                  V((2, D // 4, D), bf16), V((2, R, D), bf16), SD, SD((2,)), SD((2,)))
+
+
+def forward_kernel(tok, cot, wq, small, fa, fb, fc, heads, hd):
     n_it, R, D = tok.shape
     FF = fa.shape[1]
     W = heads * hd
@@ -509,24 +641,26 @@
     full = lambda a: sd((2, 2, 4, 2) + a.shape, bf16)
     return pl.pallas_call(
         functools.partial(fwd_kernel, hd, heads),
-        in_specs=[hbm] * 6,
-        out_specs=[hbm] + [vm] * 6 + [hbm] * 3 + [vm] * 4 + [hbm] * 3,
+        in_specs=[hbm] * 7,
+        out_specs=[hbm] + [vm] * 6 + [hbm] * 5 + [vm] * 2 + [hbm, vm] + [hbm] * 3,
         out_shape=[
             sd((8, R, D), bf16), sd((3 * W, N), bf16), sd((W, N), f32), sd((heads, N), f32), sd((2, R, D), bf16), sd((16, D), f32),
-            sd((3 * W, D), bf16), sd((2, D // 4, FF), bf16), sd((2, 2, C, D), bf16), sd((2, D // 4, D), bf16), sd((4, W, C), bf16),
+            sd((3 * W, D), bf16), sd((2, 4) + fa.shape, bf16), sd((2, 4) + fa.shape, bf16), sd((4, 2) + fb.shape, bf16),
+            sd((4, 2) + fb.shape, bf16), sd((2, D // 4, D), bf16), sd((4, W, C), bf16),
             sd((2, R, D), f32), sd((2, R, D), bf16), sd((16, D), f32), full(fa), full(fb), full(fc),
         ],
         scratch_shapes=[
             V((8, R, D), bf16), V((8, 4, 32, 3 * W + 128), bf16), V((8, FF), f32), V((4, W, C), bf16), V((2, R, D), bf16),
-            V((4, C, D), bf16), V((4, D // 4, D), bf16), V((2, D // 4, D), bf16),
+            V((2, 4, 2, R // 8, 2 * C), bf16), V((C, D), bf16), V((2, D // 4, D), bf16),
             S((2,)), S((2,)), S, S((2,)), S((2,)), S((2,)), S((2,)), S((2,)), S((2,)),
-            S((3,)), S((3,)), S, S((3,)), S((3,)), S((4,)), S((4,)), S((3,)), S((3,)), S, S,
+            S((3, 4)), S((3, 4)), S((4,)), S((6,)), S((6,)), S((7,)), S((7,)), S((3,)), S((3,)), S, S,
             S((2,)), S((2,)), S, S((3,)), S((3,)), S((3, 6)), S((3, 6)), S((3, 7)), S((3, 7)), S((3, 7)), S((3, 7)), S((3, 7)), S((3, 7)),
-            S((8,)), S((8,)), S((4,)), S((4,)), S((2,)), S((2,)), S((8, 2)), S((4,)), S,
+            S((8,)), S((8,)), S((8,)), S((8,)), S((2,)), S((2,)), S((8, 2)), S((2,)), S,
+            S((8, 2)), S((8, 2)), S((2,)), S((2,)), S((2,)), S((2,)), S,
         ],
         compiler_params=pltpu.CompilerParams(collective_id=0, has_side_effects=True, vmem_limit_bytes=60 << 20),
         name="forward",
-    )(tok, cot, wp, fa, fb, fc)
+    )(tok, cot, wq, small, fa, fb, fc)
 
 
 def put_sum(dst, pieces):
@@ -536,11 +670,11 @@
     dst[...] = total.astype(dst.dtype)
 
 
-def tail_kernel(hd, heads, dob, qkvT, oT, lse, a1, a2, a3, normed, wT, own, rows, mgrad, sums0, bout,
-                o1, o2, o3, gq, home, sums, bo,
+def tail_kernel(hd, heads, dob, qkvT, oT, lse, a1, h1, a2, h2, a3, normed, wT, own, rows, mgrad, sums0,
+                o1, o2, o3, gq, home, sums,
                 do_s, dq_s, k1, r11, r12, r13, k2, r21, r22, r23, k3, r31, r32, r33,
-                Gb, gx, gz, go, ds_s, dr_c, dy_s, dr_y, ig, hm, vs, vr,
-                sd, rd, ld, s1, q1, s2, q2, s3, q3, lk, sg, qg, sgz, qgz, sga, qga, sdc, qdc, sdy, qdy, sh, qh, lh, sv, qv, ll, sb, qb, lb):
+                nm, w_s, Gb, gx, gz, go, ds_s, dr_c, dy_s, dr_y, ig, hm, vs, vr,
+                sd, rd, ld, s1, q1, s2, q2, s3, q3, lk, sg, qg, sgz, qgz, sga, qga, sdc, qdc, sdy, qdy, sh, qh, lh, sv, qv, ll, lnm):
     x, c, z, y = place()
     hg = c * 2 + y
     W = heads * hd
@@ -560,22 +694,25 @@
     n1, n2 = k1.shape[2] // 2, k2.shape[2] // 2
 
     class Piece:
-        def __init__(self, i, h, n, a, k, r1, r2, r3, out, s, q, lsem, yfirst):
+        def __init__(self, i, h, n, a, first, k, r1, r2, r3, out, s, q, lsem, yfirst):
+            self.h = None if first is None else part(first, h, n)
             self.a, self.k, self.r1, self.r2, self.r3, self.out = [part(v, h, n) for v in (a, k, r1, r2, r3, out)]
             self.s, self.q, self.lsem, self.yfirst, self.b = s, q, lsem, yfirst, h * 5
             self.i = i
         def copies(self):
             b, s, q = self.b, self.s, self.q
             if self.yfirst:
-                first = rcopy(self.a.at[:, :, 1 - y], self.r1, s.at[b], q.at[b], yp)
                 second = rcopy(self.k.at[1 - x], self.r2, s.at[b + 1], q.at[b + 1], xp)
-                kept = self.a.at[:, :, y]
                 mine = lambda zz: self.k.at[x, zz]
             else:
+                second = rcopy(self.k.at[:, 1 - y], self.r2, s.at[b + 1], q.at[b + 1], yp)
+                mine = lambda zz: self.k.at[zz, y]
+            if self.h is None:
                 first = rcopy(self.a.at[1 - x], self.r1, s.at[b], q.at[b], xp)
-                second = rcopy(self.k.at[:, 1 - y], self.r2, s.at[b + 1], q.at[b + 1], yp)
                 kept = self.a.at[x]
-                mine = lambda zz: self.k.at[zz, y]
+            else:
+                first = pltpu.make_async_copy(self.h, self.r1, s.at[b])
+                kept = self.a
             zs = [rcopy(mine(zoff[j]), self.r3.at[j], s.at[b + 2 + j], q.at[b + 2 + j], zp[j]) for j in range(3)]
             return first, second, zs, pltpu.make_async_copy(kept, self.k, self.lsem.at[self.i]), mine
         def start(self):
@@ -608,78 +745,122 @@
                 cp.wait()
             put_sum(self.out, [mine(z)[...]] + [self.r3[j] for j in range(3)])
 
-    f1 = [Piece(h, h, n1, a1, k1, r11, r12, r13, o1, s1, q1, lk, True) for h in range(2)]
-    f2 = [Piece(2 + h, h, n2, a2, k2, r21, r22, r23, o2, s2, q2, lk, False) for h in range(2)]
-    f3 = Piece(4, 0, None, a3, k3, r31, r32, r33, o3, s3, q3, lk, False)
-    f2[0].start()
-    f1[0].start()
-
-    def out_copy(j):
-        zt = 2 * c + j
-        return zt, rcopy(bout.at[j], bo.at[lax.rem(z, 2)], sb.at[j], qb.at[lax.rem(z, 2)], dev(x, lax.div(z, 2), zt, y))
-    def out_start():
-        for j in range(2):
-            zt, cp = out_copy(j)
-            @pl.when(zt != z)
-            def _():
-                cp.start()
-            @pl.when(zt == z)
-            def _():
-                pltpu.make_async_copy(bout.at[j], bo.at[lax.rem(z, 2)], lb).start()
-    def out_wait():
-        for i in range(2):
-            @pl.when(2 * c + i != z)
-            def _():
-                rcopy(bout.at[0], bo.at[i], sb.at[0], qb.at[i], sib).wait_recv()
-            @pl.when(2 * c + i == z)
-            def _():
-                pltpu.make_async_copy(bout.at[0], bo.at[i], lb).wait()
-            zt, cp = out_copy(i)
-            @pl.when(zt != z)
-            def _():
-                cp.wait_send()
-    out_start()
+    f1 = [Piece(h, h, n1, a1, h1, k1, r11, r12, r13, o1, s1, q1, lk, True) for h in range(2)]
+    f2 = [Piece(2 + h, h, n2, a2, h2, k2, r21, r22, r23, o2, s2, q2, lk, False) for h in range(2)]
+    f3 = Piece(4, 0, None, a3, None, k3, r31, r32, r33, o3, s3, q3, lk, False)
+    for piece in (f2[0], f1[0], f2[1], f1[1], f3):
+        piece.start()
 
     QB, KB = N // 4, 512
     cs = LOG2E * hd ** -0.5
     sc = hd ** -0.5
     nk = N // KB
 
+    ld_n = pltpu.make_async_copy(normed, nm, lnm.at[0])
+    ld_w = pltpu.make_async_copy(wT, w_s, lnm.at[1])
+    ld_n.start()
+    ld_w.start()
+
+    def G_first(pr):
+        rows_ = [dq_s[q * W + pr * 2 * hd:q * W + (pr + 1) * 2 * hd, :] for q in range(3)]
+        g = dot_nn(jnp.concatenate(rows_, axis=0), nm[...].reshape(N, nm.shape[2])).astype(bf16).T
+        Gb[pr] = g.reshape(Gb.shape[1:])
+        G_x(pr).start()
+    def G_x(pr):
+        return rcopy(Gb.at[pr, 1 - x], gx.at[pr], sg.at[pr], qg.at[pr], xp)
+    def G_z(pr):
+        return [rcopy(Gb.at[pr, x, :, zoff[j]], gz.at[pr, j], sgz.at[pr, j], qgz.at[pr, j], zp[j]) for j in range(3)]
+    def G_second(pr):
+        G_x(pr).wait()
+        def add(i, carry):
+            cc, zz = lax.div(i, 4), lax.rem(i, 4)
+            put_sum(Gb.at[pr, x, cc, zz], [Gb[pr, x, cc, zz], gx[pr, cc, zz]])
+            return carry
+        lax.fori_loop(0, 8, add, 0)
+        for cp in G_z(pr):
+            cp.start()
+    def G_own(pr):
+        cps = [rcopy(Gb.at[pr, x, cc, z, yy], go.at[pr, hg], sga.at[pr, k], qga.at[pr, k], d)
+               for k, (d, cc, yy) in enumerate(((sib, 1 - c, y), (yp, c, 1 - y), (diag, 1 - c, 1 - y)))]
+        return cps, pltpu.make_async_copy(Gb.at[pr, x, c, z, y], go.at[pr, hg], ll.at[pr])
+    def G_third(pr):
+        for cp in G_z(pr):
+            cp.wait()
+        def add(i, carry):
+            cc, yy = lax.div(i, 2), lax.rem(i, 2)
+            put_sum(Gb.at[pr, x, cc, z, yy], [Gb[pr, x, cc, z, yy]] + [gz[pr, k, cc, yy] for k in range(3)])
+            return carry
+        lax.fori_loop(0, 4, add, 0)
+        cps, own_ = G_own(pr)
+        for cp in cps:
+            cp.start()
+        own_.start()
+    def G_done(pr):
+        cps, own_ = G_own(pr)
+        own_.wait()
+        for cp in cps:
+            cp.wait()
+        D_ = gq.shape[1] // 3
+        for g in range(4):
+            for q in range(3):
+                at = q * D_ + g * W + pr * 2 * hd
+                gq[:, at:at + 2 * hd] = go[pr, g, :, q * 2 * hd:(q + 1) * 2 * hd].astype(f32)
+
+    PLAN = {
+        1: ((Piece.second, f1[1]),),
+        2: ((Piece.second, f2[0]),),
+        5: ((Piece.second, f2[1]), (Piece.third, f1[1]),),
+        6: ((Piece.second, f1[0]),),
+        7: ((Piece.third, f2[0]),),
+        8: ((Piece.second, f3),),
+        11: ((Piece.third, f2[1]), (Piece.third, f3),),
+        13: ((G_second, 0),),
+        15: ((Piece.third, f1[0]),),
+        17: ((G_second, 1),),
+        19: ((G_third, 0),),
+        21: ((G_third, 1), (G_done, 0),),
+        22: ((Piece.finish, f2[0]),),
+        24: ((Piece.finish, f3), (G_done, 1),),
+        25: ((Piece.finish, f1[0]), (Piece.finish, f1[1]), (Piece.finish, f2[1]),),
+    }
+
+    def slot(i):
+        for f, a in PLAN.get(i, ()):
+            f(a)
+
     def attention(k_s, v_s, dk_s, dv_s):
-        for h in range(heads):
-            k_s[h] = qkvT[W + h * hd:W + (h + 1) * hd, :].T
-            v_s[h] = qkvT[2 * W + h * hd:2 * W + (h + 1) * hd, :].T
-        dk_s[...] = jnp.zeros_like(dk_s)
-        dv_s[...] = jnp.zeros_like(dv_s)
         loc.wait()
-        def group(k, carry):
-            @pl.when(k > 0)
-            def _():
-                rcopy(dob.at[0], do_s.at[0], sd.at[k - 1], rd.at[k - 1], sib).wait()
-            cc = jnp.where((k == 1) | (k == 3), 1 - c, c)
-            yy = jnp.where(k >= 2, 1 - y, y)
-            g = cc * 2 + yy
-            qcols = pl.ds(g * QB, QB)
-            def head(h, carry):
-                @pl.when((k == 1) & (h == 1))
+        def head(h, carry):
+            hr = pl.ds(h * hd, hd)
+            @pl.when(h == 2)
+            def _():
+                ld_n.wait()
+                G_first(0)
+            k_s[...] = qkvT[pl.ds(W + h * hd, hd), :].T
+            v_s[...] = qkvT[pl.ds(2 * W + h * hd, hd), :].T
+            dk_s[...] = jnp.zeros_like(dk_s)
+            dv_s[...] = jnp.zeros_like(dv_s)
+            def group(k, carry):
+                step = h * 4 + k
+                @pl.when((step > 0) & (step < 4))
                 def _():
-                    f2[1].start()
-                    f1[1].start()
-                @pl.when((k == 2) & (h == 1))
-                def _():
-                    f2[0].second()
-                @pl.when((k == 2) & (h == 3))
-                def _():
-                    f1[0].second()
-                    f3.start()
-                hr = pl.ds(h * hd, hd)
+                    rcopy(dob.at[0], do_s.at[0], sd.at[k - 1], rd.at[k - 1], sib).wait()
+                for i in range(16):
+                    if i in PLAN:
+                        @pl.when(step == i)
+                        def _():
+                            slot(i)
+                cc = jnp.where((k == 1) | (k == 3), 1 - c, c)
+                yy = jnp.where(k >= 2, 1 - y, y)
+                g = cc * 2 + yy
+                qcols = pl.ds(g * QB, QB)
                 qt = qkvT[hr, qcols]
                 dt = do_s[g, hr, :]
                 delta = jnp.sum(dt.astype(f32) * oT[hr, qcols], axis=0, keepdims=True)
                 ls = lse[pl.ds(h, 1), qcols]
                 def first(i):
                     ks = slice(i * KB, (i + 1) * KB)
-                    return dot_nn(k_s[h, ks, :], qt), dot_nn(v_s[h, ks, :], dt)
+                    return dot_nn(k_s[ks, :], qt), dot_nn(v_s[ks, :], dt)
                 dq = None
                 cur = first(0)
                 for i in range(nk):
@@ -690,104 +871,97 @@
                     ds = (p * (dp - delta)).astype(bf16)
                     prt = dot_nn(qkvT[pl.ds(W + h * hd, hd), ks], ds)
                     dq = prt if dq is None else dq + prt
-                    dk_s[h, :, ks] += dot_nt(qt, ds)
-                    dv_s[h, :, ks] += dot_nt(dt, p.astype(bf16))
+                    dk_s[:, ks] += dot_nt(qt, ds)
+                    dv_s[:, ks] += dot_nt(dt, p.astype(bf16))
                     cur = nxt
                 dq_s[hr, qcols] = (dq * sc).astype(bf16)
                 return carry
-            lax.fori_loop(0, heads, head, 0)
+            lax.fori_loop(0, 4, group, 0)
+            dq_s[pl.ds(W + h * hd, hd), :] = (dk_s[...] * sc).astype(bf16)
+            dq_s[pl.ds(2 * W + h * hd, hd), :] = dv_s[...].astype(bf16)
             return carry
-        lax.fori_loop(0, 4, group, 0)
-        for h in range(heads):
-            dq_s[W + h * hd:W + (h + 1) * hd, :] = (dk_s[h] * sc).astype(bf16)
-            dq_s[2 * W + h * hd:2 * W + (h + 1) * hd, :] = dv_s[h].astype(bf16)
-
-    pl.run_scoped(attention, pltpu.VMEM((heads, N, hd), bf16), pltpu.VMEM((heads, N, hd), bf16),
-                  pltpu.VMEM((heads, hd, N), f32), pltpu.VMEM((heads, hd, N), f32))
-
-    def after(nm, w_s, tok_s, mg_s, dn, lsem):
+        lax.fori_loop(0, heads, head, 0)
+
+    pl.run_scoped(attention, pltpu.VMEM((N, hd), bf16), pltpu.VMEM((N, hd), bf16),
+                  pltpu.VMEM((hd, N), f32), pltpu.VMEM((hd, N), f32))
+
+    def after(tok_s, mg_s, dn, lsem):
         R = tok_s.shape[1]
-        loads = [pltpu.make_async_copy(a, b, lsem.at[i]) for i, (a, b) in enumerate(((normed, nm), (wT, w_s), (own, tok_s), (mgrad, mg_s)))]
+        B = R // 2
+        loads = [pltpu.make_async_copy(a, b, lsem.at[i]) for i, (a, b) in enumerate(((own, tok_s), (mgrad, mg_s)))]
         for cp in loads:
             cp.start()
-        loads[1].wait()
-        def proj(g, j):
-            cols = pl.ds(g * QB + j * R, R)
-            return dot_nn(dq_s[:, cols].T, w_s[...])
+        ld_w.wait()
+        def proj(g, b):
+            return dot_nn(dq_s[:, pl.ds(pl.multiple_of(g * QB + b * B, B), B)].T, w_s[...])
         g_sy, g_s, g_oy = (1 - c) * 2 + 1 - y, (1 - c) * 2 + y, c * 2 + 1 - y
-        def to_sib(a, j):
-            return rcopy(ds_s.at[a, j], dr_c.at[a, j], sdc.at[a * 2 + j], qdc.at[a * 2 + j], sib)
-        def to_y(j):
-            return rcopy(dy_s.at[j], dr_y.at[j], sdy.at[j], qdy.at[j], yp)
-        for j in range(2):
-            ds_s[0, j] = proj(g_sy, j).astype(bf16)
-            to_sib(0, j).start()
-        for j in range(2):
-            mine = proj(g_oy, j)
-            to_sib(0, j).wait()
-            dy_s[j] = (mine + dr_c[0, j].astype(f32)).astype(bf16)
-            to_y(j).start()
-        f2[1].second()
-        f1[1].second()
-        loads[0].wait()
-        nm2 = nm[...].reshape(N, nm.shape[2])
-        for q in range(3):
-            t = dot_nn(dq_s[q * W:(q + 1) * W, :], nm2).astype(bf16).T
-            Gb[..., q * W:(q + 1) * W] = t.reshape(2, 2, 4, 2, Gb.shape[4], W)
-        gxc = rcopy(Gb.at[1 - x], gx, sg, qg, xp)
-        gxc.start()
-        for j in range(2):
-            ds_s[1, j] = proj(g_s, j).astype(bf16)
-            to_sib(1, j).start()
-        for j in range(2):
-            dn[j] = proj(hg, j)
-        f2[0].third()
-        f1[0].third()
-        f3.second()
+        def rows_of(b):
+            return b // 2, pl.ds((b % 2) * B, B)
+        def to_sib(a, b):
+            j, rw = rows_of(b)
+            return rcopy(ds_s.at[a, j, rw], dr_c.at[a, j, rw], sdc.at[a * 4 + b], qdc.at[a * 4 + b], sib)
+        def to_y(b):
+            j, rw = rows_of(b)
+            return rcopy(dy_s.at[j, rw], dr_y.at[j, rw], sdy.at[b], qdy.at[b], yp)
+        for b in range(4):
+            j, rw = rows_of(b)
+            ds_s[0, j, rw, :] = proj(g_sy, b).astype(bf16)
+            to_sib(0, b).start()
+        for b in range(4):
+            j, rw = rows_of(b)
+            mine = proj(g_oy, b)
+            to_sib(0, b).wait()
+            dy_s[j, rw, :] = (mine + dr_c[0, j, rw, :].astype(f32)).astype(bf16)
+            to_y(b).start()
+        slot(16)
+        G_first(1)
+        for b in range(4):
+            j, rw = rows_of(b)
+            ds_s[1, j, rw, :] = proj(g_s, b).astype(bf16)
+            to_sib(1, b).start()
+        for b in range(4):
+            j, rw = rows_of(b)
+            dn[j, rw, :] = proj(hg, b)
         ones = jnp.ones((8, N), bf16)
         vs[...] = sums0[...]
         for row, q in ((12, 0), (13, 2)):
             tot = dot_nt(ones, dq_s[q * W:(q + 1) * W, :])
             vs[row:row + 1, :] = jnp.zeros((1, vs.shape[1]), f32)
             vs[row:row + 1, pl.ds(pl.multiple_of(hg * W, W), W)] = tot[0:1]
-        gxc.wait()
-        for cc in range(2):
-            for zz in range(4):
-                put_sum(Gb.at[x, cc, zz], [Gb[x, cc, zz], gx[cc, zz]])
-        gzs = [rcopy(Gb.at[x, :, zoff[j]], gz.at[j], sgz.at[j], qgz.at[j], zp[j]) for j in range(3)]
-        for cp in gzs:
-            cp.start()
-        f2[1].third()
-        f1[1].third()
+        slot(17)
         gain = rows[2:3, :]
         shift = rows[15:16, :]
         acc = [jnp.zeros((1, dn.shape[2]), f32) for _ in range(3)]
-        loads[2].wait()
-        loads[3].wait()
-        homes = []
-        for j in range(2):
-            to_sib(1, j).wait()
-            to_y(j).wait()
-            u = dn[j] + dr_c[1, j].astype(f32) + dr_y[j].astype(f32)
-            v = tok_s[j].astype(f32) + shift
+        for cp in loads:
+            cp.wait()
+        def home_copy(b):
+            j, rw = rows_of(b)
+            i = lax.rem(z, 2)
+            zt = 2 * c + j
+            return zt, rcopy(ig.at[j, rw], hm.at[i, rw], sh.at[b], qh.at[i, b % 2], dev(x, lax.div(z, 2), zt, y)), \
+                pltpu.make_async_copy(ig.at[j, rw], hm.at[i, rw], lh.at[b % 2])
+        for b in range(4):
+            j, rw = rows_of(b)
+            to_sib(1, b).wait()
+            to_y(b).wait()
+            u = dn[j, rw, :] + dr_c[1, j, rw, :].astype(f32) + dr_y[j, rw, :].astype(f32)
+            v = tok_s[j, rw, :].astype(f32) + shift
             cen = v - jnp.mean(v, axis=-1, keepdims=True)
             r = lax.rsqrt(jnp.mean(cen * cen, axis=-1, keepdims=True) + EPS)
             xh = cen * r
             e = u * gain
-            res = mg_s[j] + r * (e - jnp.mean(e, axis=-1, keepdims=True) - xh * jnp.mean(e * xh, axis=-1, keepdims=True))
-            ig[j] = res.astype(bf16)
+            res = mg_s[j, rw, :] + r * (e - jnp.mean(e, axis=-1, keepdims=True) - xh * jnp.mean(e * xh, axis=-1, keepdims=True))
+            ig[j, rw, :] = res.astype(bf16)
             for n, val in enumerate((u * xh, u, res)):
                 acc[n] = acc[n] + jnp.sum(val, axis=0, keepdims=True)
-            zt = 2 * c + j
-            cp = rcopy(ig.at[j], hm.at[lax.rem(z, 2)], sh.at[j], qh.at[lax.rem(z, 2)], dev(x, lax.div(z, 2), zt, y))
-            lc = pltpu.make_async_copy(ig.at[j], hm.at[lax.rem(z, 2)], lh)
+            zt, cp, lc = home_copy(b)
             @pl.when(zt != z)
             def _():
                 cp.start()
             @pl.when(zt == z)
             def _():
                 lc.start()
-            homes.append((zt, cp, lc))
+            slot(18 + b)
         vs[8:9, :] = acc[0]
         vs[9:10, :] = acc[1]
         vs[10:11, :] = acc[2] * rows[14:15, :]
@@ -795,62 +969,40 @@
         for k, d in enumerate((sib, yp, xp)):
             cp = rcopy(vs, vr.at[k], sv.at[k], qv.at[k], d)
             cp.start()
+            slot(22 + k)
             cp.wait()
             vs[...] = vs[...] + vr[k]
         zv = [rcopy(vs, vr.at[3 + k], sv.at[3 + k], qv.at[3 + k], zp[k]) for k in range(3)]
         for cp in zv:
             cp.start()
-        f3.third()
-        for cp in gzs:
-            cp.wait()
-        for cc in range(2):
-            for yy in range(2):
-                put_sum(Gb.at[x, cc, z, yy], [Gb[x, cc, z, yy]] + [gz[k, cc, yy] for k in range(3)])
-        gas = []
-        for k, (d, cc, yy) in enumerate(((sib, 1 - c, y), (yp, c, 1 - y), (diag, 1 - c, 1 - y))):
-            cp = rcopy(Gb.at[x, cc, z, yy], go.at[hg], sga.at[k], qga.at[k], d)
-            cp.start()
-            gas.append(cp)
-        lcl = pltpu.make_async_copy(Gb.at[x, c, z, y], go.at[hg], ll)
-        lcl.start()
+        slot(25)
+        for i in range(2):
+            src = 2 * c + i
+            for hb in range(2):
+                rw = pl.ds(hb * B, B)
+                @pl.when(src != z)
+                def _():
+                    rcopy(ig.at[0, rw], hm.at[i, rw], sh.at[0], qh.at[i, hb], sib).wait_recv()
+                @pl.when(src == z)
+                def _():
+                    pltpu.make_async_copy(ig.at[0, rw], hm.at[i, rw], lh.at[hb]).wait()
+                home[i, rw, :] = hm[i, rw, :].astype(f32)
         for cp in zv:
             cp.wait()
         sums[...] = vs[...] + vr[3] + vr[4] + vr[5]
-        f2[0].finish()
-        f1[0].finish()
-        f2[1].finish()
-        f1[1].finish()
-        f3.finish()
-        lcl.wait()
-        for cp in gas:
-            cp.wait()
-        D = gq.shape[1] // 3
-        for g in range(4):
-            for q in range(3):
-                gq[:, q * D + g * W:q * D + (g + 1) * W] = go[g, :, q * W:(q + 1) * W].astype(f32)
-        for i in range(2):
-            src = 2 * c + i
-            arr = rcopy(ig.at[0], hm.at[i], sh.at[0], qh.at[i], sib)
-            @pl.when(src != z)
-            def _():
-                arr.wait_recv()
-            @pl.when(src == z)
-            def _():
-                pltpu.make_async_copy(ig.at[0], hm.at[i], lh).wait()
-            home[i] = hm[i].astype(f32)
-        out_wait()
-        for zt, cp, lc in homes:
+        slot(26)
+        for b in range(4):
+            zt, cp, lc = home_copy(b)
             @pl.when(zt != z)
             def _():
                 cp.wait_send()
 
     R = own.shape[1]
     D = own.shape[2]
-    pl.run_scoped(after, pltpu.VMEM(normed.shape, bf16), pltpu.VMEM(wT.shape, bf16), pltpu.VMEM((2, R, D), bf16),
-                  pltpu.VMEM((2, R, D), f32), pltpu.VMEM((2, R, D), f32), pltpu.SemaphoreType.DMA((4,)))
-
-
-def backward_kernel(dob, qkvT, oT, lse, a1, a2, a3, normed, wT, own, rows, mgrad, sums0, bout, heads, hd):
+    pl.run_scoped(after, pltpu.VMEM((2, R, D), bf16), pltpu.VMEM((2, R, D), f32), pltpu.VMEM((2, R, D), f32), pltpu.SemaphoreType.DMA((2,)))
+
+
+def backward_kernel(dob, qkvT, oT, lse, a1, h1, a2, h2, a3, normed, wT, own, rows, mgrad, sums0, heads, hd):
     W3, N = qkvT.shape
     W = heads * hd
     _, R, D = own.shape
@@ -858,31 +1010,31 @@
     V = pltpu.VMEM
     vm = pl.BlockSpec(memory_space=pltpu.VMEM)
     hbm = pl.BlockSpec(memory_space=pl.ANY)
-    b1, b2, b3 = a1.shape[3:], a2.shape[3:], a3.shape[3:]
+    b1, b2, b3 = a1.shape[2:], a2.shape[2:], a3.shape[3:]
     def bufs(b, yfirst):
         k = (2, 4) if yfirst else (4, 2)
         return [V(k + b, bf16), V(k + b, bf16), V((4,) + b, bf16), V((3,) + b, bf16)]
     rq = D // 32
     return pl.pallas_call(
         functools.partial(tail_kernel, hd, heads),
-        in_specs=[hbm, vm, vm, vm, hbm, hbm, hbm, hbm, hbm, hbm, vm, hbm, vm, hbm],
-        out_specs=[vm] * 6 + [hbm],
+        in_specs=[hbm, vm, vm, vm, hbm, hbm, hbm, hbm, hbm, hbm, hbm, hbm, vm, hbm, vm],
+        out_specs=[vm] * 6,
         out_shape=[
             jax.ShapeDtypeStruct(b1, f32), jax.ShapeDtypeStruct(b2, f32), jax.ShapeDtypeStruct(b3, f32),
             jax.ShapeDtypeStruct((rq, 3 * D), f32), jax.ShapeDtypeStruct((2, R, D), f32), jax.ShapeDtypeStruct((16, D), f32),
-            jax.ShapeDtypeStruct((2, R, D), bf16),
         ],
         scratch_shapes=[V((4, W, N // 4), bf16), V((W3, N), bf16)] + bufs(b1, True) + bufs(b2, False) + bufs(b3, False) + [
-            V((2, 2, 4, 2, rq, W3), bf16), V((2, 4, 2, rq, W3), bf16), V((3, 2, 2, rq, W3), bf16), V((4, rq, W3), bf16),
+            V((8, R, D), bf16), V((W3, D), bf16),
+            V((2, 2, 2, 4, 2, rq, W3 // 2), bf16), V((2, 2, 4, 2, rq, W3 // 2), bf16), V((2, 3, 2, 2, rq, W3 // 2), bf16), V((2, 4, rq, W3 // 2), bf16),
             V((2, 2, R, D), bf16), V((2, 2, R, D), bf16), V((2, R, D), bf16), V((2, R, D), bf16), V((2, R, D), bf16), V((2, R, D), bf16),
             V((16, D), f32), V((6, 16, D), f32),
             S((3,)), S((3,)), S, S((10,)), S((10,)), S((10,)), S((10,)), S((5,)), S((5,)), S((5,)),
-            S, S, S((3,)), S((3,)), S((3,)), S((3,)), S((4,)), S((4,)), S((2,)), S((2,)), S((2,)), S((2,)), S, S((6,)), S((6,)), S,
-            S((2,)), S((2,)), S,
+            S((2,)), S((2,)), S((2, 3)), S((2, 3)), S((2, 3)), S((2, 3)), S((8,)), S((8,)), S((4,)), S((4,)),
+            S((4,)), S((2, 2)), S((2,)), S((6,)), S((6,)), S((2,)), S((2,)),
         ],
         compiler_params=pltpu.CompilerParams(collective_id=1, has_side_effects=True, vmem_limit_bytes=60 << 20),
         name="backward",
-    )(dob, qkvT, oT, lse, a1, a2, a3, normed, wT, own, rows, mgrad, sums0, bout)
+    )(dob, qkvT, oT, lse, a1, h1, a2, h2, a3, normed, wT, own, rows, mgrad, sums0)
 
 
 HEADS = 16
@@ -1151,17 +1303,14 @@
     heads = HEADS // 4
     W = heads * hd
     rows = w_qkv.shape[0]
-    small = jnp.zeros((32, 128), bf16)
-    for k, v in enumerate((lead_weight, lead_bias, ln1_gain, ln1_bias, q_bias, v_bias, out_bias, ln2_gain, ln2_bias, fc2_bias)):
-        small = small.at[k, :rows].set(v)
-    small = small.at[10].set(fc1_bias).at[11, :2].set(lead_hours.astype(bf16))
-    slices = w_qkv.reshape(rows, 3, 4, W).transpose(2, 0, 1, 3).reshape(4, rows, 3 * W)
-    wp = jnp.concatenate([slices, jnp.broadcast_to(small, (4, 32, 128))], axis=2)
-    normed, qkvT, oT, lse, own, vec, wT, a1, a2, a3, dob, mgrad, bout, sums0 = forward_kernel(
-        tokens_in, cotangent, wp, w_fc1, w_fc2, w_out, heads, hd)[:14]
-    grad_fc1, grad_fc2, grad_out, grad_qkv, home, sums, block_output = backward_kernel(
-        dob, qkvT, oT, lse, a1.reshape(2, 4, 2, rows, FF), a2.reshape(2, 4, 2, -1, D), a3.reshape(2, 4, 2, rows, D), normed, wT,
-        own, vec, mgrad, sums0, bout, heads, hd)
+    vectors = (lead_weight, lead_bias, ln1_gain, ln1_bias, q_bias, v_bias, out_bias, ln2_gain, ln2_bias, fc2_bias, fc1_bias,
+               lead_hours.astype(bf16))
+    small = sum(lax.pad(v[None].astype(f32), f32(0), ((k, 31 - k, 0), (0, 128 - v.shape[0], 0))) for k, v in enumerate(vectors)).astype(bf16)
+    normed, qkvT, oT, lse, own, vec, wT, a1, h1, a2, h2, a3, dob, mgrad, block_output, sums0 = forward_kernel(
+        tokens_in, cotangent, w_qkv, small, w_fc1, w_fc2, w_out, heads, hd)[:16]
+    grad_fc1, grad_fc2, grad_out, grad_qkv, home, sums = backward_kernel(
+        dob, qkvT, oT, lse, a1, h1, a2, h2, a3.reshape(2, 4, 2, rows, D), normed, wT,
+        own, vec, mgrad, sums0, heads, hd)
     index = (x * 2 + c) * 8 + z * 2 + y
     mine = lax.dynamic_slice(sums, (0, index * rows), (16, rows))
     g_fc1_bias = lax.dynamic_slice(sums[4:4 + FF // D].reshape(FF), (index * fc1_bias.shape[0],), (fc1_bias.shape[0],))

time: 399 us -> 350 us (0.88)
  Pallas kernels: 376 us -> 338 us
  local copies, waits for them, and re-layouts: 19.7 us -> 8.41 us
    pallas_call x1, Pallas kernels: 188 us -> 131 us  [backward_kernel(): pl.pallas_call(functools.partial(tail_kernel, hd, heads), in_specs=[hbm,...]
    pallas_call x1, Pallas kernels: 188 us -> 207 us  [forward_kernel(): pl.pallas_call(functools.partial(fwd_kernel, hd, heads), in_specs=[hbm] *...]
    scatter x12 -> x0, local copies, waits for them, and re-layouts: 8.51 us -> none  [the longest x10 7.75 us: on_device(): small = small.at[k, :rows].set(v)]
where the time goes in v3:
time: 350 us; the launch traced here: 349 us
  Pallas kernels  338 us (97%)
  local copies, waits for them, and re-layouts  8.41 us (2%)
    pallas_call x1, Pallas kernels, forward_kernel(): pl.pallas_call(functools.partial(fwd_kernel, hd, heads), in_specs=[hbm] *...  207 us
    pallas_call x1, Pallas kernels, backward_kernel(): pl.pallas_call(functools.partial(tail_kernel, hd, heads), in_specs=[hbm,...  131 us

profile of v3, /device:TPU:0, one launch (start us, length us, event | category | flops | bytes accessed | tf_op | source)
XLA Modules:
  0.0 349.3 jit_solution(15682727610251832927)
XLA Ops:
  0.7 0.7 convert_bitcast_fusion
  1.3 1.4 add_convert_fusion.small
  2.7 206.7 %forward.1 = (bf16[8,256,1024]{2,1,0:T(8,128)(2,1)}, bf16[768,2048]{1,0:T(8,128)(2,1)}, f32[256,2048]{1,0:T(8,128)}, f32[4,2048]{1,0:T(4,128)}, bf16[2,256,1024]...) custom-call(bf16[2,256,1024]{2,1,0:T(8,128)(2,1)} %tok.1, ...), custom_call_target="tpu_custom_call" | custom-call | tf_op jit(solution)/shard_map/forward/pallas_call | solution.py:642
  209.4 0.0 copy-start.1
  209.4 131.4 %backward.1 = (f32[32,4096]{1,0:T(8,128)}, f32[128,1024]{1,0:T(8,128)}, f32[32,1024]{1,0:T(8,128)}, f32[32,3072]{1,0:T(8,128)}, f32[2,256,1024]{2,1,0:T(8,128)}, /*index=5*/f32[16,1024]{1,0:T(8,128)}) custom-call(bf16[4,256,512]{2,1,0:T(8,128)(2,1)} %get-tuple-element.40.dob, bf16[768,2048]{1,0:T(8,128)(2,1)} %get-tuple-element.41.qkvT, ...), custom_call_target="tpu_custom_call" | custom-call | tf_op jit(solution)/shard_map/backward/pallas_call | solution.py:1018
  340.8 0.0 copy-start
  340.8 0.9 slice_bitcast_fusion
  341.8 0.6 dynamic_slice.7
  342.3 1.6 dynamic-slice_bitcast_fusion
  344.0 0.0 copy-done.1
  344.0 1.0 copy.44
  344.9 0.0 copy-done
  344.9 0.0 copy-start.4
  344.9 0.0 copy-start.5
  344.9 0.0 copy-start.3
  344.9 1.3 copy.45
  346.3 0.0 copy-done.4
  346.3 0.0 copy-start.2
  346.3 0.7 copy.46
  347.0 0.0 copy-done.5
  347.0 0.7 copy.47
  347.7 0.0 copy-done.3
  347.7 0.8 copy.48
  348.5 0.0 copy-done.2
  348.5 0.8 copy.49
  (1 shorter events, 0.0 us)
Async XLA Ops:
  209.4 134.5 %copy-start.1 = (bf16[2,256,1024]{2,1,0:T(8,128)(2,1)S(1)}, bf16[2,256,1024]{2,1,0:T(8,128)(2,1)}, u32[]{:S(2)}) copy-start(bf16[2,256,1024]{2,1,0:T(8,128)(2,1)} %get-tuple-element.88) | copy-start | bytes 3145732
  340.8 4.1 %copy-start = (f32[2,256,1024]{2,1,0:T(8,128)S(1)}, f32[2,256,1024]{2,1,0:T(8,128)}, u32[]{:S(2)}) copy-start(f32[2,256,1024]{2,1,0:T(8,128)} %get-tuple-element.89) | copy-start | bytes 6291460
  344.9 1.3 copy-start.4
  344.9 2.1 copy-start.5
  344.9 2.7 copy-start.3
  346.3 2.2 copy-start.2

commit v4 on v3

--- a/solution.py
+++ b/solution.py
@@ -40,10 +40,10 @@
     pl.semaphore_wait(bar, len(partners))
 
 
-def fwd_kernel(hd, heads, tok, cot, wq, small, fa, fb, fc, normed, qkvT, oT, lse, own, vec, wT, a1, h1, a2, h2, a3, dob, mgrad, bo, sums,
-               ga, gb, gc, T, Ws, fb1, bt, up, r1, r2, r3, st, rt, lt, sy, ry, sc, rc, scy, rcy, sa, ra, la, sz, rz, sx, rx, so, ro, lo,
+def fwd_kernel(hd, heads, tok, cot, wq, small, fa, fb, fc, normed, qkv_out, o_out, lse, own, vec, w_out_, a1, h1, a2, h2, a3, dob, mgrad, bo, sums,
+               ga, gb, gc, qkvT, oT, wT, T, Ws, fb1, bt, up, r1, r2, r3, st, rt, lt, sy, ry, sc, rc, scy, rcy, sa, ra, la, sz, rz, sx, rx, so, ro, lo,
                ln, su, ru, lu, gss, grs, gsz, grz, gs1, gr1, gs2, gr2, gsc, grc, sf1, rf1, sf2, rf2, sf3, rf3, la1, la2, la3,
-               sh1, qh1, sh2, qh2, sbo, qbo, lbo):
+               sh1, qh1, sh2, qh2, sbo, qbo, lbo, lq):
     x, c, z, y = place()
     hg = c * 2 + y
     W = heads * hd
@@ -119,21 +119,27 @@
     w_x(0).start()
     ca = 1 - c
     gat = ((fa, ga, False), (fb, gb, True), (fc, gc, False))
+    before_z = (False, True, True)
+    known = set()
 
     def g_start(p):
         f, g, _ = gat[p]
         return rcopy(f, g.at[x, c, z, y], gss.at[p], grs.at[p], sib)
 
+    def z_block(p, u):
+        g, xfirst = gat[p][1:]
+        if not before_z[p]:
+            return g.at[x, ca, zz_of(u), y]
+        return g.at[:, ca, zz_of(u), y] if xfirst else g.at[x, ca, zz_of(u)]
+
     def g_z(p, u, down):
-        g = gat[p][1]
-        v = g.at[x, ca, zz_of(u), y]
+        v = z_block(p, u)
         d = u if u <= 3 else u - 3
         k = d + (3 if down else 0)
         return rcopy(v, v, gsz.at[p, k], grz.at[p, k], dev(x, c, z - 1 if down else z + 1, y))
 
     def g_zarr(p, u):
-        g = gat[p][1]
-        v = g.at[x, ca, zz_of(u), y]
+        v = z_block(p, u)
         return rcopy(v, v, gsz.at[p, u - 1], grz.at[p, u - 1], sib)
 
     def g_one(p, u):
@@ -154,7 +160,14 @@
         g_start(p).wait()
         g_one(p, 0).start()
 
+    def one_own(p):
+        if p not in known:
+            known.add(p)
+            g_one(p, 0).wait()
+
     def ag_z0(p, d):
+        if before_z[p]:
+            one_own(p)
         guard(z < 3, lambda: g_z(p, 0, False).start())
         guard(z > 0, lambda: g_z(p, 0, True).start())
 
@@ -164,16 +177,21 @@
                 g_zarr(p, u).wait_recv()
                 if d < 3:
                     guard((z > 0) if u > 3 else (z < 3), lambda: g_z(p, u, u > 3).start())
-                g_one(p, u).start()
+                (g_two if before_z[p] else g_one)(p, u).start()
             guard(ok(u), go)
 
     def units(d):
         return (0,) if d == 0 else (d, d + 3)
 
     def ag_two(p, d):
+        if before_z[p] and d > 0:
+            return
         for u in units(d):
             def go(u=u):
-                g_one(p, u).wait()
+                if u == 0:
+                    one_own(p)
+                else:
+                    g_one(p, u).wait()
                 g_two(p, u).start()
             guard(ok(u), go)
 
@@ -196,32 +214,35 @@
             guard((z + u <= 3) & (z > 0), lambda: g_z(p, u + 3 if u else 0, True).wait_send())
 
     PLAN = {
-        0: ((ag_z0, 2, 0), (ag_two, 0, 0), (ag_two, 1, 0),),
-        1: ((ag_two, 2, 0),),
-        2: ((ag_z0, 1, 0),),
-        3: ((ag_z0, 0, 0), (ag_core, 0, 0),),
-        6: ((ag_recv, 0, 1), (ag_recv, 1, 1),),
-        7: ((ag_recv, 0, 2), (ag_recv, 1, 2),),
-        8: ((ag_two, 1, 1),),
-        10: ((ag_two, 0, 1),),
-        12: ((ag_core, 2, 0),),
-        13: ((ag_recv, 2, 1), (ag_recv, 2, 2), (ag_recv, 0, 3),),
-        14: ((ag_two, 0, 2),),
-        16: ((ag_two, 2, 1), (ag_two, 2, 2), (ag_recv, 2, 3),),
-        17: ((ag_core, 0, 1),),
-        19: ((ag_recv, 1, 3),),
-        20: ((ag_two, 2, 3),),
-        21: ((ag_two, 1, 2),),
-        22: ((ag_core, 2, 2),),
-        23: ((ag_two, 0, 3), (ag_core, 1, 0),),
-        24: ((ag_core, 2, 1), (ag_core, 2, 3), (ag_core, 0, 2), (ag_core, 1, 1),),
-        25: ((ag_core, 0, 3),),
-        26: ((ag_two, 1, 3),),
-        28: ((ag_core, 1, 2),),
-        29: ((ag_core, 1, 3),),
+        0: ((ag_two, 1, 0),),
+        2: ((ag_z0, 1, 0), (ag_two, 0, 0),),
+        3: ((ag_z0, 0, 0),),
+        5: ((ag_recv, 0, 1),),
+        6: ((ag_two, 2, 0),),
+        7: ((ag_recv, 1, 1),),
+        9: ((ag_recv, 2, 1),),
+        10: ((ag_two, 1, 1),),
+        11: ((ag_recv, 2, 2), (ag_recv, 0, 3),),
+        12: ((ag_two, 2, 1),),
+        13: ((ag_two, 0, 2),),
+        14: ((ag_two, 2, 2),),
+        15: ((ag_core, 0, 0),),
+        17: ((ag_core, 2, 0),),
+        19: ((ag_two, 0, 3),),
+        20: ((ag_recv, 1, 2),),
+        22: ((ag_core, 0, 1), (ag_core, 0, 2), (ag_recv, 2, 3),),
+        23: ((ag_core, 2, 2), (ag_core, 1, 1),),
+        24: ((ag_two, 2, 3), (ag_two, 1, 2), (ag_core, 2, 1), (ag_core, 2, 3),),
+        25: ((ag_two, 1, 3), (ag_core, 0, 3), (ag_recv, 1, 3),),
+        26: ((ag_core, 1, 2),),
+        28: ((ag_core, 1, 3),),
+        34: ((ag_recv, 0, 2),),
+        35: ((ag_z0, 2, 0),),
+        36: ((ag_core, 1, 0),),
+        38: ((ag_two, 0, 1),),
     }
 
-    COT = 9
+    COT = 14
 
     def ag_slot(i):
         for f, p, d in PLAN.get(i, ()):
@@ -293,6 +314,11 @@
     gain, bias = vec[2:3, :], vec[3:4, :]
     qb = vec[:, pl.ds(hg * W, W)].T
     def blk(p, carry):
+        for i in range(8):
+            if 34 + i in PLAN:
+                @pl.when(p == i)
+                def _():
+                    ag_slot(34 + i)
         v = T[p].astype(f32) + shift
         cen = v - jnp.mean(v, axis=-1, keepdims=True)
         r = lax.rsqrt(jnp.mean(cen * cen, axis=-1, keepdims=True) + EPS)
@@ -308,6 +334,9 @@
     lax.fori_loop(0, T.shape[0], blk, 0)
     keep = pltpu.make_async_copy(T, normed, ln)
     keep.start()
+    early = [pltpu.make_async_copy(a, b, lq.at[i]) for i, (a, b) in enumerate(((qkvT, qkv_out), (wT, w_out_), (oT, o_out)))]
+    early[0].start()
+    early[1].start()
     ag_slot(7)
     keep.wait()
     def cot_copy(i):
@@ -400,6 +429,7 @@
             cp.wait_send()
 
 
+    early[2].start()
     FF = fb1.shape[1]
     C = 2 * R
 
@@ -614,6 +644,8 @@
         for i in range(2):
             go2(i * 4 + c)[0].wait_recv()
         cp3.wait()
+        for cp in early:
+            cp.wait()
         out_wait(bout)
         for p in range(3):
             ag_sent(p)
@@ -642,7 +674,7 @@
     return pl.pallas_call(
         functools.partial(fwd_kernel, hd, heads),
         in_specs=[hbm] * 7,
-        out_specs=[hbm] + [vm] * 6 + [hbm] * 5 + [vm] * 2 + [hbm, vm] + [hbm] * 3,
+        out_specs=[hbm] * 3 + [vm] * 3 + [hbm] * 6 + [vm] * 2 + [hbm, vm] + [hbm] * 3,
         out_shape=[
             sd((8, R, D), bf16), sd((3 * W, N), bf16), sd((W, N), f32), sd((heads, N), f32), sd((2, R, D), bf16), sd((16, D), f32),
             sd((3 * W, D), bf16), sd((2, 4) + fa.shape, bf16), sd((2, 4) + fa.shape, bf16), sd((4, 2) + fb.shape, bf16),
@@ -650,13 +682,14 @@
             sd((2, R, D), f32), sd((2, R, D), bf16), sd((16, D), f32), full(fa), full(fb), full(fc),
         ],
         scratch_shapes=[
+            V((3 * W, N), bf16), V((W, N), f32), V((3 * W, D), bf16),
             V((8, R, D), bf16), V((8, 4, 32, 3 * W + 128), bf16), V((8, FF), f32), V((4, W, C), bf16), V((2, R, D), bf16),
             V((2, 4, 2, R // 8, 2 * C), bf16), V((C, D), bf16), V((2, D // 4, D), bf16),
             S((2,)), S((2,)), S, S((2,)), S((2,)), S((2,)), S((2,)), S((2,)), S((2,)),
             S((3, 4)), S((3, 4)), S((4,)), S((6,)), S((6,)), S((7,)), S((7,)), S((3,)), S((3,)), S, S,
             S((2,)), S((2,)), S, S((3,)), S((3,)), S((3, 6)), S((3, 6)), S((3, 7)), S((3, 7)), S((3, 7)), S((3, 7)), S((3, 7)), S((3, 7)),
             S((8,)), S((8,)), S((8,)), S((8,)), S((2,)), S((2,)), S((8, 2)), S((2,)), S,
-            S((8, 2)), S((8, 2)), S((2,)), S((2,)), S((2,)), S((2,)), S,
+            S((8, 2)), S((8, 2)), S((2,)), S((2,)), S((2,)), S((2,)), S, S((3,)),
         ],
         compiler_params=pltpu.CompilerParams(collective_id=0, has_side_effects=True, vmem_limit_bytes=60 << 20),
         name="forward",
@@ -671,9 +704,9 @@
 
 
 def tail_kernel(hd, heads, dob, qkvT, oT, lse, a1, h1, a2, h2, a3, normed, wT, own, rows, mgrad, sums0,
-                o1, o2, o3, gq, home, sums,
+                o1, o2, o3, gq, hm, sums,
                 do_s, dq_s, k1, r11, r12, r13, k2, r21, r22, r23, k3, r31, r32, r33,
-                nm, w_s, Gb, gx, gz, go, ds_s, dr_c, dy_s, dr_y, ig, hm, vs, vr,
+                nm, w_s, Gb, gx, gz, go, ds_s, dr_c, dy_s, dr_y, ig, vs, vr,
                 sd, rd, ld, s1, q1, s2, q2, s3, q3, lk, sg, qg, sgz, qgz, sga, qga, sdc, qdc, sdy, qdy, sh, qh, lh, sv, qv, ll, lnm):
     x, c, z, y = place()
     hg = c * 2 + y
@@ -726,7 +759,7 @@
             n0, n1_ = self.k.shape[0], self.k.shape[1]
             def add(j, carry):
                 p, q_ = lax.div(j, n1_), lax.rem(j, n1_)
-                put_sum(self.k.at[p, q_], [self.k[p, q_], self.r1[p, q_]])
+                self.k[p, q_] = self.k[p, q_] + self.r1[p, q_]
                 return carry
             lax.fori_loop(0, n0 * n1_, add, 0)
             second.start()
@@ -734,7 +767,7 @@
             _, second, zs, _, mine = self.copies()
             second.wait()
             def add(zz, carry):
-                put_sum(mine(zz), [mine(zz)[...], self.r2[zz]])
+                mine(zz)[...] = mine(zz)[...] + self.r2[zz]
                 return carry
             lax.fori_loop(0, 4, add, 0)
             for cp in zs:
@@ -774,7 +807,7 @@
         G_x(pr).wait()
         def add(i, carry):
             cc, zz = lax.div(i, 4), lax.rem(i, 4)
-            put_sum(Gb.at[pr, x, cc, zz], [Gb[pr, x, cc, zz], gx[pr, cc, zz]])
+            Gb[pr, x, cc, zz] = Gb[pr, x, cc, zz] + gx[pr, cc, zz]
             return carry
         lax.fori_loop(0, 8, add, 0)
         for cp in G_z(pr):
@@ -986,7 +1019,7 @@
                 @pl.when(src == z)
                 def _():
                     pltpu.make_async_copy(ig.at[0, rw], hm.at[i, rw], lh.at[hb]).wait()
-                home[i, rw, :] = hm[i, rw, :].astype(f32)
+                pass
         for cp in zv:
             cp.wait()
         sums[...] = vs[...] + vr[3] + vr[4] + vr[5]
@@ -1018,15 +1051,15 @@
     return pl.pallas_call(
         functools.partial(tail_kernel, hd, heads),
         in_specs=[hbm, vm, vm, vm, hbm, hbm, hbm, hbm, hbm, hbm, hbm, hbm, vm, hbm, vm],
-        out_specs=[vm] * 6,
+        out_specs=[vm] * 4 + [hbm, vm],
         out_shape=[
             jax.ShapeDtypeStruct(b1, f32), jax.ShapeDtypeStruct(b2, f32), jax.ShapeDtypeStruct(b3, f32),
-            jax.ShapeDtypeStruct((rq, 3 * D), f32), jax.ShapeDtypeStruct((2, R, D), f32), jax.ShapeDtypeStruct((16, D), f32),
+            jax.ShapeDtypeStruct((rq, 3 * D), f32), jax.ShapeDtypeStruct((2, R, D), bf16), jax.ShapeDtypeStruct((16, D), f32),
         ],
         scratch_shapes=[V((4, W, N // 4), bf16), V((W3, N), bf16)] + bufs(b1, True) + bufs(b2, False) + bufs(b3, False) + [
             V((8, R, D), bf16), V((W3, D), bf16),
             V((2, 2, 2, 4, 2, rq, W3 // 2), bf16), V((2, 2, 4, 2, rq, W3 // 2), bf16), V((2, 3, 2, 2, rq, W3 // 2), bf16), V((2, 4, rq, W3 // 2), bf16),
-            V((2, 2, R, D), bf16), V((2, 2, R, D), bf16), V((2, R, D), bf16), V((2, R, D), bf16), V((2, R, D), bf16), V((2, R, D), bf16),
+            V((2, 2, R, D), bf16), V((2, 2, R, D), bf16), V((2, R, D), bf16), V((2, R, D), bf16), V((2, R, D), bf16),
             V((16, D), f32), V((6, 16, D), f32),
             S((3,)), S((3,)), S, S((10,)), S((10,)), S((10,)), S((10,)), S((5,)), S((5,)), S((5,)),
             S((2,)), S((2,)), S((2, 3)), S((2, 3)), S((2, 3)), S((2, 3)), S((8,)), S((8,)), S((4,)), S((4,)),
@@ -1035,6 +1068,42 @@
         compiler_params=pltpu.CompilerParams(collective_id=1, has_side_effects=True, vmem_limit_bytes=60 << 20),
         name="backward",
     )(dob, qkvT, oT, lse, a1, h1, a2, h2, a3, normed, wT, own, rows, mgrad, sums0)
+
+
+def result_kernel(rows, fc, o1, o2, o3, gq, hm, bo, sums, r1, r2, r3, rq, rh, rb, *rest):
+    for a, b in ((o1, r1), (o2, r2), (o3, r3), (gq, rq), (bo, rb)):
+        b[...] = a[...]
+    rh[...] = hm[...].astype(f32)
+    x, c, z, y = place()
+    index = (x * 2 + c) * 8 + z * 2 + y
+    per = 128 // rows
+    block = sums[:, pl.ds(pl.multiple_of(lax.div(index, per) * 128, 128), 128)]
+    mine = pltpu.roll(block, lax.rem(per - lax.rem(index, per), per) * rows, 1)
+    for ref, row in zip(rest, (8, 9, 12, 13, 0, 1, 2, None, 3, 10, 11)):
+        if row is None:
+            per_row = sums.shape[1] // fc
+            at = pl.ds(pl.multiple_of(lax.rem(index, per_row) * fc, fc), fc)
+            part = sums[0:8, at]
+            val = part[4:5]
+            for i in range(1, 4):
+                val = jnp.where(lax.div(index, per_row) == i, part[4 + i:5 + i], val)
+            ref[...] = val
+        else:
+            ref[...] = mine[row:row + 1, 0:rows]
+
+
+def results(o1, o2, o3, gq, hm, bo, sums, rows, fc):
+    vm = pl.BlockSpec(memory_space=pltpu.VMEM)
+    sd = jax.ShapeDtypeStruct
+    widths = [rows] * 7 + [fc] + [rows] * 3
+    return pl.pallas_call(
+        functools.partial(result_kernel, rows, fc),
+        in_specs=[vm] * 7,
+        out_specs=[vm] * 17,
+        out_shape=[sd(a.shape, f32) for a in (o1, o2, o3, gq, hm)] + [sd(bo.shape, bf16)] + [sd((1, w), f32) for w in widths],
+        compiler_params=pltpu.CompilerParams(vmem_limit_bytes=60 << 20),
+        name="results",
+    )(o1, o2, o3, gq, hm, bo, sums)
 
 
 HEADS = 16
@@ -1296,7 +1365,6 @@
 
 def on_device(mesh_shape, tokens_in, lead_hours, cotangent, w_qkv, w_out, w_fc1, w_fc2, ln1_gain, ln1_bias, q_bias, v_bias,
               out_bias, ln2_gain, ln2_bias, fc1_bias, fc2_bias, lead_weight, lead_bias):
-    x, c, z, y = place()
     _, R, D = tokens_in.shape
     FF = w_fc1.shape[1]
     hd = D // HEADS
@@ -1308,14 +1376,12 @@
     small = sum(lax.pad(v[None].astype(f32), f32(0), ((k, 31 - k, 0), (0, 128 - v.shape[0], 0))) for k, v in enumerate(vectors)).astype(bf16)
     normed, qkvT, oT, lse, own, vec, wT, a1, h1, a2, h2, a3, dob, mgrad, block_output, sums0 = forward_kernel(
         tokens_in, cotangent, w_qkv, small, w_fc1, w_fc2, w_out, heads, hd)[:16]
-    grad_fc1, grad_fc2, grad_out, grad_qkv, home, sums = backward_kernel(
+    o1, o2, o3, gq, hm, sums = backward_kernel(
         dob, qkvT, oT, lse, a1, h1, a2, h2, a3.reshape(2, 4, 2, rows, D), normed, wT,
         own, vec, mgrad, sums0, heads, hd)
-    index = (x * 2 + c) * 8 + z * 2 + y
-    mine = lax.dynamic_slice(sums, (0, index * rows), (16, rows))
-    g_fc1_bias = lax.dynamic_slice(sums[4:4 + FF // D].reshape(FF), (index * fc1_bias.shape[0],), (fc1_bias.shape[0],))
-    return (block_output, home, grad_qkv, grad_out, grad_fc1, grad_fc2, mine[8], mine[9], mine[12], mine[13], mine[0],
-            mine[1], mine[2], g_fc1_bias, mine[3], mine[10], mine[11])
+    grad_fc1, grad_fc2, grad_out, grad_qkv, home, block_output, *small = results(
+        o1, o2, o3, gq, hm, block_output, sums, rows, fc1_bias.shape[0])
+    return (block_output, home, grad_qkv, grad_out, grad_fc1, grad_fc2) + tuple(v.reshape(-1) for v in small)
 
 
 def choose(mesh_shape, *args):

time: 350 us -> 331 us (0.946)
  Pallas kernels: 338 us -> 327 us
  local copies, waits for them, and re-layouts: 8.41 us -> 0 us
    pallas_call x1, Pallas kernels: 207 us -> 189 us  [forward_kernel(): pl.pallas_call(functools.partial(fwd_kernel, hd, heads), in_specs=[hbm] *...]
    unnamed x20 -> x0, local copies, waits for them, and re-layouts: 6.22 us -> none
    pallas_call x0 -> x1, Pallas kernels: none -> 4.31 us  [results(): pl.pallas_call(functools.partial(result_kernel, rows, fc), in_specs=[vm]...]
where the time goes in v4:
time: 331 us; the launch traced here: 330 us
  Pallas kernels  327 us (99%)
    pallas_call x1, Pallas kernels, forward_kernel(): pl.pallas_call(functools.partial(fwd_kernel, hd, heads), in_specs=[hbm] *...  189 us
    pallas_call x1, Pallas kernels, backward_kernel(): pl.pallas_call(functools.partial(tail_kernel, hd, heads), in_specs=[hbm,...  134 us

profile of v4, /device:TPU:0, one launch (start us, length us, event | category | flops | bytes accessed | tf_op | source)
XLA Modules:
  0.0 330.4 jit_solution(13673111700703750688)
XLA Ops:
  0.7 0.7 convert_bitcast_fusion
  1.3 1.4 add_convert_fusion.small
  2.7 188.9 %forward.1 = (bf16[8,256,1024]{2,1,0:T(8,128)(2,1)}, bf16[768,2048]{1,0:T(8,128)(2,1)}, f32[256,2048]{1,0:T(8,128)}, f32[4,2048]{1,0:T(4,128)}, bf16[2,256,1024]...) custom-call(bf16[2,256,1024]{2,1,0:T(8,128)(2,1)} %tok.1, ...), custom_call_target="tpu_custom_call" | custom-call | tf_op jit(solution)/shard_map/forward/pallas_call | solution.py:674
  191.7 134.2 %backward.1 = (f32[32,4096]{1,0:T(8,128)}, f32[128,1024]{1,0:T(8,128)}, f32[32,1024]{1,0:T(8,128)}, f32[32,3072]{1,0:T(8,128)}, bf16[2,256,1024]{2,1,0:T(8,128)(2,1)}, /*index=5*/f32[16,1024]{1,0:T(8,128)}) custom-call(bf16[4,256,512]{2,1,0:T(8,128)(2,1)} %get-tuple-element.56.dob, bf16[768,2048]{1,0:T(8,128)(2,1)} %get-tuple-element.57.qkvT, ...), custom_call_target="tpu_custom_call" | custom-call | tf_op jit(solution)/shard_map/backward/pallas_call | solution.py:1051
  325.9 4.3 %results.1 = (f32[32,4096]{1,0:T(8,128)}, f32[128,1024]{1,0:T(8,128)}, f32[32,1024]{1,0:T(8,128)}, f32[32,3072]{1,0:T(8,128)}, f32[2,256,1024]{2,1,0:T(8,128)}, ...) custom-call(f32[32,4096]{1,0:T(8,128)} %get-tuple-element.71.o1, ...), custom_call_target="tpu_custom_call" | custom-call | tf_op jit(solution)/shard_map/results/pallas_call | solution.py:1099

commit v5 on v4

--- a/solution.py
+++ b/solution.py
@@ -40,8 +40,8 @@
     pl.semaphore_wait(bar, len(partners))
 
 
-def fwd_kernel(hd, heads, tok, cot, wq, small, fa, fb, fc, normed, qkv_out, o_out, lse, own, vec, w_out_, a1, h1, a2, h2, a3, dob, mgrad, bo, sums,
-               ga, gb, gc, qkvT, oT, wT, T, Ws, fb1, bt, up, r1, r2, r3, st, rt, lt, sy, ry, sc, rc, scy, rcy, sa, ra, la, sz, rz, sx, rx, so, ro, lo,
+def fwd_kernel(hd, heads, tok, cot, wq, small, fa, fb, fc, normed, qkv_out, o_out, lse, own_out, vec, w_out_, a1, h1, a2, h2, a3, dob_out, mg_out, bo, sums,
+               ga, gb, gc, qkvT, oT, wT, own, dob, mgrad, T, Ws, fb1, bt, up, r1, r2, r3, st, rt, lt, sy, ry, sc, rc, scy, rcy, sa, ra, la, sz, rz, sx, rx, so, ro, lo,
                ln, su, ru, lu, gss, grs, gsz, grz, gs1, gr1, gs2, gr2, gsc, grc, sf1, rf1, sf2, rf2, sf3, rf3, la1, la2, la3,
                sh1, qh1, sh2, qh2, sbo, qbo, lbo, lq):
     x, c, z, y = place()
@@ -217,10 +217,9 @@
         0: ((ag_two, 1, 0),),
         2: ((ag_z0, 1, 0), (ag_two, 0, 0),),
         3: ((ag_z0, 0, 0),),
+        4: ((ag_two, 2, 0),),
         5: ((ag_recv, 0, 1),),
-        6: ((ag_two, 2, 0),),
-        7: ((ag_recv, 1, 1),),
-        9: ((ag_recv, 2, 1),),
+        7: ((ag_recv, 2, 1), (ag_recv, 1, 1),),
         10: ((ag_two, 1, 1),),
         11: ((ag_recv, 2, 2), (ag_recv, 0, 3),),
         12: ((ag_two, 2, 1),),
@@ -228,18 +227,17 @@
         14: ((ag_two, 2, 2),),
         15: ((ag_core, 0, 0),),
         17: ((ag_core, 2, 0),),
+        18: ((ag_recv, 2, 3),),
         19: ((ag_two, 0, 3),),
         20: ((ag_recv, 1, 2),),
-        22: ((ag_core, 0, 1), (ag_core, 0, 2), (ag_recv, 2, 3),),
+        22: ((ag_core, 0, 1), (ag_core, 0, 2),),
         23: ((ag_core, 2, 2), (ag_core, 1, 1),),
-        24: ((ag_two, 2, 3), (ag_two, 1, 2), (ag_core, 2, 1), (ag_core, 2, 3),),
-        25: ((ag_two, 1, 3), (ag_core, 0, 3), (ag_recv, 1, 3),),
+        24: ((ag_two, 2, 3), (ag_core, 2, 1), (ag_core, 2, 3),),
+        25: ((ag_two, 1, 2), (ag_two, 1, 3), (ag_core, 0, 3), (ag_recv, 1, 3),),
         26: ((ag_core, 1, 2),),
         28: ((ag_core, 1, 3),),
-        34: ((ag_recv, 0, 2),),
-        35: ((ag_z0, 2, 0),),
-        36: ((ag_core, 1, 0),),
-        38: ((ag_two, 0, 1),),
+        35: ((ag_z0, 2, 0), (ag_two, 0, 1),),
+        36: ((ag_core, 1, 0), (ag_recv, 0, 2),),
     }
 
     COT = 14
@@ -335,8 +333,10 @@
     keep = pltpu.make_async_copy(T, normed, ln)
     keep.start()
     early = [pltpu.make_async_copy(a, b, lq.at[i]) for i, (a, b) in enumerate(((qkvT, qkv_out), (wT, w_out_), (oT, o_out)))]
+    early.append(pltpu.make_async_copy(own, own_out, lq.at[3]))
     early[0].start()
     early[1].start()
+    early[3].start()
     ag_slot(7)
     keep.wait()
     def cot_copy(i):
@@ -624,6 +624,9 @@
             rcopy(sb3.at[q], r3.at[q], sf3.at[q], rf3.at[q], sib).start()
         for q in range(4):
             dob[q] = dot_nt(Wo[q // 2, q % 2].reshape(D // 4, D), ag).astype(bf16)
+        late = [pltpu.make_async_copy(dob, dob_out, lq.at[4]), pltpu.make_async_copy(mgrad, mg_out, lq.at[5])]
+        for cp in late:
+            cp.start()
         for q in range(2):
             rcopy(sb3.at[q], r3.at[q], sf3.at[q], rf3.at[q], sib).wait()
             r3[q] = (r3[q].astype(f32) + dot_nn(bt[q * 2 + c], ag)).astype(bf16)
@@ -644,7 +647,7 @@
         for i in range(2):
             go2(i * 4 + c)[0].wait_recv()
         cp3.wait()
-        for cp in early:
+        for cp in early + late:
             cp.wait()
         out_wait(bout)
         for p in range(3):
@@ -674,7 +677,7 @@
     return pl.pallas_call(
         functools.partial(fwd_kernel, hd, heads),
         in_specs=[hbm] * 7,
-        out_specs=[hbm] * 3 + [vm] * 3 + [hbm] * 6 + [vm] * 2 + [hbm, vm] + [hbm] * 3,
+        out_specs=[hbm] * 3 + [vm, hbm, vm] + [hbm] * 9 + [vm] + [hbm] * 3,
         out_shape=[
             sd((8, R, D), bf16), sd((3 * W, N), bf16), sd((W, N), f32), sd((heads, N), f32), sd((2, R, D), bf16), sd((16, D), f32),
             sd((3 * W, D), bf16), sd((2, 4) + fa.shape, bf16), sd((2, 4) + fa.shape, bf16), sd((4, 2) + fb.shape, bf16),
@@ -682,14 +685,14 @@
             sd((2, R, D), f32), sd((2, R, D), bf16), sd((16, D), f32), full(fa), full(fb), full(fc),
         ],
         scratch_shapes=[
-            V((3 * W, N), bf16), V((W, N), f32), V((3 * W, D), bf16),
+            V((3 * W, N), bf16), V((W, N), f32), V((3 * W, D), bf16), V((2, R, D), bf16), V((4, W, C), bf16), V((2, R, D), f32),
             V((8, R, D), bf16), V((8, 4, 32, 3 * W + 128), bf16), V((8, FF), f32), V((4, W, C), bf16), V((2, R, D), bf16),
             V((2, 4, 2, R // 8, 2 * C), bf16), V((C, D), bf16), V((2, D // 4, D), bf16),
             S((2,)), S((2,)), S, S((2,)), S((2,)), S((2,)), S((2,)), S((2,)), S((2,)),
             S((3, 4)), S((3, 4)), S((4,)), S((6,)), S((6,)), S((7,)), S((7,)), S((3,)), S((3,)), S, S,
             S((2,)), S((2,)), S, S((3,)), S((3,)), S((3, 6)), S((3, 6)), S((3, 7)), S((3, 7)), S((3, 7)), S((3, 7)), S((3, 7)), S((3, 7)),
             S((8,)), S((8,)), S((8,)), S((8,)), S((2,)), S((2,)), S((8, 2)), S((2,)), S,
-            S((8, 2)), S((8, 2)), S((2,)), S((2,)), S((2,)), S((2,)), S, S((3,)),
+            S((8, 2)), S((8, 2)), S((2,)), S((2,)), S((2,)), S((2,)), S, S((6,)),
         ],
         compiler_params=pltpu.CompilerParams(collective_id=0, has_side_effects=True, vmem_limit_bytes=60 << 20),
         name="forward",
@@ -703,18 +706,21 @@
     dst[...] = total.astype(dst.dtype)
 
 
-def tail_kernel(hd, heads, dob, qkvT, oT, lse, a1, h1, a2, h2, a3, normed, wT, own, rows, mgrad, sums0,
+def tail_kernel(hd, heads, dob, qkv_in, o_in, lse, a1, h1, a2, h2, a3, normed, wT, own, rows, mgrad, sums0,
                 o1, o2, o3, gq, hm, sums,
-                do_s, dq_s, k1, r11, r12, r13, k2, r21, r22, r23, k3, r31, r32, r33,
+                qkvT, oT, do_s, dq_s, k1, r11, r12, r13, k2, r21, r22, r23, k3, r31, r32, r33,
                 nm, w_s, Gb, gx, gz, go, ds_s, dr_c, dy_s, dr_y, ig, vs, vr,
-                sd, rd, ld, s1, q1, s2, q2, s3, q3, lk, sg, qg, sgz, qgz, sga, qga, sdc, qdc, sdy, qdy, sh, qh, lh, sv, qv, ll, lnm):
+                sd, rd, ld, s1, q1, s2, q2, s3, q3, lk, sg, qg, sgz, qgz, sga, qga, sdc, qdc, sdy, qdy, sh, qh, lh, sv, qv, ll, lnm, lqo):
     x, c, z, y = place()
     hg = c * 2 + y
     W = heads * hd
-    N = qkvT.shape[1]
+    N = qkv_in.shape[1]
     zoff = [lax.rem(z + k, 4) for k in (1, 2, 3)]
     sib, yp, diag, xp = dev(x, 1 - c, z, y), dev(x, c, z, 1 - y), dev(x, 1 - c, z, 1 - y), dev(1 - x, c, z, y)
     zp = [dev(x, c, zz, y) for zz in zoff]
+    ins = [pltpu.make_async_copy(a, b, lqo.at[i]) for i, (a, b) in enumerate(((qkv_in, qkvT), (o_in, oT)))]
+    for cp in ins:
+        cp.start()
     greet(zp + [dev(x, 1 - c, zz, y) for zz in zoff] + [sib, yp, diag, xp])
     peers = ((sib, (1 - c) * 2 + y), (yp, c * 2 + 1 - y), (diag, (1 - c) * 2 + 1 - y))
     for k, (d, g) in enumerate(peers):
@@ -863,6 +869,8 @@
 
     def attention(k_s, v_s, dk_s, dv_s):
         loc.wait()
+        for cp in ins:
+            cp.wait()
         def head(h, carry):
             hr = pl.ds(h * hd, hd)
             @pl.when(h == 2)
@@ -1050,20 +1058,20 @@
     rq = D // 32
     return pl.pallas_call(
         functools.partial(tail_kernel, hd, heads),
-        in_specs=[hbm, vm, vm, vm, hbm, hbm, hbm, hbm, hbm, hbm, hbm, hbm, vm, hbm, vm],
+        in_specs=[hbm, hbm, hbm, vm, hbm, hbm, hbm, hbm, hbm, hbm, hbm, hbm, vm, hbm, vm],
         out_specs=[vm] * 4 + [hbm, vm],
         out_shape=[
             jax.ShapeDtypeStruct(b1, f32), jax.ShapeDtypeStruct(b2, f32), jax.ShapeDtypeStruct(b3, f32),
             jax.ShapeDtypeStruct((rq, 3 * D), f32), jax.ShapeDtypeStruct((2, R, D), bf16), jax.ShapeDtypeStruct((16, D), f32),
         ],
-        scratch_shapes=[V((4, W, N // 4), bf16), V((W3, N), bf16)] + bufs(b1, True) + bufs(b2, False) + bufs(b3, False) + [
+        scratch_shapes=[V((W3, N), bf16), V((W, N), f32), V((4, W, N // 4), bf16), V((W3, N), bf16)] + bufs(b1, True) + bufs(b2, False) + bufs(b3, False) + [
             V((8, R, D), bf16), V((W3, D), bf16),
             V((2, 2, 2, 4, 2, rq, W3 // 2), bf16), V((2, 2, 4, 2, rq, W3 // 2), bf16), V((2, 3, 2, 2, rq, W3 // 2), bf16), V((2, 4, rq, W3 // 2), bf16),
             V((2, 2, R, D), bf16), V((2, 2, R, D), bf16), V((2, R, D), bf16), V((2, R, D), bf16), V((2, R, D), bf16),
             V((16, D), f32), V((6, 16, D), f32),
             S((3,)), S((3,)), S, S((10,)), S((10,)), S((10,)), S((10,)), S((5,)), S((5,)), S((5,)),
             S((2,)), S((2,)), S((2, 3)), S((2, 3)), S((2, 3)), S((2, 3)), S((8,)), S((8,)), S((4,)), S((4,)),
-            S((4,)), S((2, 2)), S((2,)), S((6,)), S((6,)), S((2,)), S((2,)),
+            S((4,)), S((2, 2)), S((2,)), S((6,)), S((6,)), S((2,)), S((2,)), S((2,)),
         ],
         compiler_params=pltpu.CompilerParams(collective_id=1, has_side_effects=True, vmem_limit_bytes=60 << 20),
         name="backward",

time: 331 us -> 324 us (0.979)
  Pallas kernels: 327 us -> 321 us
    pallas_call x1, Pallas kernels: 189 us -> 184 us  [forward_kernel(): pl.pallas_call(functools.partial(fwd_kernel, hd, heads), in_specs=[hbm] *...]
where the time goes in v5:
time: 324 us
  Pallas kernels  321 us (99%)
    pallas_call x1, Pallas kernels, forward_kernel(): pl.pallas_call(functools.partial(fwd_kernel, hd, heads), in_specs=[hbm] *...  184 us
    pallas_call x1, Pallas kernels, backward_kernel(): pl.pallas_call(functools.partial(tail_kernel, hd, heads), in_specs=[hbm,...  133 us

profile of v5, /device:TPU:0, one launch (start us, length us, event | category | flops | bytes accessed | tf_op | source)
XLA Modules:
  0.0 324.1 jit_solution(519055025351473564)
XLA Ops:
  0.7 0.7 convert_bitcast_fusion
  1.3 1.4 add_convert_fusion.small
  2.7 184.1 %forward.1 = (bf16[8,256,1024]{2,1,0:T(8,128)(2,1)}, bf16[768,2048]{1,0:T(8,128)(2,1)}, f32[256,2048]{1,0:T(8,128)}, f32[4,2048]{1,0:T(4,128)}, bf16[2,256,1024]...) custom-call(bf16[2,256,1024]{2,1,0:T(8,128)(2,1)} %tok.1, ...), custom_call_target="tpu_custom_call" | custom-call | tf_op jit(solution)/shard_map/forward/pallas_call | solution.py:677
  186.8 132.8 %backward.1 = (f32[32,4096]{1,0:T(8,128)}, f32[128,1024]{1,0:T(8,128)}, f32[32,1024]{1,0:T(8,128)}, f32[32,3072]{1,0:T(8,128)}, bf16[2,256,1024]{2,1,0:T(8,128)(2,1)}, /*index=5*/f32[16,1024]{1,0:T(8,128)}) custom-call(bf16[4,256,512]{2,1,0:T(8,128)(2,1)} %get-tuple-element.56.dob, bf16[768,2048]{1,0:T(8,128)(2,1)} %get-tuple-element.57.qkv_in, ...), custom_call_target="tpu_custom_call" | custom-call | tf_op jit(solution)/shard_map/backward/pallas_call | solution.py:1059
  319.6 4.3 %results.1 = (f32[32,4096]{1,0:T(8,128)}, f32[128,1024]{1,0:T(8,128)}, f32[32,1024]{1,0:T(8,128)}, f32[32,3072]{1,0:T(8,128)}, f32[2,256,1024]{2,1,0:T(8,128)}, ...) custom-call(f32[32,4096]{1,0:T(8,128)} %get-tuple-element.71.o1, ...), custom_call_target="tpu_custom_call" | custom-call | tf_op jit(solution)/shard_map/results/pallas_call | solution.py:1107

commit v6 on v5

--- a/solution.py
+++ b/solution.py
@@ -40,7 +40,7 @@
     pl.semaphore_wait(bar, len(partners))
 
 
-def fwd_kernel(hd, heads, tok, cot, wq, small, fa, fb, fc, normed, qkv_out, o_out, lse, own_out, vec, w_out_, a1, h1, a2, h2, a3, dob_out, mg_out, bo, sums,
+def fwd_kernel(hd, heads, tok, cot, wq, small, fa, fb, fc, normed, qkv_out, o_out, lse, own_out, vec, w_out_, a1, h1, a2, h2, a3, dob_out, mg_out, bo, bout_b, sums,
                ga, gb, gc, qkvT, oT, wT, own, dob, mgrad, T, Ws, fb1, bt, up, r1, r2, r3, st, rt, lt, sy, ry, sc, rc, scy, rcy, sa, ra, la, sz, rz, sx, rx, so, ro, lo,
                ln, su, ru, lu, gss, grs, gsz, grz, gs1, gr1, gs2, gr2, gsc, grc, sf1, rf1, sf2, rf2, sf3, rf3, la1, la2, la3,
                sh1, qh1, sh2, qh2, sbo, qbo, lbo, lq):
@@ -433,19 +433,21 @@
     FF = fb1.shape[1]
     C = 2 * R
 
+    H = R // 2
     def out_copy(bout, j):
         zt = 2 * c + j
-        return zt, rcopy(bout.at[j], bo.at[lax.rem(z, 2)], sbo.at[j], qbo.at[lax.rem(z, 2)], dev(x, lax.div(z, 2), zt, y)), \
-            pltpu.make_async_copy(bout.at[j], bo.at[lax.rem(z, 2)], lbo)
+        src, dst = bout.at[j, pl.ds(0, H)], bo.at[lax.rem(z, 2)]
+        return zt, rcopy(src, dst, sbo.at[j], qbo.at[lax.rem(z, 2)], dev(x, lax.div(z, 2), zt, y)), pltpu.make_async_copy(src, dst, lbo)
     def out_wait(bout):
+        src = bout.at[0, pl.ds(0, H)]
         for i in range(2):
             zt, cp, lc = out_copy(bout, i)
             @pl.when(2 * c + i != z)
             def _():
-                rcopy(bout.at[0], bo.at[i], sbo.at[0], qbo.at[i], sib).wait_recv()
+                rcopy(src, bo.at[i], sbo.at[0], qbo.at[i], sib).wait_recv()
             @pl.when(2 * c + i == z)
             def _():
-                pltpu.make_async_copy(bout.at[0], bo.at[i], lbo).wait()
+                pltpu.make_async_copy(src, bo.at[i], lbo).wait()
             @pl.when(zt != z)
             def _():
                 cp.wait_send()
@@ -599,6 +601,8 @@
             @pl.when(zt == z)
             def _():
                 lc.start()
+        second = pltpu.make_async_copy(bout.at[:, pl.ds(H, H)], bout_b, lq.at[6])
+        second.start()
         last = jnp.int32(7)
         finish(last)
 
@@ -647,7 +651,7 @@
         for i in range(2):
             go2(i * 4 + c)[0].wait_recv()
         cp3.wait()
-        for cp in early + late:
+        for cp in early + late + [second]:
             cp.wait()
         out_wait(bout)
         for p in range(3):
@@ -677,12 +681,12 @@
     return pl.pallas_call(
         functools.partial(fwd_kernel, hd, heads),
         in_specs=[hbm] * 7,
-        out_specs=[hbm] * 3 + [vm, hbm, vm] + [hbm] * 9 + [vm] + [hbm] * 3,
+        out_specs=[hbm] * 3 + [vm, hbm, vm] + [hbm] * 10 + [vm] + [hbm] * 3,
         out_shape=[
             sd((8, R, D), bf16), sd((3 * W, N), bf16), sd((W, N), f32), sd((heads, N), f32), sd((2, R, D), bf16), sd((16, D), f32),
             sd((3 * W, D), bf16), sd((2, 4) + fa.shape, bf16), sd((2, 4) + fa.shape, bf16), sd((4, 2) + fb.shape, bf16),
             sd((4, 2) + fb.shape, bf16), sd((2, D // 4, D), bf16), sd((4, W, C), bf16),
-            sd((2, R, D), f32), sd((2, R, D), bf16), sd((16, D), f32), full(fa), full(fb), full(fc),
+            sd((2, R, D), f32), sd((2, R // 2, D), bf16), sd((2, R // 2, D), bf16), sd((16, D), f32), full(fa), full(fb), full(fc),
         ],
         scratch_shapes=[
             V((3 * W, N), bf16), V((W, N), f32), V((3 * W, D), bf16), V((2, R, D), bf16), V((4, W, C), bf16), V((2, R, D), f32),
@@ -692,7 +696,7 @@
             S((3, 4)), S((3, 4)), S((4,)), S((6,)), S((6,)), S((7,)), S((7,)), S((3,)), S((3,)), S, S,
             S((2,)), S((2,)), S, S((3,)), S((3,)), S((3, 6)), S((3, 6)), S((3, 7)), S((3, 7)), S((3, 7)), S((3, 7)), S((3, 7)), S((3, 7)),
             S((8,)), S((8,)), S((8,)), S((8,)), S((2,)), S((2,)), S((8, 2)), S((2,)), S,
-            S((8, 2)), S((8, 2)), S((2,)), S((2,)), S((2,)), S((2,)), S, S((6,)),
+            S((8, 2)), S((8, 2)), S((2,)), S((2,)), S((2,)), S((2,)), S, S((7,)),
         ],
         compiler_params=pltpu.CompilerParams(collective_id=0, has_side_effects=True, vmem_limit_bytes=60 << 20),
         name="forward",
@@ -706,11 +710,11 @@
     dst[...] = total.astype(dst.dtype)
 
 
-def tail_kernel(hd, heads, dob, qkv_in, o_in, lse, a1, h1, a2, h2, a3, normed, wT, own, rows, mgrad, sums0,
-                o1, o2, o3, gq, hm, sums,
-                qkvT, oT, do_s, dq_s, k1, r11, r12, r13, k2, r21, r22, r23, k3, r31, r32, r33,
+def tail_kernel(hd, heads, dob, qkv_in, o_in, lse, a1, h1, a2, h2, a3, normed, wT, own, rows, mgrad, sums0, bout_b,
+                o1, o2, o3, gq, hm, sums, bo_b,
+                qkvT, oT, out_vm, do_s, dq_s, k1, r11, r12, r13, k2, r21, r22, r23, k3, r31, r32, r33,
                 nm, w_s, Gb, gx, gz, go, ds_s, dr_c, dy_s, dr_y, ig, vs, vr,
-                sd, rd, ld, s1, q1, s2, q2, s3, q3, lk, sg, qg, sgz, qgz, sga, qga, sdc, qdc, sdy, qdy, sh, qh, lh, sv, qv, ll, lnm, lqo):
+                sd, rd, ld, s1, q1, s2, q2, s3, q3, lk, sg, qg, sgz, qgz, sga, qga, sdc, qdc, sdy, qdy, sh, qh, lh, sv, qv, ll, lnm, lqo, sbo, qbo, lbo):
     x, c, z, y = place()
     hg = c * 2 + y
     W = heads * hd
@@ -727,6 +731,37 @@
         rcopy(dob.at[g], do_s.at[hg], sd.at[k], rd.at[k], d).start()
     loc = pltpu.make_async_copy(dob.at[hg], do_s.at[hg], ld)
     loc.start()
+
+    def out_copy(j):
+        zt = 2 * c + j
+        src, dst = bout_b.at[j], bo_b.at[lax.rem(z, 2)]
+        return zt, rcopy(src, dst, sbo.at[j], qbo.at[lax.rem(z, 2)], dev(x, lax.div(z, 2), zt, y))
+    def out_local(j):
+        v = out_vm.at[j]
+        return pltpu.make_async_copy(bout_b.at[j], v, lbo.at[0]), pltpu.make_async_copy(v, bo_b.at[lax.rem(z, 2)], lbo.at[1])
+    for j in range(2):
+        zt, cp = out_copy(j)
+        @pl.when(zt != z)
+        def _():
+            cp.start()
+        @pl.when(zt == z)
+        def _():
+            out_local(j)[0].start()
+    def out_wait():
+        for i in range(2):
+            zt, cp = out_copy(i)
+            @pl.when(2 * c + i != z)
+            def _():
+                rcopy(bout_b.at[0], bo_b.at[i], sbo.at[0], qbo.at[i], sib).wait_recv()
+            @pl.when(2 * c + i == z)
+            def _():
+                first, then = out_local(i)
+                first.wait()
+                then.start()
+                then.wait()
+            @pl.when(zt != z)
+            def _():
+                cp.wait_send()
 
     def part(ref, h, n):
         return ref if n is None else ref.at[..., pl.ds(h * n, n), :]
@@ -933,8 +968,8 @@
         for cp in loads:
             cp.start()
         ld_w.wait()
-        def proj(g, b):
-            return dot_nn(dq_s[:, pl.ds(pl.multiple_of(g * QB + b * B, B), B)].T, w_s[...])
+        def proj(g, j):
+            return dot_nn(dq_s[:, pl.ds(pl.multiple_of(g * QB + j * R, R), R)].T, w_s[...])
         g_sy, g_s, g_oy = (1 - c) * 2 + 1 - y, (1 - c) * 2 + y, c * 2 + 1 - y
         def rows_of(b):
             return b // 2, pl.ds((b % 2) * B, B)
@@ -944,25 +979,25 @@
         def to_y(b):
             j, rw = rows_of(b)
             return rcopy(dy_s.at[j, rw], dr_y.at[j, rw], sdy.at[b], qdy.at[b], yp)
-        for b in range(4):
-            j, rw = rows_of(b)
-            ds_s[0, j, rw, :] = proj(g_sy, b).astype(bf16)
-            to_sib(0, b).start()
-        for b in range(4):
-            j, rw = rows_of(b)
-            mine = proj(g_oy, b)
-            to_sib(0, b).wait()
-            dy_s[j, rw, :] = (mine + dr_c[0, j, rw, :].astype(f32)).astype(bf16)
-            to_y(b).start()
+        for j in range(2):
+            ds_s[0, j] = proj(g_sy, j).astype(bf16)
+            to_sib(0, 2 * j).start()
+            to_sib(0, 2 * j + 1).start()
+        for j in range(2):
+            mine = proj(g_oy, j)
+            for b in (2 * j, 2 * j + 1):
+                rw = rows_of(b)[1]
+                to_sib(0, b).wait()
+                dy_s[j, rw, :] = (mine[(b % 2) * B:(b % 2 + 1) * B] + dr_c[0, j, rw, :].astype(f32)).astype(bf16)
+                to_y(b).start()
         slot(16)
         G_first(1)
-        for b in range(4):
-            j, rw = rows_of(b)
-            ds_s[1, j, rw, :] = proj(g_s, b).astype(bf16)
-            to_sib(1, b).start()
-        for b in range(4):
-            j, rw = rows_of(b)
-            dn[j, rw, :] = proj(hg, b)
+        for j in range(2):
+            ds_s[1, j] = proj(g_s, j).astype(bf16)
+            to_sib(1, 2 * j).start()
+            to_sib(1, 2 * j + 1).start()
+        for j in range(2):
+            dn[j] = proj(hg, j)
         ones = jnp.ones((8, N), bf16)
         vs[...] = sums0[...]
         for row, q in ((12, 0), (13, 2)):
@@ -1032,6 +1067,7 @@
             cp.wait()
         sums[...] = vs[...] + vr[3] + vr[4] + vr[5]
         slot(26)
+        out_wait()
         for b in range(4):
             zt, cp, lc = home_copy(b)
             @pl.when(zt != z)
@@ -1043,7 +1079,7 @@
     pl.run_scoped(after, pltpu.VMEM((2, R, D), bf16), pltpu.VMEM((2, R, D), f32), pltpu.VMEM((2, R, D), f32), pltpu.SemaphoreType.DMA((2,)))
 
 
-def backward_kernel(dob, qkvT, oT, lse, a1, h1, a2, h2, a3, normed, wT, own, rows, mgrad, sums0, heads, hd):
+def backward_kernel(dob, qkvT, oT, lse, a1, h1, a2, h2, a3, normed, wT, own, rows, mgrad, sums0, bout_b, heads, hd):
     W3, N = qkvT.shape
     W = heads * hd
     _, R, D = own.shape
@@ -1058,29 +1094,33 @@
     rq = D // 32
     return pl.pallas_call(
         functools.partial(tail_kernel, hd, heads),
-        in_specs=[hbm, hbm, hbm, vm, hbm, hbm, hbm, hbm, hbm, hbm, hbm, hbm, vm, hbm, vm],
-        out_specs=[vm] * 4 + [hbm, vm],
+        in_specs=[hbm, hbm, hbm, vm, hbm, hbm, hbm, hbm, hbm, hbm, hbm, hbm, vm, hbm, vm, hbm],
+        out_specs=[vm] * 4 + [hbm, vm, hbm],
         out_shape=[
             jax.ShapeDtypeStruct(b1, f32), jax.ShapeDtypeStruct(b2, f32), jax.ShapeDtypeStruct(b3, f32),
             jax.ShapeDtypeStruct((rq, 3 * D), f32), jax.ShapeDtypeStruct((2, R, D), bf16), jax.ShapeDtypeStruct((16, D), f32),
+            jax.ShapeDtypeStruct((2, R // 2, D), bf16),
         ],
-        scratch_shapes=[V((W3, N), bf16), V((W, N), f32), V((4, W, N // 4), bf16), V((W3, N), bf16)] + bufs(b1, True) + bufs(b2, False) + bufs(b3, False) + [
+        scratch_shapes=[V((W3, N), bf16), V((W, N), f32), V((2, R // 2, D), bf16), V((4, W, N // 4), bf16), V((W3, N), bf16)] + bufs(b1, True) + bufs(b2, False) + bufs(b3, False) + [
             V((8, R, D), bf16), V((W3, D), bf16),
             V((2, 2, 2, 4, 2, rq, W3 // 2), bf16), V((2, 2, 4, 2, rq, W3 // 2), bf16), V((2, 3, 2, 2, rq, W3 // 2), bf16), V((2, 4, rq, W3 // 2), bf16),
             V((2, 2, R, D), bf16), V((2, 2, R, D), bf16), V((2, R, D), bf16), V((2, R, D), bf16), V((2, R, D), bf16),
             V((16, D), f32), V((6, 16, D), f32),
             S((3,)), S((3,)), S, S((10,)), S((10,)), S((10,)), S((10,)), S((5,)), S((5,)), S((5,)),
             S((2,)), S((2,)), S((2, 3)), S((2, 3)), S((2, 3)), S((2, 3)), S((8,)), S((8,)), S((4,)), S((4,)),
-            S((4,)), S((2, 2)), S((2,)), S((6,)), S((6,)), S((2,)), S((2,)), S((2,)),
+            S((4,)), S((2, 2)), S((2,)), S((6,)), S((6,)), S((2,)), S((2,)), S((2,)), S((2,)), S((2,)), S((2,)),
         ],
         compiler_params=pltpu.CompilerParams(collective_id=1, has_side_effects=True, vmem_limit_bytes=60 << 20),
         name="backward",
-    )(dob, qkvT, oT, lse, a1, h1, a2, h2, a3, normed, wT, own, rows, mgrad, sums0)
-
-
-def result_kernel(rows, fc, o1, o2, o3, gq, hm, bo, sums, r1, r2, r3, rq, rh, rb, *rest):
-    for a, b in ((o1, r1), (o2, r2), (o3, r3), (gq, rq), (bo, rb)):
+    )(dob, qkvT, oT, lse, a1, h1, a2, h2, a3, normed, wT, own, rows, mgrad, sums0, bout_b)
+
+
+def result_kernel(rows, fc, o1, o2, o3, gq, hm, bo_a, bo_b, sums, r1, r2, r3, rq, rh, rb, *rest):
+    for a, b in ((o1, r1), (o2, r2), (o3, r3), (gq, rq)):
         b[...] = a[...]
+    half = bo_a.shape[1]
+    rb[:, 0:half, :] = bo_a[...]
+    rb[:, half:, :] = bo_b[...]
     rh[...] = hm[...].astype(f32)
     x, c, z, y = place()
     index = (x * 2 + c) * 8 + z * 2 + y
@@ -1100,18 +1140,18 @@
             ref[...] = mine[row:row + 1, 0:rows]
 
 
-def results(o1, o2, o3, gq, hm, bo, sums, rows, fc):
+def results(o1, o2, o3, gq, hm, bo_a, bo_b, sums, rows, fc):
     vm = pl.BlockSpec(memory_space=pltpu.VMEM)
     sd = jax.ShapeDtypeStruct
     widths = [rows] * 7 + [fc] + [rows] * 3
     return pl.pallas_call(
         functools.partial(result_kernel, rows, fc),
-        in_specs=[vm] * 7,
+        in_specs=[vm] * 8,
         out_specs=[vm] * 17,
-        out_shape=[sd(a.shape, f32) for a in (o1, o2, o3, gq, hm)] + [sd(bo.shape, bf16)] + [sd((1, w), f32) for w in widths],
+        out_shape=[sd(a.shape, f32) for a in (o1, o2, o3, gq, hm)] + [sd(hm.shape, bf16)] + [sd((1, w), f32) for w in widths],
         compiler_params=pltpu.CompilerParams(vmem_limit_bytes=60 << 20),
         name="results",
-    )(o1, o2, o3, gq, hm, bo, sums)
+    )(o1, o2, o3, gq, hm, bo_a, bo_b, sums)
 
 
 HEADS = 16
@@ -1382,13 +1422,13 @@
     vectors = (lead_weight, lead_bias, ln1_gain, ln1_bias, q_bias, v_bias, out_bias, ln2_gain, ln2_bias, fc2_bias, fc1_bias,
                lead_hours.astype(bf16))
     small = sum(lax.pad(v[None].astype(f32), f32(0), ((k, 31 - k, 0), (0, 128 - v.shape[0], 0))) for k, v in enumerate(vectors)).astype(bf16)
-    normed, qkvT, oT, lse, own, vec, wT, a1, h1, a2, h2, a3, dob, mgrad, block_output, sums0 = forward_kernel(
-        tokens_in, cotangent, w_qkv, small, w_fc1, w_fc2, w_out, heads, hd)[:16]
-    o1, o2, o3, gq, hm, sums = backward_kernel(
+    normed, qkvT, oT, lse, own, vec, wT, a1, h1, a2, h2, a3, dob, mgrad, bo_a, bout_b, sums0 = forward_kernel(
+        tokens_in, cotangent, w_qkv, small, w_fc1, w_fc2, w_out, heads, hd)[:17]
+    o1, o2, o3, gq, hm, sums, bo_b = backward_kernel(
         dob, qkvT, oT, lse, a1, h1, a2, h2, a3.reshape(2, 4, 2, rows, D), normed, wT,
-        own, vec, mgrad, sums0, heads, hd)
+        own, vec, mgrad, sums0, bout_b, heads, hd)
     grad_fc1, grad_fc2, grad_out, grad_qkv, home, block_output, *small = results(
-        o1, o2, o3, gq, hm, block_output, sums, rows, fc1_bias.shape[0])
+        o1, o2, o3, gq, hm, bo_a, bo_b, sums, rows, fc1_bias.shape[0])
     return (block_output, home, grad_qkv, grad_out, grad_fc1, grad_fc2) + tuple(v.reshape(-1) for v in small)
 
 

time: 324 us -> 321 us (level)
  Pallas kernels: 321 us -> 317 us
where the time goes in v6:
time: 321 us; the launch traced here: 320 us
  Pallas kernels  317 us (99%)
    pallas_call x1, Pallas kernels, forward_kernel(): pl.pallas_call(functools.partial(fwd_kernel, hd, heads), in_specs=[hbm] *...  183 us
    pallas_call x1, Pallas kernels, backward_kernel(): pl.pallas_call(functools.partial(tail_kernel, hd, heads), in_specs=[hbm,...  130 us

profile of v6, /device:TPU:0, one launch (start us, length us, event | category | flops | bytes accessed | tf_op | source)
XLA Modules:
  0.0 320.4 jit_solution(1154887445162720411)
XLA Ops:
  0.7 0.7 convert_bitcast_fusion
  1.3 1.4 add_convert_fusion.small
  2.7 182.9 %forward.1 = (bf16[8,256,1024]{2,1,0:T(8,128)(2,1)}, bf16[768,2048]{1,0:T(8,128)(2,1)}, f32[256,2048]{1,0:T(8,128)}, f32[4,2048]{1,0:T(4,128)}, bf16[2,256,1024]...) custom-call(bf16[2,256,1024]{2,1,0:T(8,128)(2,1)} %tok.1, ...), custom_call_target="tpu_custom_call" | custom-call | tf_op jit(solution)/shard_map/forward/pallas_call | solution.py:681
  185.6 130.3 %backward.1 = (f32[32,4096]{1,0:T(8,128)}, f32[128,1024]{1,0:T(8,128)}, f32[32,1024]{1,0:T(8,128)}, f32[32,3072]{1,0:T(8,128)}, bf16[2,256,1024]{2,1,0:T(8,128)(...) custom-call(bf16[4,256,512]{2,1,0:T(8,128)(2,1)} %get-tuple-element.58.dob, ...), custom_call_target="tpu_custom_call" | custom-call | tf_op jit(solution)/shard_map/backward/pallas_call | solution.py:1095
  315.9 4.3 %results.1 = (f32[32,4096]{1,0:T(8,128)}, f32[128,1024]{1,0:T(8,128)}, f32[32,1024]{1,0:T(8,128)}, f32[32,3072]{1,0:T(8,128)}, f32[2,256,1024]{2,1,0:T(8,128)}, ...) custom-call(f32[32,4096]{1,0:T(8,128)} %get-tuple-element.74.o1, ...), custom_call_target="tpu_custom_call" | custom-call | tf_op jit(solution)/shard_map/results/pallas_call | solution.py:1147
